TPU v7x, 32 devices: a whole 2x2x4 slice. The times are simulated.
32 devices in a mesh: head: 4 (over z), seq: 8 (over y, x, core).
Axes of the slice: x: 2, y: 2, z: 4, core: 2. Of those that a mesh axis runs over, the one named last changes fastest.
Arguments:
- tokens: bfloat16 [4096, 1536], P('seq'), may hold values from -8 to 8
- cotangent: bfloat16 [4096, 1536], P('seq'), may hold values from -6 to 6
- starts: int32 [4096], P('seq'), may hold values from 0 to 1, as said below
- gain_attn: bfloat16 [1536], P('seq'), may hold values from 0.5 to 1.5
- w_query: bfloat16 [1536, 1536], P('seq', 'head'), may hold values from -0.15625 to 0.15625
- w_key: bfloat16 [1536, 1536], P('seq', 'head'), may hold values from -0.15625 to 0.15625
- w_value: bfloat16 [1536, 1536], P('seq', 'head'), may hold values from -0.15625 to 0.15625
- w_dir: bfloat16 [1536, 1536], P('seq', 'head'), may hold values from -0.15625 to 0.15625
- w_beta: bfloat16 [1536, 12], P('seq', 'head'), may hold values from -3 to 3
- w_out: bfloat16 [1536, 1536], P('head', 'seq'), may hold values from -3.5 to 3.5
- gain_mlp: bfloat16 [1536], P('seq'), may hold values from 0.5 to 1.5
- w_gate: bfloat16 [1536, 4096], P('seq', 'head'), may hold values from -0.15625 to 0.15625
- w_up: bfloat16 [1536, 4096], P('seq', 'head'), may hold values from -0.15625 to 0.15625
- w_down: bfloat16 [4096, 1536], P('head', 'seq'), may hold values from -0.09375 to 0.09375
Outputs:
- result: bfloat16 [4096, 1536], P('seq')
- d_tokens: float32 [4096, 1536], P('seq')
- grad_gain_attn: float32 [1536], P('seq')
- grad_w_query: float32 [1536, 1536], P('seq', 'head')
- grad_w_key: float32 [1536, 1536], P('seq', 'head')
- grad_w_value: float32 [1536, 1536], P('seq', 'head')
- grad_w_dir: float32 [1536, 1536], P('seq', 'head')
- grad_w_beta: float32 [1536, 12], P('seq', 'head')
- grad_w_out: float32 [1536, 1536], P('head', 'seq')
- grad_gain_mlp: float32 [1536], P('seq')
- grad_w_gate: float32 [1536, 4096], P('seq', 'head')
- grad_w_up: float32 [1536, 4096], P('seq', 'head')
- grad_w_down: float32 [4096, 1536], P('head', 'seq')
Inputs may be any that keep to these rules, and one draw needn't show every extreme that they name: `starts`: 1 marks the first token of a document, 0 any other token; the first token of every packed row of 4096 tokens is marked.
All inputs are finite; a program needn't handle non-finite values.
Results may differ from a plain program's by a relative error of at most 0.028.
The roundings to bfloat16 on the way count: a program that leaves them out, or rounds other values in their place, can miss the bound.
Values may be sent and summed in bfloat16 or wider, within the bound.
No kernel may reach another device: no remote copies, remote signals or barrier semaphores. Data moves between devices by JAX's collectives and lax.ppermute only.
A program may use at most 192 MiB of HBM per device.

v0:
```python
import jax
import jax.numpy as jnp
from jax import lax
from jax.sharding import PartitionSpec as P

SPAN = 8


EPSILON = 1e-06
NEGATIVE = -1e30


def shifted(value, axis, steps):
    count = lax.axis_size(axis)
    initial, last = (max(0, -steps), min(count, count - steps))
    return lax.ppermute(value, axis, [(source, source + steps) for source in range(initial, last)])


def exact_dot(left, right):
    return jnp.matmul(left, right, precision=lax.Precision.HIGHEST)


def norm_rows(value, gain):
    scale = lax.rsqrt(jnp.mean(value * value, axis=-1, keepdims=True) + EPSILON)
    return (value * scale * gain, scale)


def norm_back(grad, value, scale, gain):
    weighted = grad * gain
    d_gain = jnp.sum(grad * value * scale, axis=0)
    d_value = scale * weighted - value * scale * scale * scale * jnp.mean(
        weighted * value, axis=-1, keepdims=True
    )
    return (d_value, d_gain)


def householder_block(query, key_rows, dir_raw, beta_raw):
    unit_dir = dir_raw * lax.rsqrt(jnp.sum(dir_raw * dir_raw, axis=-1, keepdims=True) + EPSILON)
    beta_gate = 2.0 * jax.nn.sigmoid(beta_raw)
    length = query.shape[0]
    row_ids = lax.broadcasted_iota(jnp.int32, (length, length), 0)
    col_ids = lax.broadcasted_iota(jnp.int32, (length, length), 1)
    dir_gram = exact_dot(unit_dir, unit_dir.T)
    lower_mat = jnp.where(row_ids > col_ids, dir_gram, 0.0) + jnp.diag(1.0 / beta_gate)
    inner_solve = lax.linalg.triangular_solve(lower_mat, unit_dir, left_side=True, lower=True)
    dir_key = jnp.where(row_ids > col_ids, exact_dot(unit_dir, key_rows.T), 0.0)
    carried = lax.linalg.triangular_solve(lower_mat, dir_key, left_side=True, lower=True)
    query_dir = jnp.where(row_ids >= col_ids, exact_dot(query, unit_dir.T), 0.0)
    q_moved = query - exact_dot(query_dir, inner_solve)
    k_moved = key_rows - exact_dot(carried.T, unit_dir)
    inside = exact_dot(query, key_rows.T) - exact_dot(query_dir, carried)
    identity_mat = jnp.eye(query.shape[1], dtype=query.dtype)
    through = identity_mat - exact_dot(unit_dir.T, inner_solve)
    return (q_moved, k_moved, inside, through)


def per_device(
    tokens,
    cotangent,
    starts,
    gain_attn,
    w_query,
    w_key,
    w_value,
    w_dir,
    w_beta,
    w_out,
    gain_mlp,
    w_gate,
    w_up,
    w_down,
):
    highest = lax.Precision.HIGHEST
    row_count = tokens.shape[0]
    seq_place = lax.axis_index("seq")
    group_first = seq_place // SPAN * SPAN
    gathered = (
        lax.all_gather(gain_attn, "seq", axis=0, tiled=True),
        lax.all_gather(w_query, "seq", axis=0, tiled=True),
        lax.all_gather(w_key, "seq", axis=0, tiled=True),
        lax.all_gather(w_value, "seq", axis=0, tiled=True),
        lax.all_gather(w_dir, "seq", axis=0, tiled=True),
        lax.all_gather(w_beta, "seq", axis=0, tiled=True),
        lax.all_gather(w_out, "seq", axis=1, tiled=True),
        lax.all_gather(gain_mlp, "seq", axis=0, tiled=True),
        lax.all_gather(w_gate, "seq", axis=0, tiled=True),
        lax.all_gather(w_up, "seq", axis=0, tiled=True),
        lax.all_gather(w_down, "seq", axis=1, tiled=True),
        lax.all_gather(starts.astype(jnp.bfloat16), "seq", axis=0, tiled=True),
    )
    (
        gain_one,
        full_query,
        full_key,
        full_value,
        full_dir,
        full_beta,
        full_out,
        gain_two,
        full_gate,
        full_up,
        full_down,
        start_row,
    ) = gathered
    gain_one = gain_one.astype(jnp.float32)
    gain_two = gain_two.astype(jnp.float32)
    doc_row = jnp.cumsum(start_row.astype(jnp.int32))
    my_docs = lax.dynamic_slice_in_dim(doc_row, seq_place * row_count, row_count)
    stream = tokens.astype(jnp.float32)
    normed, scale_one = norm_rows(stream, gain_one)
    normed_low = normed.astype(jnp.bfloat16)
    query = jnp.dot(normed_low, full_query, preferred_element_type=jnp.float32)
    key_in = jnp.dot(normed_low, full_key, preferred_element_type=jnp.float32)
    dir_in = jnp.dot(normed_low, full_dir, preferred_element_type=jnp.float32)
    beta_in = jnp.dot(normed_low, full_beta, preferred_element_type=jnp.float32)
    values = jnp.dot(normed_low, full_value, preferred_element_type=jnp.float32).astype(
        jnp.bfloat16
    )
    local_heads = beta_in.shape[1]
    head_dim = query.shape[1] // local_heads

    def split_heads(array_in):
        return array_in.reshape(row_count, local_heads, head_dim).transpose(1, 0, 2)

    def merge_heads(array_in):
        return array_in.transpose(1, 0, 2).reshape(row_count, local_heads * head_dim)

    value_heads = split_heads(values)
    moved_out, pull_block = jax.vjp(
        jax.vmap(householder_block),
        split_heads(query),
        split_heads(key_in),
        split_heads(dir_in),
        beta_in.T,
    )
    q_moved, k_moved, inside, through = moved_out
    score_scale = head_dim ** (-0.5)
    row_ids = lax.broadcasted_iota(jnp.int32, (row_count, row_count), 0)
    col_ids = lax.broadcasted_iota(jnp.int32, (row_count, row_count), 1)
    own_ok = (my_docs[:, None] == my_docs[None, :]) & (row_ids >= col_ids)
    own_scores = jnp.where(own_ok[None], inside * score_scale, NEGATIVE)
    row_peak = jnp.max(own_scores, axis=-1)
    exp_scores = jnp.exp(own_scores - row_peak[..., None])
    row_total = jnp.sum(exp_scores, axis=-1)
    accumulated = jnp.einsum(
        "hij,hjd->hid",
        exp_scores.astype(jnp.bfloat16),
        value_heads,
        preferred_element_type=jnp.float32,
    )

    def cross_scores(moved_keys, anchor):
        key_docs = lax.dynamic_slice_in_dim(
            doc_row, jnp.maximum(anchor, group_first) * row_count, row_count
        )
        allowed = (anchor >= group_first) & (my_docs[:, None] == key_docs[None, :])
        raw_scores = (
            jnp.einsum("hid,hjd->hij", q_moved, moved_keys, precision=highest) * score_scale
        )
        return jnp.where(allowed[None], raw_scores, NEGATIVE)

    def absorb(stats, moved_keys, moved_vals, anchor):
        old_peak, old_total, old_acc = stats
        scores = cross_scores(moved_keys, anchor)
        new_peak = jnp.maximum(old_peak, jnp.max(scores, axis=-1))
        rescale = jnp.exp(old_peak - new_peak)
        exp_new = jnp.exp(scores - new_peak[..., None])
        new_total = old_total * rescale + jnp.sum(exp_new, axis=-1)
        new_acc = old_acc * rescale[..., None] + jnp.einsum(
            "hij,hjd->hid",
            exp_new.astype(jnp.bfloat16),
            moved_vals,
            preferred_element_type=jnp.float32,
        )
        return (new_peak, new_total, new_acc)

    offsets = jnp.arange(1, SPAN, dtype=jnp.int32)
    stats_init = (row_peak, row_total, accumulated)

    def hop_forward(carry, offset):
        send_keys, send_vals, stats = carry
        recv_keys, recv_vals = (
            shifted(send_keys.astype(jnp.bfloat16), "seq", 1).astype(send_keys.dtype),
            shifted(send_vals.astype(jnp.bfloat16), "seq", 1).astype(send_vals.dtype),
        )
        recv_low = recv_vals.astype(jnp.bfloat16)
        stats = absorb(stats, recv_keys, recv_low, seq_place - offset)
        onward = jnp.einsum("hnd,hed->hne", recv_keys, through, precision=highest)
        return ((onward, recv_vals, stats), (recv_keys, recv_low))

    carry_out, kept = lax.scan(
        hop_forward, (k_moved, value_heads.astype(jnp.float32), stats_init), offsets
    )
    stats_final = carry_out[2]
    peak_final, total_final, acc_final = stats_final
    attention = acc_final / total_final[..., None]
    log_total = peak_final + jnp.log(total_final)
    attention_low = merge_heads(attention).astype(jnp.bfloat16)
    branch = lax.psum(
        jnp.dot(attention_low, full_out, preferred_element_type=jnp.float32).astype(jnp.bfloat16),
        "head",
    ).astype(jnp.float32)
    middle = stream + branch
    normed_two, scale_two = norm_rows(middle, gain_two)
    normed_two_low = normed_two.astype(jnp.bfloat16)
    gate_in = jnp.dot(normed_two_low, full_gate, preferred_element_type=jnp.float32)
    up_in = jnp.dot(normed_two_low, full_up, preferred_element_type=jnp.float32)
    gate_sig = jax.nn.sigmoid(gate_in)
    hidden = (gate_in * gate_sig * up_in).astype(jnp.bfloat16)
    mlp_out = lax.psum(
        jnp.dot(hidden, full_down, preferred_element_type=jnp.float32).astype(jnp.bfloat16), "head"
    ).astype(jnp.float32)
    result = (middle + mlp_out).astype(jnp.bfloat16)
    grad_stream = cotangent.astype(jnp.float32)
    d_hidden = jnp.dot(cotangent, full_down.T, preferred_element_type=jnp.float32)
    grad_down = jnp.dot(hidden.T, cotangent, preferred_element_type=jnp.float32)
    d_gate = (d_hidden * up_in * gate_sig * (1.0 + gate_in * (1.0 - gate_sig))).astype(jnp.bfloat16)
    d_up = (d_hidden * gate_in * gate_sig).astype(jnp.bfloat16)
    back_two = jnp.dot(d_gate, full_gate.T, preferred_element_type=jnp.float32) + jnp.dot(
        d_up, full_up.T, preferred_element_type=jnp.float32
    )
    grad_gate = jnp.dot(normed_two_low.T, d_gate, preferred_element_type=jnp.float32)
    grad_up = jnp.dot(normed_two_low.T, d_up, preferred_element_type=jnp.float32)
    d_normed_two = lax.psum(back_two.astype(jnp.bfloat16), "head").astype(jnp.float32)
    d_middle_norm, grad_gain_two = norm_back(d_normed_two, middle, scale_two, gain_two)
    d_middle = grad_stream + d_middle_norm
    d_branch = d_middle.astype(jnp.bfloat16)
    grad_out_w = jnp.dot(attention_low.T, d_branch, preferred_element_type=jnp.float32)
    d_attention = split_heads(
        jnp.dot(d_branch, full_out.T, preferred_element_type=jnp.float32).astype(jnp.bfloat16)
    )
    delta = jnp.sum(d_attention.astype(jnp.float32) * attention, axis=-1)
    own_probs = jnp.exp(own_scores - log_total[..., None])
    own_dprob = jnp.einsum(
        "hid,hjd->hij", d_attention, value_heads, preferred_element_type=jnp.float32
    )
    d_inside = own_probs * (own_dprob - delta[..., None]) * score_scale
    d_vals_own = jnp.einsum(
        "hij,hid->hjd",
        own_probs.astype(jnp.bfloat16),
        d_attention,
        preferred_element_type=jnp.float32,
    )

    def release(moved_keys, moved_vals, anchor):
        scores = cross_scores(moved_keys, anchor)
        probs = jnp.exp(scores - log_total[..., None])
        d_prob = jnp.einsum(
            "hid,hjd->hij", d_attention, moved_vals, preferred_element_type=jnp.float32
        )
        d_scores = probs * (d_prob - delta[..., None]) * score_scale
        d_query = jnp.einsum("hij,hjd->hid", d_scores, moved_keys, precision=highest)
        d_keys = jnp.einsum("hij,hid->hjd", d_scores, q_moved, precision=highest)
        d_vals = jnp.einsum(
            "hij,hid->hjd",
            probs.astype(jnp.bfloat16),
            d_attention,
            preferred_element_type=jnp.float32,
        )
        return (d_query, d_keys, d_vals)

    zero_heads = jnp.zeros_like(q_moved)
    zero_through = jnp.zeros_like(through)
    kept_keys, kept_vals = kept

    def hop_back(carry, inputs):
        back_keys, back_vals, d_query_acc, d_through = carry
        moved_keys, moved_vals, offset = inputs
        d_query, d_keys, d_vals = release(moved_keys, moved_vals, seq_place - offset)
        d_keys = d_keys + jnp.einsum("hne,hed->hnd", back_keys, through, precision=highest)
        d_through = d_through + jnp.einsum("hne,hnd->hed", back_keys, moved_keys, precision=highest)
        d_vals = d_vals + back_vals
        back_keys, back_vals = (
            shifted(d_keys.astype(jnp.bfloat16), "seq", -1).astype(d_keys.dtype),
            shifted(d_vals.astype(jnp.bfloat16), "seq", -1).astype(d_vals.dtype),
        )
        return ((back_keys, back_vals, d_query_acc + d_query, d_through), None)

    carry_back, unused = lax.scan(
        hop_back,
        (zero_heads, zero_heads, zero_heads, zero_through),
        (kept_keys, kept_vals, offsets),
        reverse=True,
    )
    d_k_moved, d_vals_far, d_q_moved, d_through = carry_back
    d_query_h, d_key_h, d_dir_h, d_beta_h = pull_block((d_q_moved, d_k_moved, d_inside, d_through))
    d_query_low = merge_heads(d_query_h).astype(jnp.bfloat16)
    d_key_low = merge_heads(d_key_h).astype(jnp.bfloat16)
    d_dir_low = merge_heads(d_dir_h).astype(jnp.bfloat16)
    d_value_low = merge_heads(d_vals_own + d_vals_far).astype(jnp.bfloat16)
    d_beta_low = d_beta_h.T.astype(jnp.bfloat16)
    back_one = jnp.dot(d_query_low, full_query.T, preferred_element_type=jnp.float32)
    back_one = back_one + jnp.dot(d_key_low, full_key.T, preferred_element_type=jnp.float32)
    back_one = back_one + jnp.dot(d_value_low, full_value.T, preferred_element_type=jnp.float32)
    back_one = back_one + jnp.dot(d_dir_low, full_dir.T, preferred_element_type=jnp.float32)
    back_one = back_one + jnp.dot(d_beta_low, full_beta.T, preferred_element_type=jnp.float32)
    grad_query = jnp.dot(normed_low.T, d_query_low, preferred_element_type=jnp.float32)
    grad_key = jnp.dot(normed_low.T, d_key_low, preferred_element_type=jnp.float32)
    grad_value = jnp.dot(normed_low.T, d_value_low, preferred_element_type=jnp.float32)
    grad_dir = jnp.dot(normed_low.T, d_dir_low, preferred_element_type=jnp.float32)
    grad_beta = jnp.dot(normed_low.T, d_beta_low, preferred_element_type=jnp.float32)
    d_normed = lax.psum(back_one.astype(jnp.bfloat16), "head").astype(jnp.float32)
    d_stream_norm, grad_gain_one = norm_back(d_normed, stream, scale_one, gain_one)
    d_tokens = d_middle + d_stream_norm
    reduced = (
        lax.psum_scatter(
            grad_gain_one.astype(jnp.bfloat16), "seq", scatter_dimension=0, tiled=True
        ).astype(jnp.float32),
        lax.psum_scatter(
            grad_query.astype(jnp.bfloat16), "seq", scatter_dimension=0, tiled=True
        ).astype(jnp.float32),
        lax.psum_scatter(
            grad_key.astype(jnp.bfloat16), "seq", scatter_dimension=0, tiled=True
        ).astype(jnp.float32),
        lax.psum_scatter(
            grad_value.astype(jnp.bfloat16), "seq", scatter_dimension=0, tiled=True
        ).astype(jnp.float32),
        lax.psum_scatter(
            grad_dir.astype(jnp.bfloat16), "seq", scatter_dimension=0, tiled=True
        ).astype(jnp.float32),
        lax.psum_scatter(
            grad_beta.astype(jnp.bfloat16), "seq", scatter_dimension=0, tiled=True
        ).astype(jnp.float32),
        lax.psum_scatter(
            grad_out_w.astype(jnp.bfloat16), "seq", scatter_dimension=1, tiled=True
        ).astype(jnp.float32),
        lax.psum_scatter(
            grad_gain_two.astype(jnp.bfloat16), "seq", scatter_dimension=0, tiled=True
        ).astype(jnp.float32),
        lax.psum_scatter(
            grad_gate.astype(jnp.bfloat16), "seq", scatter_dimension=0, tiled=True
        ).astype(jnp.float32),
        lax.psum_scatter(
            grad_up.astype(jnp.bfloat16), "seq", scatter_dimension=0, tiled=True
        ).astype(jnp.float32),
        lax.psum_scatter(
            grad_down.astype(jnp.bfloat16), "seq", scatter_dimension=1, tiled=True
        ).astype(jnp.float32),
    )
    return (result, d_tokens) + tuple(reduced)


def solution(mesh):
    placed = (
        P("seq", None),
        P("seq", None),
        P("seq"),
        P("seq"),
        P("seq", "head"),
        P("seq", "head"),
        P("seq", "head"),
        P("seq", "head"),
        P("seq", "head"),
        P("head", "seq"),
        P("seq"),
        P("seq", "head"),
        P("seq", "head"),
        P("head", "seq"),
    )
    return jax.shard_map(
        per_device,
        mesh=mesh,
        in_specs=placed,
        out_specs=(
            P("seq", None),
            P("seq", None),
            P("seq"),
            P("seq", "head"),
            P("seq", "head"),
            P("seq", "head"),
            P("seq", "head"),
            P("seq", "head"),
            P("head", "seq"),
            P("seq"),
            P("seq", "head"),
            P("seq", "head"),
            P("head", "seq"),
        ),
        check_vma=False,
    )
```

profile of v0, /device:TPU:0, one launch (start us, length us, event | category | flops | bytes accessed | tf_op | source)
XLA Modules:
  0.0 1560.6 jit_solution(2317792008611411234)
XLA Ops:
  17.2 16.1 %all-reduce.5 = (bf16[1536]{0:T(1024)(128)(2,1)S(1)}, bf16[1536]{0:T(1024)(128)(2,1)}) all-reduce(bf16[1536]{0:T(1024)(128)(2,1)S(1)} %dynamic-update-slice.7, bf16[1536]{0:T(1024)(128)(2,1)S(1)} %dynamic-update-slice.8), channel_id=1, replica_groups=mesh['head'=4,'seq'=8] {'seq'}, use_global_device_ids=true, to_apply=%add | all-reduce | flops 3072 | bytes 12288
  35.2 7.9 all-gather
  44.4 9.2 all-gather.1
  79.1 14.8 while.51
  93.9 119.2 %custom-call.11 = f32[3,4,128,128]{2,3,1,0:T(8,128)S(1)} custom-call(f32[3,4,128,128]{3,2,1,0:T(8,128)} %bitcast.351), custom_call_target="InvertDiagBlocksLowerTriangular" | custom-call | tf_op jit(solution)/shard_map/jvp(vmap())/triangular_solve | solution.py:47
  274.0 134.2 %while.50 = (s32[]{:T(128)}, bf16[3,512,128]{2,1,0:T(8,128)(2,1)}, bf16[3,512,128]{2,1,0:T(8,128)(2,1)}, f32[3,512]{1,0:T(4,128)S(1)}, f32[3,512]{1,0:T(4,128)S(...) while((s32[]{:T(128)}, bf16[3,512,128]{2,1,0:T(8,128)(2,1)}, ...), condition=%wide.region_9.10_spmd, body=%wide.region_6.9_spmd.sunk | while | flops 1721043968 | bytes 26911140 | solution.py:191
  416.0 71.8 %all-reduce.11.cloned.1.call-done = bf16[512,1536]{1,0:T(8,128)(2,1)} async-done(((bf16[512,1536]{1,0:T(8,128)(2,1)}), bf16[512,1536]{1,0:T(8,128)(2,1)}) %all-reduce.11.cloned.1.call-update) | async-done | bytes 1572880 | tf_op jit(solution)/shard_map/psum | solution.py:199
  491.6 29.4 %all-gather.21.cloned.1.call-done = bf16[1536,1024]{1,0:T(8,128)(2,1)} async-done(((bf16[192,1024]{1,0:T(8,128)(2,1)}), bf16[1536,1024]{1,0:T(8,128)(2,1)}) %all-gather.21.cloned.1.call-update) | async-done | bytes 3145744 | tf_op jit(solution)/shard_map/all_gather | solution.py:86
  526.5 28.8 %all-gather.23.cloned.1.call-done = bf16[1536,1024]{1,0:T(8,128)(2,1)} async-done(((bf16[192,1024]{1,0:T(8,128)(2,1)}), bf16[1536,1024]{1,0:T(8,128)(2,1)}) %all-gather.23.cloned.1.call-update) | async-done | bytes 3145744 | tf_op jit(solution)/shard_map/all_gather | solution.py:87
  560.8 28.7 %all-gather.25.cloned.1.call-done = bf16[1024,1536]{0,1:T(8,128)(2,1)} async-done(((bf16[1024,192]{0,1:T(8,128)(2,1)}), bf16[1024,1536]{0,1:T(8,128)(2,1)}) %all-gather.25.cloned.1.call-update) | async-done | bytes 3145744 | tf_op jit(solution)/shard_map/all_gather | solution.py:88
  602.5 69.2 %all-reduce.13.cloned.1.call-done = bf16[512,1536]{1,0:T(8,128)(2,1)} async-done(((bf16[512,1536]{1,0:T(8,128)(2,1)}), bf16[512,1536]{1,0:T(8,128)(2,1)}) %all-reduce.13.cloned.1.call-update) | async-done | bytes 1572880 | tf_op jit(solution)/shard_map/psum | solution.py:224
  691.1 255.7 %while.52 = (s32[]{:T(128)}, f32[3,512,128]{2,1,0:T(8,128)}, f32[3,512,128]{2,1,0:T(8,128)}, f32[3,512,128]{2,1,0:T(8,128)}, f32[3,128,128]{1,2,0:T(8,128)}, /*i...) while((s32[]{:T(128)}, f32[3,512,128]{2,1,0:T(8,128)}, ...), condition=%wide.region_17.18_spmd.clone, body=%wide.region_16.17_spmd.clone.sunk | while | flops 4641161216 | bytes 57667644 | solution.py:279
  961.3 10.5 fusion.116
  980.6 10.5 add_select_fusion
  1056.3 8.2 fusion.321
  1125.6 26.6 %reduce-scatter.14.cloned.1.call-done = bf16[192,384]{1,0:T(8,128)(2,1)} async-done(((bf16[1536,384]{1,0:T(8,128)(2,1)}), bf16[192,384]{1,0:T(8,128)(2,1)}) %reduce-scatter.14.cloned.1.call-update) | async-done | bytes 147472 | tf_op jit(solution)/shard_map/reduce_scatter | solution.py:312
  1153.8 38.2 %reduce-scatter.16.cloned.1.call-done = bf16[192,384]{1,0:T(8,128)(2,1)} async-done(((bf16[1536,384]{1,0:T(8,128)(2,1)}), bf16[192,384]{1,0:T(8,128)(2,1)}) %reduce-scatter.16.cloned.1.call-update) | async-done | bytes 147472 | tf_op jit(solution)/shard_map/reduce_scatter | solution.py:315
  1193.7 38.6 %reduce-scatter.18.cloned.1.call-done = bf16[192,384]{1,0:T(8,128)(2,1)} async-done(((bf16[1536,384]{1,0:T(8,128)(2,1)}), bf16[192,384]{1,0:T(8,128)(2,1)}) %reduce-scatter.18.cloned.1.call-update) | async-done | bytes 147472 | tf_op jit(solution)/shard_map/reduce_scatter | solution.py:318
  1233.9 38.2 %reduce-scatter.20.cloned.1.call-done = bf16[384,192]{0,1:T(8,128)(2,1)} async-done(((bf16[384,1536]{0,1:T(8,128)(2,1)}), bf16[384,192]{0,1:T(8,128)(2,1)}) %reduce-scatter.20.cloned.1.call-update) | async-done | bytes 147472 | tf_op jit(solution)/shard_map/reduce_scatter | solution.py:324
  1273.8 48.2 %reduce-scatter.22.cloned.1.call-done = bf16[192,1024]{1,0:T(8,128)(2,1)} async-done(((bf16[1536,1024]{1,0:T(8,128)(2,1)}), bf16[192,1024]{1,0:T(8,128)(2,1)}) %reduce-scatter.22.cloned.1.call-update) | async-done | bytes 393232 | tf_op jit(solution)/shard_map/reduce_scatter | solution.py:330
  1324.0 47.6 %reduce-scatter.24.cloned.1.call-done = bf16[192,1024]{1,0:T(8,128)(2,1)} async-done(((bf16[1536,1024]{1,0:T(8,128)(2,1)}), bf16[192,1024]{1,0:T(8,128)(2,1)}) %reduce-scatter.24.cloned.1.call-update) | async-done | bytes 393232 | tf_op jit(solution)/shard_map/reduce_scatter | solution.py:333
  1373.5 122.6 %all-reduce.15.cloned.1.call-done = (bf16[512,1536]{1,0:T(8,128)(2,1)}, bf16[512,1536]{1,0:T(8,128)(2,1)}) async-done(((bf16[512,1536]{1,0:T(8,128)(2,1)}, bf16[512,1536]{1,0:T(8,128)(2,1)}), (bf16[512,1536]{1,0:T(8,128)(2,1)}, bf16[512,1536]{1,0:T(8,128)(2,1)})) %all-reduce.15.cloned.1.call-update) | async-done | bytes 3145744 | tf_op jit(solution)/shard_map/psum | solution.py:210
  1498.7 13.9 all-reduce.4
  1513.9 31.1 %reduce-scatter.26.cloned.1.call-done = bf16[1024,192]{0,1:T(8,128)(2,1)} async-done(((bf16[1024,1536]{0,1:T(8,128)(2,1)}), bf16[1024,192]{0,1:T(8,128)(2,1)}) %reduce-scatter.26.cloned.1.call-update) | async-done | bytes 393232 | tf_op jit(solution)/shard_map/reduce_scatter | solution.py:336
  (836 shorter events, 716.8 us)
Async XLA Ops:
  7.2 48.4 %all-gather.13.cloned.1.call-start = ((), (), s32[]{:S(2)}) async-start(), calls=%async_computation.10 | async-start | bytes 1327104 | tf_op jit(solution)/shard_map/all_gather | solution.py:82
  7.9 54.9 %all-gather.11.cloned.1.call-start = ((), (), s32[]{:S(2)}) async-start(), calls=%async_computation.9 | async-start | bytes 1327104 | tf_op jit(solution)/shard_map/all_gather | solution.py:80
  8.7 219.9 %all-gather.15.cloned.1.call-start = ((), (), s32[]{:S(2)}) async-start(), calls=%async_computation.11 | async-start | bytes 1327104 | tf_op jit(solution)/shard_map/all_gather | solution.py:81
  9.4 224.0 %all-gather.17.cloned.1.call-start = ((), (), s32[]{:S(2)}) async-start(), calls=%async_computation.12 | async-start | bytes 1327104 | tf_op jit(solution)/shard_map/all_gather | solution.py:79
  10.0 399.7 %all-gather.19.cloned.1.call-start = ((), (), s32[]{:S(2)}) async-start(), calls=%async_computation.13 | async-start | bytes 1327104 | tf_op jit(solution)/shard_map/all_gather | solution.py:84
  10.6 477.2 %all-reduce.11.cloned.1.call-start = ((), (), s32[]{:S(2)}) async-start(), calls=%async_computation.14 | async-start | bytes 3145728 | tf_op jit(solution)/shard_map/psum | solution.py:199
  413.5 107.6 %all-gather.21.cloned.1.call-start = ((), (), s32[]{:S(2)}) async-start(), calls=%async_computation.15 | async-start | bytes 3538944 | tf_op jit(solution)/shard_map/all_gather | solution.py:86
  414.2 141.0 %all-gather.23.cloned.1.call-start = ((), (), s32[]{:S(2)}) async-start(), calls=%async_computation.16 | async-start | bytes 3538944 | tf_op jit(solution)/shard_map/all_gather | solution.py:87
  415.0 174.5 %all-gather.25.cloned.1.call-start = ((), (), s32[]{:S(2)}) async-start(), calls=%async_computation.17 | async-start | bytes 3538944 | tf_op jit(solution)/shard_map/all_gather | solution.py:88
  415.7 255.9 %all-reduce.13.cloned.1.call-start = ((), (), s32[]{:S(2)}) async-start(), calls=%async_computation.18 | async-start | bytes 3145728 | tf_op jit(solution)/shard_map/psum | solution.py:224
  602.4 520.1 %reduce-scatter.28.cloned.1.call-start = ((), (), s32[]{:S(2)}) async-start(), calls=%async_computation.27 | async-start | bytes 442368
  745.3 16.9 %collective-permute-start.2 = (bf16[3,512,128]{2,1,0:T(8,128)(2,1)}, bf16[3,512,128]{2,1,0:T(8,128)(2,1)}, u32[]{:S(2)}, u32[]{:S(2)}) collective-permute-start(bf16[3,512,128]{2,1,0:T(8,128)(2,1)} %fusion.478), channel_id=1, source_target_pairs={{1,0},{2,1},{3,2},{4,3},{5,4},{6,5},{7,6},{9,8},{10,9},{11,10},{12... | collective-permute-start | bytes 1179656 | tf_op jit(solution)/shard_map/while/body/eval_jaxpr/ppermute | solution.py:16
  818.2 16.9 %collective-permute-start.2 = (bf16[3,512,128]{2,1,0:T(8,128)(2,1)}, bf16[3,512,128]{2,1,0:T(8,128)(2,1)}, u32[]{:S(2)}, u32[]{:S(2)}) collective-permute-start(bf16[3,512,128]{2,1,0:T(8,128)(2,1)} %fusion.478), channel_id=1, source_target_pairs={{1,0},{2,1},{3,2},{4,3},{5,4},{6,5},{7,6},{9,8},{10,9},{11,10},{12... | collective-permute-start | bytes 1179656 | tf_op jit(solution)/shard_map/while/body/eval_jaxpr/ppermute | solution.py:16
  891.0 16.9 %collective-permute-start.2 = (bf16[3,512,128]{2,1,0:T(8,128)(2,1)}, bf16[3,512,128]{2,1,0:T(8,128)(2,1)}, u32[]{:S(2)}, u32[]{:S(2)}) collective-permute-start(bf16[3,512,128]{2,1,0:T(8,128)(2,1)} %fusion.478), channel_id=1, source_target_pairs={{1,0},{2,1},{3,2},{4,3},{5,4},{6,5},{7,6},{9,8},{10,9},{11,10},{12... | collective-permute-start | bytes 1179656 | tf_op jit(solution)/shard_map/while/body/eval_jaxpr/ppermute | solution.py:16
  927.5 17.2 %collective-permute-start.2 = (bf16[3,512,128]{2,1,0:T(8,128)(2,1)}, bf16[3,512,128]{2,1,0:T(8,128)(2,1)}, u32[]{:S(2)}, u32[]{:S(2)}) collective-permute-start(bf16[3,512,128]{2,1,0:T(8,128)(2,1)} %fusion.478), channel_id=1, source_target_pairs={{1,0},{2,1},{3,2},{4,3},{5,4},{6,5},{7,6},{9,8},{10,9},{11,10},{12... | collective-permute-start | bytes 1179656 | tf_op jit(solution)/shard_map/while/body/eval_jaxpr/ppermute | solution.py:16
  1025.8 98.1 %reduce-scatter.12.cloned.1.call-start = ((), (), s32[]{:S(2)}) async-start(), calls=%async_computation.19 | async-start | bytes 1327104 | tf_op jit(solution)/shard_map/reduce_scatter | solution.py:309
  1031.2 121.0 %reduce-scatter.14.cloned.1.call-start = ((), (), s32[]{:S(2)}) async-start(), calls=%async_computation.20 | async-start | bytes 1327104 | tf_op jit(solution)/shard_map/reduce_scatter | solution.py:312
  1047.9 144.2 %reduce-scatter.16.cloned.1.call-start = ((), (), s32[]{:S(2)}) async-start(), calls=%async_computation.21 | async-start | bytes 1327104 | tf_op jit(solution)/shard_map/reduce_scatter | solution.py:315
  1074.7 157.6 %reduce-scatter.18.cloned.1.call-start = ((), (), s32[]{:S(2)}) async-start(), calls=%async_computation.22 | async-start | bytes 1327104 | tf_op jit(solution)/shard_map/reduce_scatter | solution.py:318
  1087.9 184.2 %reduce-scatter.20.cloned.1.call-start = ((), (), s32[]{:S(2)}) async-start(), calls=%async_computation.23 | async-start | bytes 1327104 | tf_op jit(solution)/shard_map/reduce_scatter | solution.py:324
  1092.4 229.6 %reduce-scatter.22.cloned.1.call-start = ((), (), s32[]{:S(2)}) async-start(), calls=%async_computation.24 | async-start | bytes 3538944 | tf_op jit(solution)/shard_map/reduce_scatter | solution.py:330
  1097.4 274.2 %reduce-scatter.24.cloned.1.call-start = ((), (), s32[]{:S(2)}) async-start(), calls=%async_computation.25 | async-start | bytes 3538944 | tf_op jit(solution)/shard_map/reduce_scatter | solution.py:333
  1103.6 392.5 %all-reduce.15.cloned.1.call-start = ((), (), s32[]{:S(2)}) async-start(), calls=%async_computation.28 | async-start | bytes 6291456 | tf_op jit(solution)/shard_map/psum | solution.py:210
  1116.8 428.2 %reduce-scatter.26.cloned.1.call-start = ((), (), s32[]{:S(2)}) async-start(), calls=%async_computation.26 | async-start | bytes 3538944 | tf_op jit(solution)/shard_map/reduce_scatter | solution.py:336
  (214 other events, 2692.6 us)
Sparse Core Ops, SparseCore 0:
  9.9 26.9 all-gather.12
  38.8 23.9 all-gather.10
  64.7 24.0 all-gather.14
  90.6 24.4 all-gather.16
  116.8 24.5 all-gather.18
  413.6 74.1 all-reduce.10
  489.6 31.3 all-gather.20
  522.9 32.3 all-gather.22
  557.2 32.3 all-gather.24
  602.5 69.1 all-reduce.12
  1025.9 45.9 reduce-scatter.27
  1075.0 36.7 reduce-scatter.11
  1115.4 36.7 reduce-scatter.13
  1155.3 36.7 reduce-scatter.15
  1195.5 36.7 reduce-scatter.17
  1235.4 36.7 reduce-scatter.19
  1275.8 46.2 reduce-scatter.21
  1325.3 46.2 reduce-scatter.23
  1374.7 121.4 all-reduce.14
  1499.7 45.2 reduce-scatter.25
where the time goes:
time: 1570 us; the launch traced here: 1560 us
  waiting for transfers between devices  629 us (40%)
  matrix products  487 us (31%)
  other arithmetic  208 us (13%)
  local copies, waits for them, and re-layouts  90 us (6%)
  starting transfers between devices  70.4 us (4%)
  blocking collectives  47.1 us (3%)
  between operations  17.9 us (1%)
    psum x1, waiting for transfers between devices, per_device(): lax.psum(jnp.dot(hidden, full_down, preferred_element_type=jnp.float32).a...  123 us
    another operation x2, other arithmetic, householder_block(): lax.linalg.triangular_solve(lower_mat, dir_key, left_side=True, lower=True)  119 us
    dot_general x24, matrix products, exact_dot(): return jnp.matmul(left, right, precision=lax.Precision.HIGHEST)  110 us
    psum x1, waiting for transfers between devices, per_device(): lax.psum(jnp.dot(attention_low, full_out, preferred_element_type=jnp.floa...  71.8 us
    psum x1, waiting for transfers between devices, per_device(): lax.psum(back_two.astype(jnp.bfloat16), 'head').astype(jnp.float32)  69.2 us
    ppermute x28, starting transfers between devices, shifted(): lax.ppermute(value, axis, [(source, source + steps) for source in range(i...  68.3 us
    dot_general x14, matrix products, cross_scores(): jnp.einsum('hid,hjd->hij', q_moved, moved_keys, precision=highest)  60.9 us
    dot_general x7, matrix products, release(): jnp.einsum('hij,hjd->hid', d_scores, moved_keys, precision=highest)  51 us
  transfers between devices with their start and end apart: 48, of which 15 were waited for; matrix products, arithmetic and copies ran while one was open for 33% of the time, Pallas kernels for 0%

commit v1 on v0

v1 whole, which is shorter than its diff:
```python
import functools

import jax
import jax.numpy as jnp
from jax import lax
from jax.experimental import pallas as pl
from jax.experimental.pallas import tpu as pltpu
from jax.sharding import PartitionSpec as P

SPAN = 8
EPSILON = 1e-06
NEGATIVE = -1e30
LOW = jnp.bfloat16
WIDE = jnp.float32
VMEM_BYTES = 48 * 2**20


def mm(left, right, ta=False, tb=False):
    dims = (((0 if ta else 1,), (1 if tb else 0,)), ((), ()))
    return lax.dot_general(
        left.astype(LOW), right.astype(LOW), dims, preferred_element_type=WIDE
    )


def halves(value):
    high = value.astype(LOW)
    return high, (value - high.astype(WIDE)).astype(LOW)


def mm3(left, right, ta=False, tb=False):
    left_hi, left_lo = left if isinstance(left, tuple) else halves(left)
    right_hi, right_lo = right if isinstance(right, tuple) else halves(right)
    return mm(left_hi, right_hi, ta, tb) + (mm(left_hi, right_lo, ta, tb) + mm(left_lo, right_hi, ta, tb))


def iota(shape, axis):
    return lax.broadcasted_iota(jnp.int32, shape, axis)


def lower_inverse(strict, beta):
    length = strict.shape[0]
    size = 128
    row, col = iota((size, size), 0), iota((size, size), 1)
    subs, blocks = [], []
    for at in range(0, length, size):
        sub = strict[at : at + size, at : at + size]
        scale = beta[at : at + size]
        diag = jnp.where(row == col, scale, 0.0)
        across = jnp.sum(diag, axis=0, keepdims=True)
        pair = ((row >> 1) == (col >> 1)) & (row > col)
        subs.append(sub)
        blocks.append(diag - jnp.where(pair, sub * scale * across, 0.0))
    bit = 1
    while (1 << bit) < size:
        mask = ((row >> (bit + 1)) == (col >> (bit + 1))) & ((row >> bit) != (col >> bit)) & (row > col)
        right = [mm3(jnp.where(mask, sub, 0.0), block) for sub, block in zip(subs, blocks)]
        blocks = [block - mm3(block, part) for block, part in zip(blocks, right)]
        bit += 1
    while len(blocks) > 1:
        size = blocks[0].shape[0]
        joined = []
        for pair_at in range(len(blocks) // 2):
            first, second = blocks[2 * pair_at], blocks[2 * pair_at + 1]
            at = 2 * pair_at * size
            corner = -mm3(second, mm3(strict[at + size : at + 2 * size, at : at + size], first))
            joined.append(
                jnp.concatenate(
                    [
                        jnp.concatenate([first, jnp.zeros_like(first)], axis=1),
                        jnp.concatenate([corner, second], axis=1),
                    ],
                    axis=0,
                )
            )
        blocks = joined
    return blocks[0]


def pick_beta(beta_ref, head):
    tile = beta_ref[...]
    raw = jnp.sum(jnp.where(iota(tile.shape, 1) == head, tile, 0.0), axis=1, keepdims=True)
    return 2.0 * jax.nn.sigmoid(raw)


def block_forward(
    q_ref, k_ref, v_ref, d_ref, beta_ref, doc_col_ref, doc_row_ref,
    pack_ref, qm_ref, score_ref, inv_ref, carried_ref, qdir_ref, solve_ref, peak_ref, total_ref, acc_ref,
):
    query, key, dirs = q_ref[...], k_ref[...], d_ref[...]
    length, dim = query.shape
    beta = pick_beta(beta_ref, pl.program_id(0))
    unit = dirs * lax.rsqrt(jnp.sum(dirs * dirs, axis=-1, keepdims=True) + EPSILON)
    row, col = iota((length, length), 0), iota((length, length), 1)
    unit_two = halves(unit)
    strict = jnp.where(row > col, mm3(unit_two, unit_two, tb=True), 0.0)
    inverse = lower_inverse(strict, beta)
    inverse_two = halves(inverse)
    solve = mm3(inverse_two, unit_two)
    solve_two = halves(solve)
    dir_key = jnp.where(row > col, mm3(unit_two, key, tb=True), 0.0)
    carried = mm3(inverse_two, dir_key)
    carried_two = halves(carried)
    qdir = jnp.where(row >= col, mm3(query, unit_two, tb=True), 0.0)
    qdir_two = halves(qdir)
    qm_ref[...] = query - mm3(qdir_two, solve_two)
    value = v_ref[...].astype(LOW)
    pack_ref[0:length, :] = (key - mm3(carried_two, unit_two, ta=True)).astype(LOW)
    pack_ref[length : 2 * length, :] = value
    eye = jnp.where(iota((dim, dim), 0) == iota((dim, dim), 1), 1.0, 0.0)
    pack_ref[2 * length :, :] = (eye - mm3(unit_two, solve_two, ta=True)).astype(LOW)
    inside = mm(query, key, tb=True) - mm(qdir_two[0], carried_two[0])
    inv_ref[...] = inverse.astype(LOW)
    carried_ref[...] = carried.astype(LOW)
    qdir_ref[...] = qdir.astype(LOW)
    solve_ref[...] = solve.astype(LOW)
    allowed = (doc_col_ref[...] == doc_row_ref[...]) & (row >= col)
    score = jnp.where(allowed, inside * dim**-0.5, NEGATIVE)
    score_ref[...] = score
    peak = jnp.max(score, axis=1, keepdims=True)
    weight = jnp.exp(score - peak)
    peak_ref[...] = jnp.broadcast_to(peak, (length, dim))
    total_ref[...] = jnp.broadcast_to(jnp.sum(weight, axis=1, keepdims=True), (length, dim))
    acc_ref[...] = mm(weight, value)


def cross_forward(
    place_ref, qm_ref, pack_ref, peak_ref, total_ref, acc_ref, doc_col_ref, doc_row_ref,
    att_ref, att_low_ref, log_ref, moved_ref, stat_ref,
):
    length, dim = qm_ref.shape
    stride = 2 * length + dim
    place = place_ref[0]
    doc_col = doc_col_ref[...]

    moved_ref[...] = qm_ref[...]
    att_ref[...] = acc_ref[...]
    stat_ref[0] = peak_ref[:, 0:1]
    stat_ref[1] = total_ref[:, 0:1]

    def hop(step, carry):
        at = place - step
        base = pl.multiple_of(at * stride, 128)
        key = pack_ref[pl.ds(base, length), :]
        value = pack_ref[pl.ds(pl.multiple_of(base + length, 128), length), :]
        through = pack_ref[pl.ds(pl.multiple_of(base + 2 * length, 128), dim), :]
        allowed = doc_col == doc_row_ref[at]
        moved = moved_ref[...]
        peak = stat_ref[0]
        score = jnp.where(allowed, mm(moved, key, tb=True) * dim**-0.5, NEGATIVE)
        new_peak = jnp.maximum(peak, jnp.max(score, axis=1, keepdims=True))
        rescale = jnp.exp(peak - new_peak)
        weight = jnp.exp(score - new_peak)
        stat_ref[0] = new_peak
        stat_ref[1] = stat_ref[1] * rescale + jnp.sum(weight, axis=1, keepdims=True)
        att_ref[...] = att_ref[...] * rescale + mm(weight, value)
        moved_ref[...] = mm(moved, through)
        return carry

    lax.fori_loop(1, place + 1, hop, 0)
    total = stat_ref[1]
    attention = att_ref[...] / total
    att_ref[...] = attention
    att_low_ref[...] = attention.astype(LOW)
    log_ref[...] = jnp.broadcast_to(stat_ref[0] + jnp.log(total), (length, dim))


def cross_backward(
    place_ref, qm_ref, pack_ref, score_ref, att_ref, log_ref, datt_ref, doc_col_ref, doc_row_ref,
    dpack_ref, dqm_ref, dinside_ref, dval_ref, chain_ref, dchain_ref,
):
    length, dim = qm_ref.shape
    stride = 2 * length + dim
    place = place_ref[0]
    doc_col = doc_col_ref[...]
    scale = dim**-0.5
    datt = datt_ref[...]
    log_total = log_ref[:, 0:1]
    delta = jnp.sum(datt.astype(WIDE) * att_ref[...], axis=1, keepdims=True)
    own = pl.multiple_of(place * stride, 128)
    value = pack_ref[pl.ds(pl.multiple_of(own + length, 128), length), :]
    probs = jnp.exp(score_ref[...] - log_total)
    dprob = mm(datt, value, tb=True)
    dinside_ref[...] = (probs * (dprob - delta) * scale).astype(LOW)
    dval_ref[...] = mm(probs, datt, ta=True)
    chain_ref[1] = qm_ref[...]

    def blank(at, carry):
        base = pl.multiple_of(at * stride, 128)
        dpack_ref[pl.ds(base, stride), :] = jnp.zeros((stride, dim), LOW)
        return carry

    lax.fori_loop(place, SPAN, blank, 0)

    def hop(step, carry):
        at = place - step
        base = pl.multiple_of(at * stride, 128)
        moved = chain_ref[step]
        key = pack_ref[pl.ds(base, length), :]
        value = pack_ref[pl.ds(pl.multiple_of(base + length, 128), length), :]
        through = pack_ref[pl.ds(pl.multiple_of(base + 2 * length, 128), dim), :]
        chain_ref[step + 1] = mm(moved, through)
        allowed = doc_col == doc_row_ref[at]
        score = jnp.where(allowed, mm(moved, key, tb=True) * scale, NEGATIVE)
        probs = jnp.exp(score - log_total)
        dprob = mm(datt, value, tb=True)
        dscore = probs * (dprob - delta) * scale
        dchain_ref[step] = mm(dscore, key)
        dpack_ref[pl.ds(base, length), :] = mm(dscore, moved, ta=True).astype(LOW)
        dpack_ref[pl.ds(pl.multiple_of(base + length, 128), length), :] = mm(probs, datt, ta=True).astype(LOW)
        return carry

    lax.fori_loop(1, place + 1, hop, 0)

    def back(count, carry):
        step = place - count
        base = pl.multiple_of((place - step) * stride + 2 * length, 128)
        through = pack_ref[pl.ds(base, dim), :]
        grad = dqm_ref[...]
        dpack_ref[pl.ds(base, dim), :] = mm(chain_ref[step], grad, ta=True).astype(LOW)
        dqm_ref[...] = dchain_ref[step] + mm(grad, through, tb=True)
        return carry

    dqm_ref[...] = jnp.zeros((length, dim), WIDE)
    lax.fori_loop(0, place, back, 0)


def block_backward(
    q_ref, k_ref, d_ref, beta_ref, inv_ref, carried_ref, qdir_ref, solve_ref,
    dqm_ref, dinside_ref, dval_ref, dpack_ref,
    dq_ref, dk_ref, dv_ref, dd_ref, dbeta_ref,
):
    head = pl.program_id(0)
    query, key, dirs = q_ref[...], k_ref[...], d_ref[...]
    length, dim = query.shape
    beta = pick_beta(beta_ref, head)
    norm = lax.rsqrt(jnp.sum(dirs * dirs, axis=-1, keepdims=True) + EPSILON)
    unit = dirs * norm
    low_unit, low_key, low_query = unit.astype(LOW), key.astype(LOW), query.astype(LOW)
    row, col = iota((length, length), 0), iota((length, length), 1)
    inverse, carried, qdir, solve = inv_ref[...], carried_ref[...], qdir_ref[...], solve_ref[...]
    dqm, dinside = dqm_ref[...].astype(LOW), dinside_ref[...]
    dkm = dpack_ref[0:length, :]
    dthrough = dpack_ref[2 * length :, :]
    dv_ref[...] = (dval_ref[...] + dpack_ref[length : 2 * length, :].astype(WIDE)).astype(LOW)
    dqdir = -jnp.where(row >= col, mm(dqm, solve, tb=True) + mm(dinside, carried, tb=True), 0.0).astype(LOW)
    dq_ref[...] = (dqm_ref[...] + mm(dinside, low_key) + mm(dqdir, low_unit)).astype(LOW)
    dsolve = -(mm(qdir, dqm, ta=True) + mm(low_unit, dthrough))
    dcarried = -(mm(low_unit, dkm, tb=True) + mm(qdir, dinside, ta=True))
    ysolve = mm(inverse, dsolve, ta=True)
    ycarried = mm(inverse, dcarried, ta=True)
    ddir_key = jnp.where(row > col, ycarried, 0.0).astype(LOW)
    dlower = -(mm(ysolve, solve, tb=True) + mm(ycarried, carried, tb=True))
    ddiag = jnp.sum(jnp.where(row == col, dlower, 0.0), axis=1, keepdims=True)
    dgram = jnp.where(row > col, dlower, 0.0).astype(LOW)
    dk_ref[...] = (dkm.astype(WIDE) + mm(dinside, low_query, ta=True) + mm(ddir_key, low_unit, ta=True)).astype(LOW)
    dunit = (
        ysolve
        - mm(solve, dthrough, tb=True)
        - mm(carried, dkm)
        + mm(dqdir, low_query, ta=True)
        + mm(ddir_key, low_key)
        + mm(dgram, low_unit)
        + mm(dgram, low_unit, ta=True)
    )
    along = jnp.sum(dunit * dirs, axis=1, keepdims=True)
    dd_ref[...] = (norm * dunit - dirs * (norm * norm * norm * along)).astype(LOW)
    dbeta = -ddiag / jnp.maximum(beta, 1e-30) * (1.0 - 0.5 * beta)
    lane = iota(dbeta_ref.shape, 1)

    @pl.when(head == 0)
    def start():
        dbeta_ref[...] = jnp.zeros_like(dbeta_ref)

    dbeta_ref[...] = jnp.where(lane == head, dbeta.astype(LOW), dbeta_ref[...])


def column(rows, cols, offset=0):
    return pl.BlockSpec((rows, cols), lambda head, *unused, offset=offset: (0, head + offset))


def stacked(rows, cols):
    return pl.BlockSpec((rows, cols), lambda head, *unused: (head, 0))


def fixed(shape):
    return pl.BlockSpec(shape, lambda head, *unused: (0,) * len(shape))


def params():
    return pltpu.CompilerParams(vmem_limit_bytes=VMEM_BYTES)


def shape_of(rows, cols, dtype):
    return jax.ShapeDtypeStruct((rows, cols), dtype)


def dot(left, right, ta=False, tb=False):
    dims = (((0 if ta else 1,), (1 if tb else 0,)), ((), ()))
    return lax.dot_general(left, right, dims, preferred_element_type=WIDE)


def norm_back(grad, value, scale, gain):
    weighted = grad * gain
    return scale * weighted - value * scale * scale * scale * jnp.mean(weighted * value, axis=-1, keepdims=True)


def run_block_forward(proj, my_docs_col, my_docs, heads, inner):
    row_count = proj.shape[0]
    dim = inner // heads
    stride = 2 * row_count + dim
    wide_block = column(row_count, dim)
    square = stacked(row_count, row_count)
    beta_spec = pl.BlockSpec((row_count, 128), lambda head, *unused: (0, 4 * inner // 128))
    square_low = shape_of(heads * row_count, row_count, LOW)
    tall_wide = shape_of(row_count, inner, WIDE)
    return pl.pallas_call(
        block_forward,
        grid=(heads,),
        in_specs=[
            column(row_count, dim),
            column(row_count, dim, heads),
            column(row_count, dim, 2 * heads),
            column(row_count, dim, 3 * heads),
            beta_spec,
            fixed((row_count, 1)),
            fixed((1, row_count)),
        ],
        out_specs=[column(stride, dim), wide_block, square, square, square, square, wide_block, wide_block, wide_block, wide_block],
        out_shape=[
            shape_of(stride, inner, LOW),
            tall_wide,
            shape_of(heads * row_count, row_count, WIDE),
            square_low,
            square_low,
            square_low,
            shape_of(row_count, inner, LOW),
            tall_wide,
            tall_wide,
            tall_wide,
        ],
        compiler_params=params(),
        name="block_forward",
    )(proj, proj, proj, proj, proj, my_docs_col, my_docs)


def run_cross_forward(place, q_moved, packs, peak, total, acc, my_docs_col, docs, heads):
    row_count, inner = q_moved.shape
    dim = inner // heads
    wide_block = column(row_count, dim)
    tall_wide = shape_of(row_count, inner, WIDE)
    return pl.pallas_call(
        cross_forward,
        grid_spec=pltpu.PrefetchScalarGridSpec(
            num_scalar_prefetch=1,
            grid=(heads,),
            in_specs=[
                wide_block,
                column(packs.shape[0], dim),
                wide_block,
                wide_block,
                wide_block,
                fixed((row_count, 1)),
                fixed((SPAN, 1, row_count)),
            ],
            out_specs=[wide_block, wide_block, wide_block],
            scratch_shapes=[pltpu.VMEM((row_count, dim), WIDE), pltpu.VMEM((2, row_count, 1), WIDE)],
        ),
        out_shape=[tall_wide, shape_of(row_count, inner, LOW), tall_wide],
        compiler_params=params(),
        name="cross_forward",
    )(place, q_moved, packs, peak, total, acc, my_docs_col, docs)


def run_cross_backward(place, q_moved, packs, own_scores, attention, log_total, d_attention, my_docs_col, docs, heads):
    row_count, inner = q_moved.shape
    dim = inner // heads
    wide_block = column(row_count, dim)
    packs_spec = column(packs.shape[0], dim)
    square = stacked(row_count, row_count)
    tall_wide = shape_of(row_count, inner, WIDE)
    return pl.pallas_call(
        cross_backward,
        grid_spec=pltpu.PrefetchScalarGridSpec(
            num_scalar_prefetch=1,
            grid=(heads,),
            in_specs=[
                wide_block,
                packs_spec,
                square,
                wide_block,
                wide_block,
                wide_block,
                fixed((row_count, 1)),
                fixed((SPAN, 1, row_count)),
            ],
            out_specs=[packs_spec, wide_block, square, wide_block],
            scratch_shapes=[
                pltpu.VMEM((SPAN + 1, row_count, dim), WIDE),
                pltpu.VMEM((SPAN, row_count, dim), WIDE),
            ],
        ),
        out_shape=[shape_of(packs.shape[0], inner, LOW), tall_wide, shape_of(heads * row_count, row_count, LOW), tall_wide],
        compiler_params=params(),
        name="cross_backward",
    )(place, q_moved, packs, own_scores, attention, log_total, d_attention, my_docs_col, docs)


def run_block_backward(proj, inverse, carried, qdir, solve, dq_moved, d_inside, d_val_own, d_pack, heads):
    row_count, inner = dq_moved.shape
    dim = inner // heads
    wide_block = column(row_count, dim)
    square = stacked(row_count, row_count)
    tall_low = shape_of(row_count, inner, LOW)
    return pl.pallas_call(
        block_backward,
        grid=(heads,),
        in_specs=[
            column(row_count, dim),
            column(row_count, dim, heads),
            column(row_count, dim, 3 * heads),
            pl.BlockSpec((row_count, 128), lambda head, *unused: (0, 4 * inner // 128)),
            square,
            square,
            square,
            wide_block,
            wide_block,
            square,
            wide_block,
            column(d_pack.shape[0], dim),
        ],
        out_specs=[wide_block, wide_block, wide_block, wide_block, fixed((row_count, 128))],
        out_shape=[tall_low, tall_low, tall_low, tall_low, shape_of(row_count, 128, LOW)],
        compiler_params=params(),
        name="block_backward",
    )(proj, proj, proj, proj, inverse, carried, qdir, solve, dq_moved, d_inside, d_val_own, d_pack)


def per_device(
    tokens, cotangent, starts, gain_attn, w_query, w_key, w_value, w_dir, w_beta, w_out, gain_mlp, w_gate, w_up, w_down
):
    row_count, width = tokens.shape
    shard = w_query.shape[0]
    inner = w_query.shape[1]
    hidden_units = w_gate.shape[1]
    heads = w_beta.shape[1]
    dim = inner // heads
    count = lax.axis_size("seq")
    seq_place = lax.axis_index("seq")
    row_place = seq_place % SPAN
    groups = [list(range(at, at + SPAN)) for at in range(0, count, SPAN)]

    start_cols = -(-row_count // shard)
    marks = jnp.pad(starts.astype(LOW), (0, start_cols * shard - row_count)).reshape(start_cols, shard).T
    extra = jnp.concatenate([w_beta, gain_attn[:, None], gain_mlp[:, None], marks], axis=1)
    extra = jnp.pad(extra, ((0, 0), (0, 128 - extra.shape[1])))
    packed_in = jnp.concatenate([w_query, w_key, w_value, w_dir, extra], axis=1)
    w_in = lax.all_gather(packed_in, "seq", axis=0, tiled=True)
    tail = w_in[:, 4 * inner :]
    packed_rest = jnp.concatenate([w_out.T, w_gate, w_up, w_down.T], axis=1)
    packed_rest, tail = lax.optimization_barrier((packed_rest, tail))
    w_rest = lax.all_gather(packed_rest, "seq", axis=0, tiled=True)

    gain_one = tail[:, heads].astype(WIDE)
    gain_two = tail[:, heads + 1].astype(WIDE)
    start_all = tail[:, heads + 2 : heads + 2 + start_cols].reshape(count, shard, start_cols)
    start_all = start_all.transpose(0, 2, 1).reshape(count, start_cols * shard)[:, :row_count]
    row_marks = lax.dynamic_slice_in_dim(start_all, seq_place // SPAN * SPAN, SPAN, axis=0)
    docs = jnp.cumsum(row_marks.astype(jnp.int32).reshape(-1)).reshape(SPAN, 1, row_count)
    my_docs = lax.dynamic_slice_in_dim(docs, row_place, 1, axis=0).reshape(1, row_count)
    my_docs_col = my_docs.reshape(row_count, 1)
    place = row_place.astype(jnp.int32).reshape(1)

    stream = tokens.astype(WIDE)
    scale_one = lax.rsqrt(jnp.mean(stream * stream, axis=-1, keepdims=True) + EPSILON)
    normed = (stream * scale_one * gain_one).astype(LOW)
    proj = dot(normed, w_in)

    pack, q_moved, own_scores, inverse, carried, qdir, solve, peak, total, acc = run_block_forward(
        proj, my_docs_col, my_docs, heads, inner
    )
    packs = lax.all_gather(pack, "seq", axis=0, tiled=True, axis_index_groups=groups)
    attention, attention_low, log_total = run_cross_forward(
        place, q_moved, packs, peak, total, acc, my_docs_col, docs, heads
    )

    w_out_t = w_rest[:, :inner]
    w_gate_all = w_rest[:, inner : inner + hidden_units]
    w_up_all = w_rest[:, inner + hidden_units : inner + 2 * hidden_units]
    w_down_t = w_rest[:, inner + 2 * hidden_units :]
    branch_part = dot(attention_low, w_out_t, tb=True).astype(LOW)
    branch = lax.psum(branch_part, "head").astype(WIDE)
    middle = stream + branch
    scale_two = lax.rsqrt(jnp.mean(middle * middle, axis=-1, keepdims=True) + EPSILON)
    normed_two = (middle * scale_two * gain_two).astype(LOW)
    gate_in = dot(normed_two, w_gate_all)
    up_in = dot(normed_two, w_up_all)
    d_hidden = dot(cotangent, w_down_t)
    gate_sig = jax.nn.sigmoid(gate_in)
    hidden = (gate_in * gate_sig * up_in).astype(LOW)
    d_gate = (d_hidden * up_in * gate_sig * (1.0 + gate_in * (1.0 - gate_sig))).astype(LOW)
    d_up = (d_hidden * gate_in * gate_sig).astype(LOW)
    back_two = (dot(d_gate, w_gate_all, tb=True) + dot(d_up, w_up_all, tb=True)).astype(LOW)
    d_normed_two = lax.psum(back_two, "head").astype(WIDE)
    mlp_part = dot(hidden, w_down_t, tb=True).astype(LOW)
    mlp_part, d_normed_two = lax.optimization_barrier((mlp_part, d_normed_two))

    grad_mlp = jnp.concatenate(
        [
            dot(normed_two, d_gate, ta=True).astype(LOW),
            dot(normed_two, d_up, ta=True).astype(LOW),
            dot(cotangent, hidden, ta=True).astype(LOW),
        ],
        axis=1,
    )
    reduced_mlp = lax.psum_scatter(grad_mlp, "seq", scatter_dimension=0, tiled=True)

    grad_gain_two = jnp.sum(d_normed_two * middle * scale_two, axis=0)
    d_middle = cotangent.astype(WIDE) + norm_back(d_normed_two, middle, scale_two, gain_two)
    d_branch = d_middle.astype(LOW)
    d_attention = dot(d_branch, w_out_t).astype(LOW)
    grad_out_t = dot(d_branch, attention_low, ta=True).astype(LOW)

    d_packs, dq_moved, d_inside, d_val_own = run_cross_backward(
        place, q_moved, packs, own_scores, attention, log_total, d_attention, my_docs_col, docs, heads
    )
    d_pack = lax.psum_scatter(d_packs, "seq", scatter_dimension=0, tiled=True, axis_index_groups=groups)

    d_query, d_key, d_value, d_dir, d_beta = run_block_backward(
        proj, inverse, carried, qdir, solve, dq_moved, d_inside, d_val_own, d_pack, heads
    )
    d_proj = jnp.concatenate([d_query, d_key, d_value, d_dir, d_beta], axis=1)
    back_one = dot(d_proj, w_in, tb=True)
    d_normed = lax.psum(back_one.astype(LOW), "head").astype(WIDE)
    d_tokens = d_middle + norm_back(d_normed, stream, scale_one, gain_one)
    gain_sum = jnp.sum(d_normed * stream * scale_one, axis=0)
    gains = jnp.stack([gain_sum, grad_gain_two], axis=1).astype(LOW)

    grad_in = jnp.concatenate([dot(normed, d_proj, ta=True).astype(LOW), grad_out_t], axis=1)
    reduced_in = lax.psum_scatter(grad_in, "seq", scatter_dimension=0, tiled=True).astype(WIDE)
    gains = lax.psum_scatter(gains, "seq", scatter_dimension=0, tiled=True).astype(WIDE)

    mlp_out = lax.psum(mlp_part, "head").astype(WIDE)
    result = (middle + mlp_out).astype(LOW)
    reduced_mlp = reduced_mlp.astype(WIDE)
    end = 4 * inner + 128
    return (
        result,
        d_tokens,
        gains[:, 0],
        reduced_in[:, :inner],
        reduced_in[:, inner : 2 * inner],
        reduced_in[:, 2 * inner : 3 * inner],
        reduced_in[:, 3 * inner : 4 * inner],
        reduced_in[:, 4 * inner : 4 * inner + heads],
        reduced_in[:, end:].T,
        gains[:, 1],
        reduced_mlp[:, :hidden_units],
        reduced_mlp[:, hidden_units : 2 * hidden_units],
        reduced_mlp[:, 2 * hidden_units :].T,
    )


def solution(mesh):
    placed = (
        P("seq", None),
        P("seq", None),
        P("seq"),
        P("seq"),
        P("seq", "head"),
        P("seq", "head"),
        P("seq", "head"),
        P("seq", "head"),
        P("seq", "head"),
        P("head", "seq"),
        P("seq"),
        P("seq", "head"),
        P("seq", "head"),
        P("head", "seq"),
    )
    return jax.shard_map(
        per_device,
        mesh=mesh,
        in_specs=placed,
        out_specs=(
            P("seq", None),
            P("seq", None),
            P("seq"),
            P("seq", "head"),
            P("seq", "head"),
            P("seq", "head"),
            P("seq", "head"),
            P("seq", "head"),
            P("head", "seq"),
            P("seq"),
            P("seq", "head"),
            P("seq", "head"),
            P("head", "seq"),
        ),
        check_vma=False,
    )
```

time: 1570 us -> 823 us (0.52)
  matrix products: 487 us -> 61.1 us
  other arithmetic: 208 us -> 36.6 us
  starting transfers between devices: 70.4 us -> 1.41 us
  Pallas kernels: 0 us -> 54.3 us
  blocking collectives: 47.1 us -> 0 us
  local copies, waits for them, and re-layouts: 90 us -> 48.3 us
  waiting for transfers between devices: 629 us -> 597 us
    dot_general x126 -> x15, matrix products: 440 us -> 61.1 us  [dot(): return lax.dot_general(left, right, dims, preferred_element_type=WIDE)]
    another operation x6 -> x5, other arithmetic: 120 us -> 0.41 us  [the longest x2 119 us: householder_block(): lax.linalg.triangular_solve(lower_mat, dir_key, left_side=True, lower=True)]
    reduce_scatter x8 -> x2, waiting for transfers between devices: 269 us -> 152 us  [the longest x1 87.7 us: per_device(): lax.psum_scatter(d_packs, 'seq', scatter_dimension=0, tiled=True, axis_in...]
    unnamed x21 -> x12, waiting for transfers between devices: 5.4 us -> 85.8 us
    ppermute x28 -> x0, starting transfers between devices: 68.3 us -> none  [shifted(): lax.ppermute(value, axis, [(source, source + steps) for source in range(i...]
    all_gather x8 -> x3, waiting for transfers between devices: 91.1 us -> 146 us  [the longest x1 59.1 us: per_device(): w_rest = lax.all_gather(packed_rest, 'seq', axis=0, tiled=True)]
    pallas_call x0 -> x4, Pallas kernels: none -> 54.3 us  [the longest x1 26.1 us: run_block_forward(): pl.pallas_call(block_forward, grid=(heads,), in_specs=[column(row_count,...]
    psum x3, waiting for transfers between devices: 264 us -> 214 us  [the longest x1 87.3 us: per_device(): d_normed = lax.psum(back_one.astype(LOW), 'head').astype(WIDE)]
  transfers between devices with their start and end apart: 48 -> 10, of which waited for: 15 -> 10; matrix products, arithmetic and copies ran while one was open for 33% -> 10% of each run, Pallas kernels for 0% -> 1%
where the time goes in v1:
time: 823 us; the launch traced here: 814 us
  waiting for transfers between devices  597 us (73%)
  matrix products  61.1 us (7%)
  Pallas kernels  54.3 us (7%)
  local copies, waits for them, and re-layouts  48.3 us (6%)
  other arithmetic  36.6 us (4%)
  between operations  15 us (2%)
    reduce_scatter x1, waiting for transfers between devices, per_device(): lax.psum_scatter(d_packs, 'seq', scatter_dimension=0, tiled=True, axis_in...  87.7 us
    psum x1, waiting for transfers between devices, per_device(): d_normed = lax.psum(back_one.astype(LOW), 'head').astype(WIDE)  87.3 us
    unnamed x12, waiting for transfers between devices  85.8 us
    reduce_scatter x1, waiting for transfers between devices, per_device(): lax.psum_scatter(grad_in, 'seq', scatter_dimension=0, tiled=True)  63.9 us
    psum x1, waiting for transfers between devices, per_device(): branch = lax.psum(branch_part, 'head').astype(WIDE)  63.6 us
    psum x1, waiting for transfers between devices, per_device(): d_normed_two = lax.psum(back_two, 'head').astype(WIDE)  62.7 us
    dot_general x15, matrix products, dot(): return lax.dot_general(left, right, dims, preferred_element_type=WIDE)  61.1 us
    all_gather x1, waiting for transfers between devices, per_device(): w_rest = lax.all_gather(packed_rest, 'seq', axis=0, tiled=True)  59.1 us
  transfers between devices with their start and end apart: 10, of which 10 were waited for; matrix products, arithmetic and copies ran while one was open for 10% of the time, Pallas kernels for 1%

profile of v1, /device:TPU:0, one launch (start us, length us, event | category | flops | bytes accessed | tf_op | source)
XLA Modules:
  0.0 814.0 jit_solution(13339476595537328694)
XLA Ops:
  19.1 39.2 %all-gather.4.cloned.1.call-done = bf16[1536,1664]{1,0:T(8,128)(2,1)} async-done(((bf16[192,1664]{1,0:T(8,128)(2,1)}), bf16[1536,1664]{1,0:T(8,128)(2,1)}) %all-gather.4.cloned.1.call-update) | async-done | bytes 5111824 | tf_op jit(solution)/shard_map/all_gather | solution.py:457
  61.3 7.3 fusion.34.q_ref.k_ref.v_ref.d_ref.beta_ref
  68.6 26.1 %block_forward.1 = (bf16[1152,384]{1,0:T(8,128)(2,1)}, f32[512,384]{1,0:T(8,128)S(1)}, f32[1536,512]{1,0:T(8,128)}, bf16[1536,512]{1,0:T(8,128)(2,1)}, bf16[1536...) custom-call(f32[512,1664]{1,0:T(8,128)} %fusion.34.q_ref.k_ref.v_ref, ...), custom_call_target="tpu_custom_call" | custom-call | tf_op jit(solution)/shard_map/block_forward/pallas_call | solution.py:316
  96.5 48.0 %all-gather.6.cloned.1.call-done.pack_ref = bf16[9216,384]{1,0:T(8,128)(2,1)} async-done(((bf16[1152,384]{1,0:T(8,128)(2,1)}), bf16[9216,384]{1,0:T(8,128)(2,1)}) %all-gather.6.cloned.1.call-update) | async-done | bytes 7077904 | tf_op jit(solution)/shard_map/all_gather | solution.py:481
  151.1 59.1 %all-gather.8.cloned.1.call-done = bf16[1536,3456]{1,0:T(8,128)(2,1)} async-done(((bf16[192,3456]{1,0:T(8,128)(2,1)}), bf16[1536,3456]{1,0:T(8,128)(2,1)}) %all-gather.8.cloned.1.call-update) | async-done | bytes 10616848 | tf_op jit(solution)/shard_map/all_gather | solution.py:461
  213.8 5.6 fusion.14
  219.4 63.6 %all-reduce.7.cloned.1.call-done = bf16[512,1536]{1,0:T(8,128)(2,1)} async-done(((bf16[512,1536]{1,0:T(8,128)(2,1)}), bf16[512,1536]{1,0:T(8,128)(2,1)}) %all-reduce.7.cloned.1.call-update) | async-done | bytes 1572880 | tf_op jit(solution)/shard_map/psum | solution.py:491
  285.8 4.3 fusion.18
  290.2 5.6 fusion.28
  301.2 5.2 convolution_convert_fusion.4
  306.4 62.7 %all-reduce.9.cloned.1.call-done = bf16[512,1536]{1,0:T(8,128)(2,1)} async-done(((bf16[512,1536]{1,0:T(8,128)(2,1)}), bf16[512,1536]{1,0:T(8,128)(2,1)}) %all-reduce.9.cloned.1.call-update) | async-done | bytes 1572880 | tf_op jit(solution)/shard_map/psum | solution.py:503
  377.1 9.0 %cross_backward.1 = (bf16[9216,384]{1,0:T(8,128)(2,1)}, f32[512,384]{1,0:T(8,128)S(1)}, bf16[1536,512]{1,0:T(8,128)(2,1)S(1)}, f32[512,384]{1,0:T(8,128)S(1)}) custom-call(s32[1]{0:T(128)} %bitcast.place_ref, f32[512,384]{1,0:T(8,128)S(1)} %get-tuple-element.40.qm_ref, bf16[9216,384]{1,0:T(8,128)(2,1)} %all-gather.6.cloned.1.call-done.pack_ref, ...), custom_call_target="tpu_custom_call" | custom-call | tf_op jit(solution)/shard_map/cross_backward/pallas_call | solution.py:381
  387.4 87.7 %reduce-scatter.9.cloned.1.call-done.dpack_ref = bf16[1152,384]{1,0:T(8,128)(2,1)} async-done(((bf16[9216,384]{1,0:T(8,128)(2,1)}), bf16[1152,384]{1,0:T(8,128)(2,1)}) %reduce-scatter.9.cloned.1.call-update) | async-done | bytes 884752 | tf_op jit(solution)/shard_map/reduce_scatter | solution.py:526
  476.2 15.0 %block_backward.1 = (bf16[512,384]{1,0:T(8,128)(2,1)S(1)}, bf16[512,384]{1,0:T(8,128)(2,1)S(1)}, bf16[512,384]{1,0:T(8,128)(2,1)S(1)}, bf16[512,384]{1,0:T(8,128)(2,1)S(1)}, bf16[512,128]{1,0:T(8,128)(2,1)S(1)}) custom-call(f32[512,1664]{1,0:T(8,128)} %fusion.34.q_ref.k_ref.v_ref.d_ref.beta_ref, f32[512,1664]{1,0:T(8,128)} %fusion.34.q_ref.k_ref.v_ref.d_ref.beta_ref, ...), custom_call_target="tpu_custom_call" | custom-call | tf_op jit(solution)/shard_map/block_backward/pallas_call | solution.py:414
  492.8 6.6 convolution_convert_fusion.6
  507.6 4.3 pad_maximum_fusion
  511.9 12.7 %copy.60 = bf16[1536,3072]{1,0:T(8,128)(2,1)} copy(bf16[1536,3072]{0,1:T(8,128)(2,1)} %pad_maximum_fusion) | data formatting | bytes 18874368
  528.7 5.0 convolution_convert_fusion
  533.6 87.3 %all-reduce.11.cloned.1.call-done = (bf16[512,1536]{1,0:T(8,128)(2,1)}, bf16[512,1536]{1,0:T(8,128)(2,1)}) async-done(((bf16[512,1536]{1,0:T(8,128)(2,1)}, bf16[512,1536]{1,0:T(8,128)(2,1)}), (bf16[512,1536]{1,0:T(8,128)(2,1)}, bf16[512,1536]{1,0:T(8,128)(2,1)})) %all-reduce.11.cloned.1.call-update) | async-done | bytes 3145744 | tf_op jit(solution)/shard_map/psum | solution.py:533
  624.8 6.4 pad_maximum_fusion.1
  631.2 69.1 %reduce-scatter.15.cloned.1.call-done = bf16[192,3072]{1,0:T(8,128)(2,1)} async-done(((bf16[1536,3072]{1,0:T(8,128)(2,1)}), bf16[192,3072]{1,0:T(8,128)(2,1)}) %reduce-scatter.15.cloned.1.call-update) | async-done | bytes 1179664
  715.1 6.6 fusion.8
  721.7 15.9 %reduce-scatter.13.cloned.1.call-done = bf16[192,2]{1,0:T(8,128)(2,1)} async-done(((bf16[1536,2]{1,0:T(8,128)(2,1)}), bf16[192,2]{1,0:T(8,128)(2,1)}) %reduce-scatter.13.cloned.1.call-update) | async-done | bytes 784
  739.0 63.9 %reduce-scatter.11.cloned.1.call-done = bf16[192,2048]{1,0:T(8,128)(2,1)} async-done(((bf16[1536,2048]{1,0:T(8,128)(2,1)}), bf16[192,2048]{1,0:T(8,128)(2,1)}) %reduce-scatter.11.cloned.1.call-update) | async-done | bytes 786448 | tf_op jit(solution)/shard_map/reduce_scatter | solution.py:539
  (166 shorter events, 82.9 us)
Async XLA Ops:
  7.2 9.6 %copy-start.24 = (bf16[1024,192]{0,1:T(8,128)(2,1)S(1)}, bf16[1024,192]{0,1:T(8,128)(2,1)}, u32[]{:S(2)}) copy-start(bf16[1024,192]{0,1:T(8,128)(2,1)} %param.27) | copy-start | bytes 1179652
  7.2 9.6 %copy-start.25 = (bf16[192,1024]{1,0:T(8,128)(2,1)S(1)}, bf16[192,1024]{1,0:T(8,128)(2,1)}, u32[]{:S(2)}) copy-start(bf16[192,1024]{1,0:T(8,128)(2,1)} %param.26) | copy-start | bytes 1179652
  7.2 9.6 %copy-start.26 = (bf16[384,192]{0,1:T(8,128)(2,1)S(1)}, bf16[384,192]{0,1:T(8,128)(2,1)}, u32[]{:S(2)}) copy-start(bf16[384,192]{0,1:T(8,128)(2,1)} %param.23) | copy-start | bytes 442372
  7.2 51.1 %all-gather.4.cloned.1.call-start = ((), (), s32[]{:S(2)}) async-start(), calls=%async_computation.4 | async-start | bytes 5750784 | tf_op jit(solution)/shard_map/all_gather | solution.py:457
  14.9 129.6 %all-gather.6.cloned.1.call-start = ((), (), s32[]{:S(2)}) async-start(), calls=%async_computation.5 | async-start | bytes 7962624 | tf_op jit(solution)/shard_map/all_gather | solution.py:481
  16.8 44.6 %copy-start.11 = (bf16[512,1536]{1,0:T(8,128)(2,1)S(1)}, bf16[512,1536]{1,0:T(8,128)(2,1)}, u32[]{:S(2)}) copy-start(bf16[512,1536]{1,0:T(8,128)(2,1)} %param.14) | copy-start | bytes 4718596
  95.5 114.7 %all-gather.8.cloned.1.call-start = ((), (), s32[]{:S(2)}) async-start(), calls=%async_computation.6 | async-start | bytes 11943936 | tf_op jit(solution)/shard_map/all_gather | solution.py:461
  96.2 186.8 %all-reduce.7.cloned.1.call-start = ((), (), s32[]{:S(2)}) async-start(), calls=%async_computation.7 | async-start | bytes 3145728 | tf_op jit(solution)/shard_map/psum | solution.py:491
  213.8 69.3 %copy-start.12 = (bf16[512,1536]{1,0:T(8,128)(2,1)S(1)}, bf16[512,1536]{1,0:T(8,128)(2,1)}, u32[]{:S(2)}) copy-start(bf16[512,1536]{1,0:T(8,128)(2,1)} %param.14) | copy-start | bytes 4718596
  213.8 155.2 %all-reduce.9.cloned.1.call-start = ((), (), s32[]{:S(2)}) async-start(), calls=%async_computation.8 | async-start | bytes 3145728 | tf_op jit(solution)/shard_map/psum | solution.py:503
  285.8 4.3 copy-start.19
  285.8 4.3 copy-start.29
  285.8 10.0 %slice-start = ((s8[10616832]{0:T(1024)(128)(4,1)}), s8[4194304]{0:T(1024)(128)(4,1)S(1)}, s32[]{:S(2)}) async-start(s8[10616832]{0:T(1024)(128)(4,1)} %bitcast.57), calls=%async_computation.14 | async-start | bytes 8388608
  290.2 5.7 slice-start.1
  290.2 5.7 slice-start.2
  300.7 174.3 %reduce-scatter.9.cloned.1.call-start = ((), (), s32[]{:S(2)}) async-start(), calls=%async_computation.9 | async-start | bytes 7962624 | tf_op jit(solution)/shard_map/reduce_scatter | solution.py:526
  387.3 87.8 %copy-start = (bf16[1536,512]{1,0:T(8,128)(2,1)S(1)}, bf16[1536,512]{1,0:T(8,128)(2,1)}, u32[]{:S(2)}) copy-start(bf16[1536,512]{1,0:T(8,128)(2,1)} %get-tuple-element.49.inv_ref) | copy-start | bytes 4718596
  387.3 87.8 %copy-start.10 = (bf16[512,384]{1,0:T(8,128)(2,1)S(1)}, bf16[512,384]{1,0:T(8,128)(2,1)}, u32[]{:S(2)}) copy-start(bf16[512,384]{1,0:T(8,128)(2,1)} %copy-done.9) | copy-start | bytes 1179652
  387.3 233.6 %all-reduce.11.cloned.1.call-start = ((), (), s32[]{:S(2)}) async-start(), calls=%async_computation.13 | async-start | bytes 6291456 | tf_op jit(solution)/shard_map/psum | solution.py:533
  499.4 4.5 copy-start.20
  499.4 201.0 %reduce-scatter.15.cloned.1.call-start = ((), (), s32[]{:S(2)}) async-start(), calls=%async_computation.12 | async-start | bytes 10616832
  524.6 212.9 %reduce-scatter.13.cloned.1.call-start = ((), (), s32[]{:S(2)}) async-start(), calls=%async_computation.11 | async-start | bytes 442368
  624.6 178.4 %reduce-scatter.11.cloned.1.call-start = ((), (), s32[]{:S(2)}) async-start(), calls=%async_computation.10 | async-start | bytes 7077888 | tf_op jit(solution)/shard_map/reduce_scatter | solution.py:539
  707.8 7.3 copy-start.17
  (23 other events, 45.1 us)
Sparse Core Ops, SparseCore 0:
  15.0 43.2 all-gather.3
  95.6 48.8 all-gather.5
  146.4 63.8 all-gather.7
  213.9 69.1 all-reduce.6
  300.8 68.1 all-reduce.8
  387.4 87.5 reduce-scatter.8
  499.5 121.4 all-reduce.10
  624.8 75.4 reduce-scatter.14
  703.7 33.8 reduce-scatter.12
  741.2 61.7 reduce-scatter.10

commit v2 on v1

v2 whole, which is shorter than its diff:
```python
import functools

import jax
import jax.numpy as jnp
from jax import lax
from jax.experimental import pallas as pl
from jax.experimental.pallas import tpu as pltpu
from jax.sharding import PartitionSpec as P

SPAN = 8
EPSILON = 1e-06
NEGATIVE = -1e30
LOW = jnp.bfloat16
WIDE = jnp.float32
VMEM_BYTES = 60 * 2**20


def mm(left, right, ta=False, tb=False):
    dims = (((0 if ta else 1,), (1 if tb else 0,)), ((), ()))
    return lax.dot_general(
        left.astype(LOW), right.astype(LOW), dims, preferred_element_type=WIDE
    )


def halves(value):
    high = value.astype(LOW)
    return high, (value - high.astype(WIDE)).astype(LOW)


def mm3(left, right, ta=False, tb=False):
    left_hi, left_lo = left if isinstance(left, tuple) else halves(left)
    right_hi, right_lo = right if isinstance(right, tuple) else halves(right)
    return mm(left_hi, right_hi, ta, tb) + (mm(left_hi, right_lo, ta, tb) + mm(left_lo, right_hi, ta, tb))


def iota(shape, axis):
    return lax.broadcasted_iota(jnp.int32, shape, axis)


def lower_inverse(strict, beta):
    length = strict.shape[0]
    size = 128
    row, col = iota((size, size), 0), iota((size, size), 1)
    subs, blocks = [], []
    for at in range(0, length, size):
        sub = strict[at : at + size, at : at + size]
        scale = beta[at : at + size]
        diag = jnp.where(row == col, scale, 0.0)
        across = jnp.sum(diag, axis=0, keepdims=True)
        pair = ((row >> 1) == (col >> 1)) & (row > col)
        subs.append(sub)
        blocks.append(diag - jnp.where(pair, sub * scale * across, 0.0))
    bit = 1
    while (1 << bit) < size:
        mask = ((row >> (bit + 1)) == (col >> (bit + 1))) & ((row >> bit) != (col >> bit)) & (row > col)
        right = [mm3(jnp.where(mask, sub, 0.0), block) for sub, block in zip(subs, blocks)]
        blocks = [block - mm3(block, part) for block, part in zip(blocks, right)]
        bit += 1
    while len(blocks) > 1:
        size = blocks[0].shape[0]
        joined = []
        for pair_at in range(len(blocks) // 2):
            first, second = blocks[2 * pair_at], blocks[2 * pair_at + 1]
            at = 2 * pair_at * size
            corner = -mm3(second, mm3(strict[at + size : at + 2 * size, at : at + size], first))
            joined.append(
                jnp.concatenate(
                    [
                        jnp.concatenate([first, jnp.zeros_like(first)], axis=1),
                        jnp.concatenate([corner, second], axis=1),
                    ],
                    axis=0,
                )
            )
        blocks = joined
    return blocks[0]


def xor_move(value, axis, mask):
    return lax.ppermute(value, axis, [(at, at ^ mask) for at in range(lax.axis_size(axis))])


def after(value, *others):
    return lax.optimization_barrier((value, *others))[0]


def doubled_again(held, mask):
    return jnp.concatenate([held, xor_move(held, "seq", mask)], axis=0)


def doubled(block, masks):
    held = block[None]
    for mask in masks:
        held = doubled_again(held, mask)
    return held


def block_forward(
    head, place_ref, normed_ref, w_ref, beta_ref, doc_col_ref, doc_row_ref,
    proj_ref, pack_ref, qm_ref, score_ref, inv_ref, carried_ref, qdir_ref, solve_ref, stat_ref, acc_ref,
):
    proj_ref[...] = mm(normed_ref[...], w_ref[...])
    length, dim = qm_ref.shape
    query, key = proj_ref[:, 0:dim], proj_ref[:, dim : 2 * dim]
    value, dirs = proj_ref[:, 2 * dim : 3 * dim].astype(LOW), proj_ref[:, 3 * dim :]
    beta = 2.0 * jax.nn.sigmoid(beta_ref[:, head : head + 1])
    unit = dirs * lax.rsqrt(jnp.sum(dirs * dirs, axis=-1, keepdims=True) + EPSILON)
    row, col = iota((length, length), 0), iota((length, length), 1)
    unit_two = halves(unit)
    strict = jnp.where(row > col, mm3(unit_two, unit_two, tb=True), 0.0)
    inverse = lower_inverse(strict, beta)
    inverse_two = halves(inverse)
    solve = mm3(inverse_two, unit_two)
    solve_two = halves(solve)
    dir_key = jnp.where(row > col, mm3(unit_two, key, tb=True), 0.0)
    carried = mm3(inverse_two, dir_key)
    carried_two = halves(carried)
    qdir = jnp.where(row >= col, mm3(query, unit_two, tb=True), 0.0)
    qdir_two = halves(qdir)
    qm_ref[...] = query - mm3(qdir_two, solve_two)
    pack_ref[0:length, :] = (key - mm3(carried_two, unit_two, ta=True)).astype(LOW)
    pack_ref[length : 2 * length, :] = value
    eye = jnp.where(iota((dim, dim), 0) == iota((dim, dim), 1), 1.0, 0.0)
    pack_ref[2 * length :, :] = (eye - mm3(unit_two, solve_two, ta=True)).astype(LOW)
    inside = mm(query, key, tb=True) - mm(qdir_two[0], carried_two[0])
    inv_ref[...] = inverse.astype(LOW)
    carried_ref[...] = carried_two[0]
    qdir_ref[...] = qdir_two[0]
    solve_ref[...] = solve_two[0]
    allowed = (doc_col_ref[:, 0:1] == doc_row_ref[pl.ds(place_ref[0], 1), :]) & (row >= col)
    score = jnp.where(allowed, inside * dim**-0.5, NEGATIVE)
    score_ref[...] = score
    peak = jnp.max(score, axis=1, keepdims=True)
    weight = jnp.exp(score - peak)
    lane = iota((length, 128), 1)
    stat_ref[...] = jnp.where(lane == 0, peak, jnp.sum(weight, axis=1, keepdims=True))
    acc_ref[...] = mm(weight, value)


def slot_of(mask, swapped):
    core, first, second = mask & 1, (mask >> 1) & 1, mask >> 2
    return 4 * core + (2 * first + second if swapped else first + 2 * second)


def cross_forward(
    swapped, place_ref, qm_ref, stat_in_ref, acc_ref, doc_col_ref, doc_row_ref, pack_ref,
    att_ref, att_x_ref, log_ref, moved_ref, stat_ref,
):
    length, dim = qm_ref.shape
    place = place_ref[0]
    doc_col = doc_col_ref[:, 0:1]
    moved_ref[...] = qm_ref[...]
    att_ref[...] = acc_ref[...]
    stat_ref[0] = stat_in_ref[:, 0:1]
    stat_ref[1] = stat_in_ref[:, 1:2]

    def hop(step, carry):
        at = place - step
        slot = slot_of(place ^ at, swapped)
        key = pack_ref[slot, 0:length, :]
        value = pack_ref[slot, length : 2 * length, :]
        through = pack_ref[slot, 2 * length :, :]
        allowed = doc_col == doc_row_ref[pl.ds(at, 1), :]
        moved = moved_ref[...]
        peak = stat_ref[0]
        score = jnp.where(allowed, mm(moved, key, tb=True) * dim**-0.5, NEGATIVE)
        new_peak = jnp.maximum(peak, jnp.max(score, axis=1, keepdims=True))
        rescale = jnp.exp(peak - new_peak)
        weight = jnp.exp(score - new_peak)
        stat_ref[0] = new_peak
        stat_ref[1] = stat_ref[1] * rescale + jnp.sum(weight, axis=1, keepdims=True)
        att_ref[...] = att_ref[...] * rescale + mm(weight, value)
        moved_ref[...] = mm(moved, through)
        return carry

    lax.fori_loop(1, place + 1, hop, 0)
    total = stat_ref[1]
    attention = att_ref[...] / total
    att_ref[...] = attention
    scatter_rows(att_x_ref, slice(None), attention.astype(LOW), place_ref[1])
    log_ref[...] = jnp.broadcast_to(stat_ref[0] + jnp.log(total), (length, dim))


def scatter_rows(ref, columns, value, mask, chunk=128):
    for at in range(value.shape[0] // chunk):
        start = pl.multiple_of((mask ^ at) * chunk, chunk)
        ref[pl.ds(start, chunk), columns] = value[at * chunk : (at + 1) * chunk]


def cross_backward(swapped, place_ref, qm_ref, score_ref, att_ref, log_ref, doc_col_ref, doc_row_ref, pack_ref, *rest):
    *datts, even_ref, odd_ref, dqm_ref, dinside_ref, dval_ref, chain_ref, dchain_ref, datt_ref = rest
    length, dim = qm_ref.shape
    place = place_ref[0]
    chunk = datts[0].shape[0]
    for at, part in enumerate(datts):
        start = pl.multiple_of((place_ref[1] ^ at) * chunk, chunk)
        datt_ref[pl.ds(start, chunk), :] = part[...]
    doc_col = doc_col_ref[:, 0:1]
    scale = dim**-0.5
    datt = datt_ref[...]
    log_total = log_ref[:, 0:1]
    delta = jnp.sum(datt.astype(WIDE) * att_ref[...], axis=1, keepdims=True)
    value = pack_ref[0, length : 2 * length, :]
    probs = jnp.exp(score_ref[...] - log_total)
    dprob = mm(datt, value, tb=True)
    dinside_ref[...] = (probs * (dprob - delta) * scale).astype(LOW)
    dval_ref[...] = mm(probs, datt, ta=True)
    chain_ref[1] = qm_ref[...]

    def put(slot, rows, part):
        @pl.when(slot < 4)
        def to_even():
            even_ref[slot, rows, :] = part.astype(LOW)

        @pl.when(slot >= 4)
        def to_odd():
            odd_ref[slot - 4, rows, :] = part.astype(LOW)

    def blank(at, carry):
        put(slot_of(place ^ at, swapped), slice(None), jnp.zeros(even_ref.shape[1:], LOW))
        return carry

    lax.fori_loop(place, SPAN, blank, 0)

    def hop(step, carry):
        at = place - step
        slot = slot_of(place ^ at, swapped)
        moved = chain_ref[step]
        key = pack_ref[slot, 0:length, :]
        value = pack_ref[slot, length : 2 * length, :]
        through = pack_ref[slot, 2 * length :, :]
        chain_ref[step + 1] = mm(moved, through)
        allowed = doc_col == doc_row_ref[pl.ds(at, 1), :]
        score = jnp.where(allowed, mm(moved, key, tb=True) * scale, NEGATIVE)
        probs = jnp.exp(score - log_total)
        dprob = mm(datt, value, tb=True)
        dscore = probs * (dprob - delta) * scale
        dchain_ref[step] = mm(dscore, key)
        put(slot, slice(0, length), mm(dscore, moved, ta=True))
        put(slot, slice(length, 2 * length), mm(probs, datt, ta=True))
        return carry

    lax.fori_loop(1, place + 1, hop, 0)

    def back(count, carry):
        step = place - count
        slot = slot_of(place ^ (place - step), swapped)
        through = pack_ref[slot, 2 * length :, :]
        grad = dqm_ref[...]
        put(slot, slice(2 * length, 2 * length + dim), mm(chain_ref[step], grad, ta=True))
        dqm_ref[...] = dchain_ref[step] + mm(grad, through, tb=True)
        return carry

    dqm_ref[...] = jnp.zeros((length, dim), WIDE)
    lax.fori_loop(0, place, back, 0)


def block_backward(
    head, place_ref, proj_ref, beta_ref, inv_ref, carried_ref, qdir_ref, solve_ref, dqm_ref, dinside_ref, dval_ref, *rest
):
    *dpacks, dproj_ref, dbeta_ref = rest
    length, dim = dqm_ref.shape
    query, key, dirs = proj_ref[:, 0:dim], proj_ref[:, dim : 2 * dim], proj_ref[:, 3 * dim :]
    beta = 2.0 * jax.nn.sigmoid(beta_ref[:, head : head + 1])
    norm = lax.rsqrt(jnp.sum(dirs * dirs, axis=-1, keepdims=True) + EPSILON)
    unit = dirs * norm
    low_unit, low_key, low_query = unit.astype(LOW), key.astype(LOW), query.astype(LOW)
    row, col = iota((length, length), 0), iota((length, length), 1)
    inverse, carried, qdir, solve = inv_ref[...], carried_ref[...], qdir_ref[...], solve_ref[...]
    dqm, dinside = dqm_ref[...].astype(LOW), dinside_ref[...]

    def summed(rows):
        return sum(part[rows, :].astype(WIDE) for part in dpacks)

    dkm = summed(slice(0, length))
    dthrough = summed(slice(2 * length, 2 * length + dim)).astype(LOW)
    dvalue = dval_ref[...] + summed(slice(length, 2 * length))
    dkm_low = dkm.astype(LOW)
    dqdir = -jnp.where(row >= col, mm(dqm, solve, tb=True) + mm(dinside, carried, tb=True), 0.0).astype(LOW)
    dquery = dqm_ref[...] + mm(dinside, low_key) + mm(dqdir, low_unit)
    dsolve = -(mm(qdir, dqm, ta=True) + mm(low_unit, dthrough))
    dcarried = -(mm(low_unit, dkm_low, tb=True) + mm(qdir, dinside, ta=True))
    ysolve = mm(inverse, dsolve, ta=True)
    ycarried = mm(inverse, dcarried, ta=True)
    ddir_key = jnp.where(row > col, ycarried, 0.0).astype(LOW)
    dlower = -(mm(ysolve, solve, tb=True) + mm(ycarried, carried, tb=True))
    ddiag = jnp.sum(jnp.where(row == col, dlower, 0.0), axis=1, keepdims=True)
    dgram = jnp.where(row > col, dlower, 0.0).astype(LOW)
    dkey = dkm + mm(dinside, low_query, ta=True) + mm(ddir_key, low_unit, ta=True)
    dunit = (
        ysolve
        - mm(solve, dthrough, tb=True)
        - mm(carried, dkm_low)
        + mm(dqdir, low_query, ta=True)
        + mm(ddir_key, low_key)
        + mm(dgram, low_unit)
        + mm(dgram, low_unit, ta=True)
    )
    along = jnp.sum(dunit * dirs, axis=1, keepdims=True)
    ddirs = norm * dunit - dirs * (norm * norm * norm * along)
    dbeta = -ddiag / jnp.maximum(beta, 1e-30) * (1.0 - 0.5 * beta)
    lane = iota((length, 128), 1)
    mask = place_ref[1]
    for at, part in enumerate((dquery, dkey, dvalue, ddirs)):
        scatter_rows(dproj_ref, slice(at * dim, (at + 1) * dim), part.astype(LOW), mask)
    scatter_rows(dbeta_ref, slice(None), jnp.where(lane == head, dbeta, 0.0).astype(LOW), mask)


def prepare(heads, place_ref, tokens_ref, cot_ref, w_ref, mark_ref, *rest):
    normed_ref, normed_t_ref, tokens_x_ref, cot_x_ref, gains_ref, beta_ref, docs_ref, doc_col_ref, marks_ref = rest
    for slot in range(SPAN):
        mask = 2 * (slot & 1) + 4 * ((slot >> 1) & 1) + (slot >> 2)
        marks_ref[place_ref[0] ^ mask] = mark_ref[slot]
    span = SPAN
    small = w_ref[...]
    across = small.astype(WIDE).T
    gains_ref[...] = across[0:8]
    gain = across[heads : heads + 1]
    stream = tokens_ref[...].astype(WIDE)
    scale = lax.rsqrt(jnp.mean(stream * stream, axis=-1, keepdims=True) + EPSILON)
    normed_wide = stream * scale * gain
    normed = normed_wide.astype(LOW)
    normed_ref[...] = normed
    beta_ref[...] = mm(normed, small)
    mask = place_ref[1]
    scatter_rows(tokens_x_ref, slice(None), tokens_ref[...], mask)
    scatter_rows(cot_x_ref, slice(None), cot_ref[...], mask)
    for at in range(normed.shape[0] // 128):
        start = pl.multiple_of((mask ^ at) * 128, 128)
        normed_t_ref[:, pl.ds(start, 128)] = normed_wide[at * 128 : (at + 1) * 128].T.astype(LOW)
    marks = jnp.sum(marks_ref[...].astype(WIDE), axis=1)
    length = marks.shape[1]
    upper = jnp.where(iota((length, length), 0) <= iota((length, length), 1), 1.0, 0.0)
    docs = mm(marks, upper)
    row = iota(docs.shape, 0)
    before = jnp.zeros_like(docs)
    for at in range(span - 1):
        before = before + jnp.where(row > at, docs[at : at + 1, length - 1 : length], 0.0)
    docs = docs + before
    docs_ref[...] = docs
    own = jnp.sum(jnp.where(row == place_ref[0], docs, 0.0), axis=0, keepdims=True)
    eye = iota((length, length), 0) == iota((length, length), 1)
    column = jnp.sum(jnp.where(eye, own, 0.0), axis=1, keepdims=True)
    doc_col_ref[...] = jnp.broadcast_to(column, doc_col_ref.shape)


def branch_forward(heads, dim, tokens_x_ref, gains_ref, w_out_ref, *rest):
    *pieces, middle_ref, normed_ref, att_ref = rest
    for at, part in enumerate(pieces):
        att_ref[:, at * dim : (at + 1) * dim] = part[...]
    middle = tokens_x_ref[...].astype(WIDE) + mm(att_ref[...], w_out_ref[...], tb=True)
    middle_ref[...] = middle
    scale = lax.rsqrt(jnp.mean(middle * middle, axis=-1, keepdims=True) + EPSILON)
    normed_ref[...] = (middle * scale * gains_ref[heads + 1 : heads + 2]).astype(LOW)


def mlp_forward(cot_ref, gate_ref, up_ref, down_ref, *rest):
    ways = (len(rest) - 3) // 2
    pieces, outs = rest[:ways], rest[ways + 1 : -2]
    all_ref, normed_ref, acc_ref = rest[ways], rest[-2], rest[-1]
    step = pl.program_id(0)
    chunk = pieces[0].shape[0]

    @pl.when(step == 0)
    def start():
        for at, part in enumerate(pieces):
            normed_ref[at * chunk : (at + 1) * chunk, :] = part[...]
        acc_ref[...] = jnp.zeros_like(acc_ref)

    normed = normed_ref[...]
    gate, up, d_hidden = mm(normed, gate_ref[...]), mm(normed, up_ref[...]), mm(cot_ref[...], down_ref[...])
    sig = jax.nn.sigmoid(gate)
    silu = gate * sig
    d_gate = (d_hidden * up * sig * (1.0 + gate * (1.0 - sig))).astype(LOW)
    d_up = (d_hidden * silu).astype(LOW)
    all_ref[0] = d_gate
    all_ref[1] = d_up
    all_ref[2] = (silu * up).astype(LOW)
    acc_ref[...] += mm(d_gate, gate_ref[...], tb=True) + mm(d_up, up_ref[...], tb=True)

    @pl.when(step == pl.num_programs(0) - 1)
    def finish():
        for at, part in enumerate(outs):
            part[...] = acc_ref[at * chunk : (at + 1) * chunk, :].astype(LOW)


def mlp_grads(cot_ref, all_ref, down_ref, middle_ref, *rest):
    ways = (len(rest) - 3) // 2
    pieces, grad_ref, outs, left_ref, acc_ref = rest[:ways], rest[ways], rest[ways + 1 : -2], rest[-2], rest[-1]
    step, third = pl.program_id(0), pl.num_programs(0) // 3
    chunk = pieces[0].shape[0]

    @pl.when(step == 0)
    def start():
        for at, part in enumerate(pieces):
            left_ref[:, at * chunk : (at + 1) * chunk] = part[...].astype(WIDE).T.astype(LOW)
        acc_ref[...] = jnp.zeros_like(acc_ref)
        acc_ref[0:chunk, :] = middle_ref[...]

    @pl.when(step == 2 * third)
    def turn():
        for at in range(ways):
            part = cot_ref[at * chunk : (at + 1) * chunk, :]
            left_ref[:, at * chunk : (at + 1) * chunk] = part.astype(WIDE).T.astype(LOW)

    right = all_ref[0]
    grad_ref[...] = mm(left_ref[...], right).astype(LOW)

    @pl.when(step >= 2 * third)
    def down():
        acc_ref[...] += mm(right, down_ref[...], tb=True)

    @pl.when(step == 3 * third - 1)
    def finish():
        for at, part in enumerate(outs):
            part[...] = acc_ref[at * chunk : (at + 1) * chunk, :].astype(LOW)


def branch_backward(heads, inner, middle_ref, gains_ref, cot_ref, w_out_ref, *rest):
    ways = (len(rest) - 3) // 2
    backs, d_middle_ref, d_branch_ref, gain_ref, d_atts = rest[:ways], rest[ways], rest[ways + 1], rest[ways + 2], rest[ways + 3 :]
    grad = total([part[...] for part in backs])
    middle = middle_ref[...]
    scale = lax.rsqrt(jnp.mean(middle * middle, axis=-1, keepdims=True) + EPSILON)
    gain_ref[...] = jnp.broadcast_to(jnp.sum(grad * middle * scale, axis=0, keepdims=True), gain_ref.shape)
    d_middle = cot_ref[...].astype(WIDE) + norm_back(grad, middle, scale, gains_ref[heads + 1 : heads + 2])
    d_middle_ref[...] = d_middle
    d_branch = d_middle.astype(LOW)
    d_branch_ref[...] = d_branch
    for at, part in enumerate(d_atts):
        part[...] = mm(d_branch, w_out_ref[:, at * inner : (at + 1) * inner]).astype(LOW)


def project_back(heads, tokens_x_ref, w_ref, part_ref, d_proj_ref, *rest):
    d_betas, (gain_ref, d_beta_ref, *outs) = rest[:heads], rest[heads:]
    cols = d_proj_ref.shape[1]
    d_beta = total([part[...] for part in d_betas]).astype(LOW)
    d_beta_ref[...] = d_beta
    back = part_ref[...] + mm(d_beta, w_ref[:, heads * cols :], tb=True)
    back = back + mm(d_proj_ref[...], w_ref[:, (heads - 1) * cols : heads * cols], tb=True)
    stream = tokens_x_ref[...].astype(WIDE)
    scale = lax.rsqrt(jnp.mean(stream * stream, axis=-1, keepdims=True) + EPSILON)
    gain_ref[...] = jnp.broadcast_to(jnp.sum(back * stream * scale, axis=0, keepdims=True), gain_ref.shape)
    chunk = outs[0].shape[0]
    for at, part in enumerate(outs):
        part[...] = back[at * chunk : (at + 1) * chunk].astype(LOW)


def token_grad(heads, tokens_x_ref, gains_ref, d_middle_ref, *rest):
    *backs, out_ref = rest
    grad = total([part[...] for part in backs])
    stream = tokens_x_ref[...].astype(WIDE)
    scale = lax.rsqrt(jnp.mean(stream * stream, axis=-1, keepdims=True) + EPSILON)
    out_ref[...] = (d_middle_ref[...] + norm_back(grad, stream, scale, gains_ref[heads : heads + 1])).astype(LOW)


def token_join(place_ref, *rest):
    *pieces, out_ref = rest
    chunk = pieces[0].shape[0]
    for at, part in enumerate(pieces):
        start = pl.multiple_of((place_ref[1] ^ at) * chunk, chunk)
        out_ref[pl.ds(start, chunk), :] = part[...].astype(out_ref.dtype)


def weight_grads(left_ref, d_proj_ref, *rest):
    rest[-1][...] = mm(left_ref[...], d_proj_ref[...]).astype(LOW)


def out_grads(heads, places_ref, branch_ref, *rest):
    atts, out_ref, turned_ref = rest[:heads], rest[-2], rest[-1]
    step = pl.program_id(0)

    @pl.when(step == 0)
    def turn():
        for at in range(branch_ref.shape[0] // 128):
            start = pl.multiple_of((places_ref[1] ^ at) * 128, 128)
            turned_ref[:, pl.ds(start, 128)] = branch_ref[at * 128 : (at + 1) * 128].astype(WIDE).T.astype(LOW)

    for head in range(heads):

        @pl.when(step == head)
        def one(head=head):
            out_ref[...] = mm(turned_ref[...], atts[head][...]).astype(LOW)


def small_grads(heads, left_ref, d_beta_ref, gain_one_ref, gain_two_ref, *rest):
    out_ref, rows_ref = rest[-2:]
    rows_ref[...] = jnp.zeros_like(rows_ref)
    rows_ref[heads : heads + 1, :] = gain_one_ref[0:1, :]
    rows_ref[heads + 1 : heads + 2, :] = gain_two_ref[0:1, :]
    out_ref[...] = (mm(left_ref[...], d_beta_ref[...]) + rows_ref[...].T).astype(LOW)


def project_more(d_proj_ref, w_ref, *rest):
    part = mm(d_proj_ref[...], w_ref[...], tb=True)
    if len(rest) > 1:
        part = rest[0][...] + part
    rest[-1][...] = part


def grad_join(heads, dim, in_ref, *outs):
    width = 4 * dim
    for head in range(heads):
        for kind, out in enumerate(outs[:4]):
            at = head * width + kind * dim
            out[:, head * dim : (head + 1) * dim] = in_ref[:, at : at + dim].astype(WIDE)
    outs[4][...] = in_ref[:, heads * width : heads * width + 128].astype(WIDE)
    outs[5][...] = in_ref[:, heads * width + 128 :].astype(WIDE)


def fixed(shape):
    return pl.BlockSpec(shape, lambda *unused: (0,) * len(shape))


def column_at(shape, at):
    return pl.BlockSpec(shape, lambda *unused: (0, at))


ANYWHERE = pl.BlockSpec(memory_space=pl.ANY)
SCALARS = pl.BlockSpec(memory_space=pltpu.SMEM)


def run(kernel, name, ins, specs, outs, scratch=(), flops=10**9):
    return pl.pallas_call(
        kernel,
        grid=(1,),
        in_specs=specs,
        out_specs=[fixed(shape) for shape, unused in outs],
        out_shape=[jax.ShapeDtypeStruct(shape, dtype) for shape, dtype in outs],
        scratch_shapes=list(scratch),
        compiler_params=pltpu.CompilerParams(vmem_limit_bytes=VMEM_BYTES),
        cost_estimate=pl.CostEstimate(flops=flops, bytes_accessed=4 * 2**20, transcendentals=2**18),
        name=name,
    )(*ins)


def whole(*arrays):
    return [fixed(array.shape) for array in arrays]


def run_block_forward(places, normed, w_in, at, beta_raw, doc_col, doc_row, dim, head):
    length, width = normed.shape
    square, tall = (length, length), (length, dim)
    return run(
        functools.partial(block_forward, head),
        "block_forward",
        (places, normed, w_in, beta_raw, doc_col, doc_row),
        [SCALARS, *whole(normed), column_at((width, 4 * dim), at), *whole(beta_raw, doc_col, doc_row)],
        [
            ((length, 4 * dim), WIDE),
            ((2 * length + dim, dim), LOW),
            (tall, WIDE),
            (square, WIDE),
            (square, LOW),
            (square, LOW),
            (square, LOW),
            (tall, LOW),
            ((length, 128), WIDE),
            (tall, WIDE),
        ],
        flops=10**10,
    )


def run_cross_forward(places, q_moved, stats, acc, doc_col, docs, packs, swapped):
    length, dim = q_moved.shape
    ins = (q_moved, stats, acc, doc_col, docs, packs)
    return run(
        functools.partial(cross_forward, swapped),
        "cross_forward",
        (places, *ins),
        [SCALARS, *whole(*ins)],
        [((length, dim), WIDE), ((length, dim), LOW), ((length, dim), WIDE)],
        [pltpu.VMEM((length, dim), WIDE), pltpu.VMEM((2, length, 1), WIDE)],
        flops=10**10,
    )


def run_cross_backward(places, q_moved, scores, attention, log_total, doc_col, docs, packs, d_atts, head, swapped):
    length, dim = q_moved.shape
    half = ((SPAN // 2,) + packs.shape[1:], LOW)
    ins = (q_moved, scores, attention, log_total, doc_col, docs, packs)
    return run(
        functools.partial(cross_backward, swapped),
        "cross_backward",
        (places, *ins, *d_atts),
        [SCALARS, *whole(*ins)] + [column_at((part.shape[0], dim), head) for part in d_atts],
        [half, half, ((length, dim), WIDE), ((length, length), LOW), ((length, dim), WIDE)],
        [
            pltpu.VMEM((SPAN + 1, length, dim), WIDE),
            pltpu.VMEM((SPAN, length, dim), WIDE),
            pltpu.VMEM((length, dim), LOW),
        ],
        flops=10**10,
    )


def run_block_backward(places, proj, beta_raw, kept, d_packs, head, dim):
    length = proj.shape[0]
    ins = (proj, beta_raw, *kept, *d_packs)
    return run(
        functools.partial(block_backward, head),
        "block_backward",
        (places, *ins),
        [SCALARS, *whole(*ins)],
        [(proj.shape, LOW), ((length, 128), LOW)],
        flops=5 * 10**9,
    )


def norm_back(grad, value, scale, gain):
    weighted = grad * gain
    return scale * weighted - value * scale * scale * scale * jnp.mean(weighted * value, axis=-1, keepdims=True)


def total(parts):
    out = parts[0].astype(WIDE)
    for part in parts[1:]:
        out = out + part.astype(WIDE)
    return out


def per_device(
    tokens, cotangent, starts, gain_attn, w_query, w_key, w_value, w_dir, w_beta, w_out, gain_mlp, w_gate, w_up, w_down
):
    row_count, width = tokens.shape
    shard, inner = w_query.shape
    hidden_units = w_gate.shape[1]
    heads = w_beta.shape[1]
    dim = inner // heads
    count = lax.axis_size("seq")
    ways = lax.axis_size("head")
    chunk = row_count // ways
    seq_place, head_place = lax.axis_index("seq"), lax.axis_index("head")
    places = jnp.stack([seq_place % SPAN, head_place, seq_place]).astype(jnp.int32)

    def to_heads(parts):
        return [xor_move(part, "head", at) if at else part for at, part in enumerate(parts)]

    def over_heads(part):
        return to_heads([part] * ways)

    parts = []
    for head in range(heads):
        cut = slice(head * dim, (head + 1) * dim)
        parts += [w_query[:, cut], w_key[:, cut], w_value[:, cut], w_dir[:, cut]]
    parts += [w_beta, gain_attn[:, None], gain_mlp[:, None], jnp.zeros((shard, 128 - heads - 2), LOW)]
    w_in = lax.all_gather(jnp.concatenate(parts, axis=1), "seq", axis=0, tiled=True)
    marks = doubled(jnp.pad(starts.astype(LOW)[None], ((0, 15), (0, 0))), (2, 4, 1))
    out_parts = jnp.concatenate(over_heads(w_out.T), axis=1)
    w_in, marks, out_parts = lax.optimization_barrier((w_in, marks, out_parts))
    w_out_x = lax.all_gather(out_parts, "seq", axis=0, tiled=True)

    tall, wide_tall, part_low = (row_count, width), (width, row_count), ((chunk, width), LOW)
    small_at = heads * 4 * dim // 128
    normed, normed_x_t, tokens_x, cot_x, gains, beta_raw, docs, doc_col = run(
        functools.partial(prepare, heads),
        "prepare",
        (places, tokens, cotangent, w_in, marks),
        [SCALARS, *whole(tokens, cotangent), column_at((width, 128), small_at), *whole(marks)],
        [
            (tall, LOW),
            (wide_tall, LOW),
            (tall, LOW),
            (tall, LOW),
            ((8, width), WIDE),
            ((row_count, 128), WIDE),
            ((SPAN, row_count), WIDE),
            ((row_count, 128), WIDE),
        ],
        [pltpu.VMEM((SPAN, 16, row_count), LOW)],
    )

    orders = [(4, 2) if head % 2 else (2, 4) for head in range(heads)]
    first, mixed, ready, full = [], [], {}, {}

    def step(kind, head):
        return (head, kind, xor_move(ready[head], "seq", orders[head][kind] if kind < 2 else 1))

    def meet(outs, moves):
        outs, arrived = lax.optimization_barrier((outs, [move[2] for move in moves]))
        for (head, unused, unused_too), part in zip(moves, arrived):
            ready[head] = jnp.concatenate([ready[head], part], axis=0)
        return outs

    flying = []
    for head in range(heads):
        held = normed if head == 0 else after(normed, first[-1][2])
        outs = run_block_forward(places, held, w_in, head, beta_raw, doc_col, docs, dim, head)
        first.append(meet(outs, flying))
        ready[head] = first[head][1][None]
        flying = [step(at, head - at) for at in range(max(0, head - 2), head + 1)]
    rest_in = jnp.concatenate([w_gate, w_up, w_down.T], axis=1)
    stage = {move[0]: move[1] for move in flying}
    for head in range(heads):
        kept = first[head]
        while stage.get(head, 2) < 2 or any(move[0] == head for move in flying):
            now = [move for move in flying if move[0] == head]
            flying = [move for move in flying if move[0] != head]
            meet((), now)
            if stage[head] < 2:
                stage[head] += 1
                flying.append(step(stage[head], head))
        if head == 0:
            held = kept[2]
        else:
            held = after(kept[2], mixed[-1][0])
        outs = run_cross_forward(places, held, kept[8], kept[9], doc_col, docs, ready[head], head % 2 == 1)
        mixed.append(meet(outs, flying))
        flying = []
        for later in range(head + 1, heads):
            if stage[later] < 2:
                stage[later] += 1
                flying.append(step(stage[later], later))
        if head == 0:
            w_rest = lax.all_gather(after(rest_in, mixed[0][0], w_out_x), "seq", axis=0, tiled=True)
    packs = [ready[head] for head in range(heads)]

    att_x = jnp.concatenate([part[1] for part in mixed], axis=1)
    att_parts = to_heads([att_x[at * chunk : (at + 1) * chunk] for at in range(ways)])
    own_rows = fixed((chunk, width))
    middle, normed_two = run(
        functools.partial(branch_forward, heads, inner),
        "branch_forward",
        (tokens_x, gains, w_out_x, *att_parts),
        [own_rows, *whole(gains, w_out_x, *att_parts)],
        [((chunk, width), WIDE), part_low],
        [pltpu.VMEM((chunk, ways * inner), LOW)],
    )
    two_parts = over_heads(normed_two)

    blocks = 4
    cols = hidden_units // blocks
    all_three, *backs = pl.pallas_call(
        mlp_forward,
        grid=(blocks,),
        in_specs=[
            fixed(tall),
            pl.BlockSpec((width, cols), lambda step: (0, step)),
            pl.BlockSpec((width, cols), lambda step: (0, blocks + step)),
            pl.BlockSpec((width, cols), lambda step: (0, 2 * blocks + step)),
            *whole(*two_parts),
        ],
        out_specs=[pl.BlockSpec((3, row_count, cols), lambda step: (0, 0, step))] + [fixed((chunk, width))] * ways,
        out_shape=[jax.ShapeDtypeStruct((3, row_count, hidden_units), LOW)]
        + [jax.ShapeDtypeStruct((chunk, width), LOW)] * ways,
        scratch_shapes=[pltpu.VMEM(tall, LOW), pltpu.VMEM(tall, WIDE)],
        compiler_params=pltpu.CompilerParams(vmem_limit_bytes=VMEM_BYTES),
        cost_estimate=pl.CostEstimate(flops=10**10, bytes_accessed=2**24, transcendentals=2**19),
        name="mlp_forward",
    )(cot_x, w_rest, w_rest, w_rest, *two_parts)
    backs = to_heads(backs)
    grad_mlp, *mlp_parts = pl.pallas_call(
        mlp_grads,
        grid=(3 * blocks,),
        in_specs=[
            fixed(tall),
            pl.BlockSpec((1, row_count, cols), lambda step: (step // blocks, 0, step % blocks)),
            pl.BlockSpec((width, cols), lambda step: (0, jnp.maximum(step, 2 * blocks))),
            fixed((chunk, width)),
            *whole(*two_parts),
        ],
        out_specs=[pl.BlockSpec((width, cols), lambda step: (0, step))] + [fixed((chunk, width))] * ways,
        out_shape=[jax.ShapeDtypeStruct((width, 3 * hidden_units), LOW)]
        + [jax.ShapeDtypeStruct((chunk, width), LOW)] * ways,
        scratch_shapes=[pltpu.VMEM(wide_tall, LOW), pltpu.VMEM(tall, WIDE)],
        compiler_params=pltpu.CompilerParams(vmem_limit_bytes=VMEM_BYTES),
        cost_estimate=pl.CostEstimate(flops=10**10, bytes_accessed=2**24, transcendentals=0),
        name="mlp_grads",
    )(cot_x, all_three, w_rest, middle, *two_parts)
    grad_mlp, mlp_parts, backs = lax.optimization_barrier((grad_mlp, mlp_parts, backs))
    reduced_mlp = lax.psum_scatter(grad_mlp, "seq", scatter_dimension=0, tiled=True)

    d_middle, d_branch, gain_two_sum, *d_atts = run(
        functools.partial(branch_backward, heads, inner),
        "branch_backward",
        (middle, gains, cot_x, w_out_x, *backs),
        [*whole(middle, gains), own_rows, *whole(w_out_x, *backs)],
        [((chunk, width), WIDE), part_low, ((8, width), WIDE)] + [((chunk, inner), LOW)] * ways,
    )
    d_atts = to_heads(d_atts)

    def add(left, right):
        return (left.astype(WIDE) + right.astype(WIDE)).astype(LOW)

    second, sums, mlp_terms = [], {}, [mlp_parts[0]]
    core, across = {}, {}
    for head in range(heads):
        kept = first[head]
        held = kept[2] if head == 0 else after(kept[2], second[-1][0])
        flying = [move for move in (core.get(head - 1), across.get(head - 2)) if move is not None]
        if head + 1 < ways:
            flying.append(xor_move(mlp_parts[head + 1], "head", head + 1))
        outs = run_cross_backward(
            places, held, kept[3], mixed[head][0], mixed[head][2], doc_col, docs, packs[head], d_atts, head, head % 2 == 1
        )
        (even, odd, *rest), flying = lax.optimization_barrier((outs, flying))
        second.append(rest)
        if head + 1 < ways:
            mlp_terms.append(flying.pop())
        if head >= 2:
            half = add(sums[head - 2][:2], flying.pop())
            sums[head - 2] = [half[0], half[1]]
        if head >= 1:
            sums[head - 1] = add(sums[head - 1], flying.pop())
            across[head - 1] = xor_move(sums[head - 1][2:], "seq", orders[head - 1][1])
        sums[head] = even
        core[head] = xor_move(odd, "seq", 1)
    mlp_terms += [xor_move(mlp_parts[at], "head", at) for at in range(heads + 1, ways)]
    result_own = total(mlp_terms).astype(LOW)
    d_branch_all = lax.all_gather(after(d_branch, reduced_mlp), "head", axis=0, tiled=True)

    cols = 4 * dim
    grad_in = None

    def grads_into(kernel, ins, specs, at, grid, name, scratch=()):
        given = () if grad_in is None else (grad_in,)
        return pl.pallas_call(
            kernel,
            grid=(grid,),
            in_specs=specs + [ANYWHERE] * len(given),
            out_specs=at,
            out_shape=jax.ShapeDtypeStruct((width, (heads + 1) * cols), LOW),
            input_output_aliases={len(ins): 0} if given else {},
            scratch_shapes=list(scratch),
            compiler_params=pltpu.CompilerParams(vmem_limit_bytes=VMEM_BYTES),
            cost_estimate=pl.CostEstimate(flops=10**9, bytes_accessed=2**22, transcendentals=0),
            name=name,
        )(*ins, *given)

    d_projs, d_betas, result_parts = [], [], [result_own]
    back_part = None
    for head in range(heads):
        if isinstance(sums[head], list):
            near_sum, far_sum = sums[head]
        else:
            half = add(sums[head][:2], across[head])
            near_sum, far_sum = half[0], half[1]
        sent = [near_sum, xor_move(far_sum, "seq", orders[head][0])]
        if head >= 1:
            grad_in = grads_into(
                weight_grads,
                (normed_x_t, d_projs[-1]),
                whole(normed_x_t, d_projs[-1]),
                column_at((width, cols), head - 1),
                1,
                "weight_grads",
            )
            ins = (d_projs[-1], w_in) + (() if back_part is None else (back_part,))
            (back_part,) = run(
                project_more,
                "project_more",
                ins,
                [*whole(d_projs[-1]), column_at((width, cols), head - 1), *whole(*ins[2:])],
                [(tall, WIDE)],
            )
            grad_in, back_part, sent = lax.optimization_barrier((grad_in, back_part, sent))
        flying = []
        if head + 1 < ways:
            flying.append(xor_move(result_own, "head", head + 1))
        if head + 1 in across:
            flying.append(across[head + 1])
        late = heads - 1 if head == 0 and heads - 1 not in across else None
        if late:
            flying.append(core[late])
        proj, inverse, carried, qdir, solve = (first[head][at] for at in (0, 4, 5, 6, 7))
        outs = run_block_backward(
            places, proj, beta_raw, (inverse, carried, qdir, solve, *second[head]), sent, head, dim
        )
        (d_proj, d_beta), flying = lax.optimization_barrier((outs, flying))
        if late:
            sums[late] = add(sums[late], flying.pop())
            across[late] = xor_move(sums[late][2:], "seq", orders[late][1])
        if head + 1 in across and head + 1 != late:
            across[head + 1] = flying.pop()
        if head + 1 < ways:
            result_parts.append(flying.pop())
        d_projs.append(d_proj)
        d_betas.append(d_beta)
    result_parts += [xor_move(result_own, "head", at) for at in range(heads + 1, ways)]
    atts = [part[1] for part in mixed]
    grad_in = grads_into(
        functools.partial(out_grads, heads),
        (places, d_branch_all, *atts),
        [SCALARS, *whole(d_branch_all, *atts)],
        pl.BlockSpec((width, 128), lambda step: (0, heads * cols // 128 + 1 + step)),
        heads,
        "out_grads",
        [pltpu.VMEM(wide_tall, LOW)],
    )
    back_ins = (tokens_x, w_in, back_part, d_projs[-1], *d_betas)
    gain_one_sum, d_beta, *backs = run(
        functools.partial(project_back, heads),
        "project_back",
        back_ins,
        whole(*back_ins),
        [((8, width), WIDE), ((row_count, 128), LOW)] + [part_low] * ways,
    )
    backs = to_heads(backs)
    (d_tokens_own,) = run(
        functools.partial(token_grad, heads),
        "token_grad",
        (tokens_x, gains, d_middle, *backs),
        [own_rows, *whole(gains, d_middle, *backs)],
        [part_low],
    )
    token_parts = over_heads(d_tokens_own)
    (result,) = run(
        token_join, "result_join", (places, *result_parts), [SCALARS, *whole(*result_parts)], [(tall, LOW)]
    )
    (d_tokens,) = run(
        token_join, "token_join", (places, *token_parts), [SCALARS, *whole(*token_parts)], [(tall, WIDE)]
    )

    grad_in = grads_into(
        weight_grads,
        (normed_x_t, d_projs[-1]),
        whole(normed_x_t, d_projs[-1]),
        column_at((width, cols), heads - 1),
        1,
        "weight_grads",
    )
    ins = (normed_x_t, d_beta, gain_one_sum, gain_two_sum)
    grad_in = grads_into(
        functools.partial(small_grads, heads),
        ins,
        whole(*ins),
        column_at((width, 128), heads * cols // 128),
        1,
        "small_grads",
        [pltpu.VMEM((128, width), WIDE)],
    )
    reduced_in = lax.psum_scatter(grad_in, "seq", scatter_dimension=0, tiled=True)
    *grads, small_sum, grad_out_t = run(
        functools.partial(grad_join, heads, dim),
        "grad_join",
        (reduced_in,),
        whole(reduced_in),
        [((shard, inner), WIDE)] * 4 + [((shard, 128), WIDE), ((shard, inner), WIDE)],
    )
    gain_sums = total(over_heads(small_sum))
    reduced_mlp = reduced_mlp.astype(WIDE)
    return (
        result,
        d_tokens,
        gain_sums[:, heads],
        *grads,
        small_sum[:, :heads],
        grad_out_t.T,
        gain_sums[:, heads + 1],
        reduced_mlp[:, :hidden_units],
        reduced_mlp[:, hidden_units : 2 * hidden_units],
        reduced_mlp[:, 2 * hidden_units :].T,
    )


def solution(mesh):
    placed = (
        P("seq", None),
        P("seq", None),
        P("seq"),
        P("seq"),
        P("seq", "head"),
        P("seq", "head"),
        P("seq", "head"),
        P("seq", "head"),
        P("seq", "head"),
        P("head", "seq"),
        P("seq"),
        P("seq", "head"),
        P("seq", "head"),
        P("head", "seq"),
    )
    return jax.shard_map(
        per_device,
        mesh=mesh,
        in_specs=placed,
        out_specs=(
            P("seq", None),
            P("seq", None),
            P("seq"),
            P("seq", "head"),
            P("seq", "head"),
            P("seq", "head"),
            P("seq", "head"),
            P("seq", "head"),
            P("head", "seq"),
            P("seq"),
            P("seq", "head"),
            P("seq", "head"),
            P("head", "seq"),
        ),
        check_vma=False,
    )
```

time: 823 us -> 591 us (0.72)
  waiting for transfers between devices: 597 us -> 233 us
  Pallas kernels: 54.3 us -> 188 us
  starting transfers between devices: 1.41 us -> 104 us
  matrix products: 61.1 us -> 0 us
  local copies, waits for them, and re-layouts: 48.3 us -> 25.4 us
  other arithmetic: 36.6 us -> 14.9 us
    psum x3 -> x0, waiting for transfers between devices: 214 us -> none  [the longest x1 87.3 us: per_device(): d_normed = lax.psum(back_one.astype(LOW), 'head').astype(WIDE)]
    ppermute x0 -> x51, waiting for transfers between devices: none -> 209 us  [xor_move(): lax.ppermute(value, axis, [(at, at ^ mask) for at in range(lax.axis_size(...]
    pallas_call x4 -> x29, Pallas kernels: 54.3 us -> 188 us  [the longest x22 131 us: run(): pl.pallas_call(kernel, grid=(1,), in_specs=specs, out_specs=[fixed(shape)...]
    all_gather x3 -> x4, waiting for transfers between devices: 146 us -> 24.5 us  [the longest x1 16.4 us: per_device(): lax.all_gather(jnp.concatenate(parts, axis=1), 'seq', axis=0, tiled=True)]
    ppermute x0 -> x51, starting transfers between devices: none -> 103 us  [xor_move(): lax.ppermute(value, axis, [(at, at ^ mask) for at in range(lax.axis_size(...]
    reduce_scatter x1, waiting for transfers between devices: 87.7 us -> 0.01 us  [per_device(): lax.psum_scatter(grad_mlp, 'seq', scatter_dimension=0, tiled=True)]
    unnamed x12 -> x6, waiting for transfers between devices: 85.8 us -> 0.1 us
    reduce_scatter x1, waiting for transfers between devices: 63.9 us -> 0.01 us  [per_device(): lax.psum_scatter(grad_in, 'seq', scatter_dimension=0, tiled=True)]
  transfers between devices with their start and end apart: 10 -> 57, of which waited for: 10 -> 31; matrix products, arithmetic and copies ran while one was open for 10% -> 4% of each run, Pallas kernels for 1% -> 26%
where the time goes in v2:
time: 591 us; the launch traced here: 580 us
  waiting for transfers between devices  233 us (39%)
  Pallas kernels  188 us (32%)
  starting transfers between devices  104 us (18%)
  local copies, waits for them, and re-layouts  25.4 us (4%)
  other arithmetic  14.9 us (3%)
  between operations  14.8 us (3%)
    ppermute x51, waiting for transfers between devices, xor_move(): lax.ppermute(value, axis, [(at, at ^ mask) for at in range(lax.axis_size(...  209 us
    pallas_call x22, Pallas kernels, run(): pl.pallas_call(kernel, grid=(1,), in_specs=specs, out_specs=[fixed(shape)...  131 us
    ppermute x51, starting transfers between devices, xor_move(): lax.ppermute(value, axis, [(at, at ^ mask) for at in range(lax.axis_size(...  103 us
    pallas_call x1, Pallas kernels, per_device(): pl.pallas_call(mlp_forward, grid=(blocks,), in_specs=[fixed(tall), pl.Blo...  20.2 us
    pallas_call x5, Pallas kernels, grads_into(): pl.pallas_call(kernel, grid=(grid,), in_specs=specs + [ANYWHERE] * len(gi...  18.9 us
    pallas_call x1, Pallas kernels, per_device(): pl.pallas_call(mlp_grads, grid=(3 * blocks,), in_specs=[fixed(tall), pl.B...  17.6 us
    all_gather x1, waiting for transfers between devices, per_device(): lax.all_gather(jnp.concatenate(parts, axis=1), 'seq', axis=0, tiled=True)  16.4 us
    unnamed x106, local copies, waits for them, and re-layouts  14 us
  transfers between devices with their start and end apart: 57, of which 31 were waited for; matrix products, arithmetic and copies ran while one was open for 4% of the time, Pallas kernels for 26%

profile of v2, /device:TPU:0, one launch (start us, length us, event | category | flops | bytes accessed | tf_op | source)
XLA Modules:
  0.0 579.9 jit_solution(13502946470804883876)
XLA Ops:
  30.4 8.3 %collective-permute-done.4 = bf16[192,384]{1,0:T(8,128)(2,1)S(1)} collective-permute-done((bf16[192,384]{1,0:T(8,128)(2,1)S(1)}, bf16[192,384]{1,0:T(8,128)(2,1)S(1)}, u32[]{:S(2)}, u32[]{:S(2)}) %collective-permute-start.4) | collective-permute-done | bytes 147488 | tf_op jit(solution)/shard_map/ppermute | solution.py:80
  39.5 16.4 %all-gather.5.cloned.1.call-done.w_ref = bf16[1536,1664]{1,0:T(8,128)(2,1)} async-done(((bf16[192,1664]{1,0:T(8,128)(2,1)}), bf16[1536,1664]{1,0:T(8,128)(2,1)}) %all-gather.5.cloned.1.call-update) | async-done | bytes 5111824 | tf_op jit(solution)/shard_map/all_gather | solution.py:648
  62.9 12.1 %block_forward.3 = (f32[512,512]{1,0:T(8,128)}, bf16[1152,128]{1,0:T(8,128)(2,1)}, f32[512,128]{1,0:T(8,128)}, f32[512,512]{1,0:T(8,128)}, bf16[512,512]{1,0:T(8...) custom-call(s32[3]{0:T(128)} %pad_add_fusion.place_ref.places_ref, ...), custom_call_target="tpu_custom_call" | custom-call | flops 10000000000 | bytes 4194304 | tf_op jit(solution)/shard_map/block_forward/pallas_call | solution.py:524
  76.5 12.6 %block_forward.4 = (f32[512,512]{1,0:T(8,128)}, bf16[1152,128]{1,0:T(8,128)(2,1)}, f32[512,128]{1,0:T(8,128)}, f32[512,512]{1,0:T(8,128)}, bf16[512,512]{1,0:T(8...) custom-call(s32[3]{0:T(128)} %pad_add_fusion.place_ref.places_ref, ...), custom_call_target="tpu_custom_call" | custom-call | flops 10000000000 | bytes 4194304 | tf_op jit(solution)/shard_map/block_forward/pallas_call | solution.py:524
  91.3 12.1 %block_forward.5 = (f32[512,512]{1,0:T(8,128)}, bf16[1152,128]{1,0:T(8,128)(2,1)}, f32[512,128]{1,0:T(8,128)}, f32[512,512]{1,0:T(8,128)}, bf16[512,512]{1,0:T(8...) custom-call(s32[3]{0:T(128)} %pad_add_fusion.place_ref.places_ref, ...), custom_call_target="tpu_custom_call" | custom-call | flops 10000000000 | bytes 4194304 | tf_op jit(solution)/shard_map/block_forward/pallas_call | solution.py:524
  103.4 11.1 %collective-permute-done.8 = bf16[2,1152,128]{2,1,0:T(8,128)(2,1)S(1)} collective-permute-done((bf16[2,1152,128]{2,1,0:T(8,128)(2,1)S(1)}, bf16[2,1152,128]{2,1,0:T(8,128)(2,1)S(1)}, u32[]{:S(2)}, u32[]{:S(2)}) %collective-permute-start.8) | collective-permute-done | bytes 589856 | tf_op jit(solution)/shard_map/ppermute | solution.py:80
  127.2 11.7 %collective-permute-done.11 = bf16[2,1152,128]{2,1,0:T(8,128)(2,1)S(1)} collective-permute-done((bf16[2,1152,128]{2,1,0:T(8,128)(2,1)S(1)}, bf16[2,1152,128]{2,1,0:T(8,128)(2,1)S(1)}, u32[]{:S(2)}, u32[]{:S(2)}) %collective-permute-start.11) | collective-permute-done | bytes 589856 | tf_op jit(solution)/shard_map/ppermute | solution.py:80
  146.9 13.2 %collective-permute-done.13 = bf16[2,1152,128]{2,1,0:T(8,128)(2,1)S(1)} collective-permute-done((bf16[2,1152,128]{2,1,0:T(8,128)(2,1)S(1)}, bf16[2,1152,128]{2,1,0:T(8,128)(2,1)S(1)}, u32[]{:S(2)}, u32[]{:S(2)}) %collective-permute-start.13) | collective-permute-done | bytes 589856 | tf_op jit(solution)/shard_map/ppermute | solution.py:80
  192.6 9.7 %collective-permute-done.20.rest_3_ = bf16[128,1536]{1,0:T(8,128)(2,1)S(1)} collective-permute-done((bf16[128,1536]{1,0:T(8,128)(2,1)}, bf16[128,1536]{1,0:T(8,128)(2,1)S(1)}, u32[]{:S(2)}, u32[]{:S(2)}) %collective-permute-start.20) | collective-permute-done | bytes 393248 | tf_op jit(solution)/shard_map/ppermute | solution.py:80
  202.3 22.6 %collective-permute-done.19.rest_2_ = bf16[128,1536]{1,0:T(8,128)(2,1)S(1)} collective-permute-done((bf16[128,1536]{1,0:T(8,128)(2,1)}, bf16[128,1536]{1,0:T(8,128)(2,1)S(1)}, u32[]{:S(2)}, u32[]{:S(2)}) %collective-permute-start.19) | collective-permute-done | bytes 393248 | tf_op jit(solution)/shard_map/ppermute | solution.py:80
  225.9 20.2 %mlp_forward.1 = (bf16[3,512,1024]{2,1,0:T(8,128)(2,1)}, bf16[128,1536]{1,0:T(8,128)(2,1)}, bf16[128,1536]{1,0:T(8,128)(2,1)}, bf16[128,1536]{1,0:T(8,128)(2,1)}, bf16[128,1536]{1,0:T(8,128)(2,1)}) custom-call(bf16[512,1536]{1,0:T(8,128)(2,1)} %get-tuple-element.207.cot_ref, bf16[1536,3072]{1,0:T(8,128)(2,1)} %all-gather.9.cloned.1.call-done.gate_ref.up_ref.down_ref, ...), custom_call_target="tpu_custom_call" | custom-call | flops 10000000000 | bytes 16777216 | tf_op jit(solution)/shard_map/mlp_forward/pallas_call | solution.py:734
  250.5 17.6 %mlp_grads.1 = (bf16[1536,3072]{1,0:T(8,128)(2,1)}, bf16[128,1536]{1,0:T(8,128)(2,1)}, bf16[128,1536]{1,0:T(8,128)(2,1)}, bf16[128,1536]{1,0:T(8,128)(2,1)}, bf16[128,1536]{1,0:T(8,128)(2,1)}) custom-call(bf16[512,1536]{1,0:T(8,128)(2,1)} %get-tuple-element.207.cot_ref, bf16[3,512,1024]{2,1,0:T(8,128)(2,1)} %get-tuple-element.270.all_ref, ...), custom_call_target="tpu_custom_call" | custom-call | flops 10000000000 | bytes 16777216 | tf_op jit(solution)/shard_map/mlp_grads/pallas_call | solution.py:753
  268.2 8.1 %collective-permute-done.22.rest_2_ = bf16[128,1536]{1,0:T(8,128)(2,1)S(1)} collective-permute-done((bf16[128,1536]{1,0:T(8,128)(2,1)}, bf16[128,1536]{1,0:T(8,128)(2,1)S(1)}, u32[]{:S(2)}, u32[]{:S(2)}) %collective-permute-start.22) | collective-permute-done | bytes 393248 | tf_op jit(solution)/shard_map/ppermute | solution.py:80
  282.5 7.4 %collective-permute-start.24 = (bf16[128,384]{1,0:T(8,128)(2,1)}, bf16[128,384]{1,0:T(8,128)(2,1)S(1)}, u32[]{:S(2)}, u32[]{:S(2)}) collective-permute-start(bf16[128,384]{1,0:T(8,128)(2,1)} %get-tuple-element.289), channel_id=1, source_target_pairs={{0,8},{8,0},{16,24},{24,16},{1,9},{9,1},{17,25},{25,17},{2,10},{10... | collective-permute-start | bytes 294920 | tf_op jit(solution)/shard_map/ppermute | solution.py:80
  317.8 19.3 %collective-permute-done.29 = bf16[128,1536]{1,0:T(8,128)(2,1)S(1)} collective-permute-done((bf16[128,1536]{1,0:T(8,128)(2,1)S(1)}, bf16[128,1536]{1,0:T(8,128)(2,1)S(1)}, u32[]{:S(2)}, u32[]{:S(2)}) %collective-permute-start.29) | collective-permute-done | bytes 393248 | tf_op jit(solution)/shard_map/ppermute | solution.py:80
  339.9 11.8 %collective-permute-start.31 = (bf16[2,1152,128]{2,1,0:T(8,128)(2,1)S(1)}, bf16[2,1152,128]{2,1,0:T(8,128)(2,1)S(1)}, u32[]{:S(2)}, u32[]{:S(2)}) collective-permute-start(bf16[2,1152,128]{2,1,0:T(8,128)(2,1)S(1)} %slice.140), channel_id=1, source_target_pairs={{0,4},{1,5},{2,6},{3,7},{4,0},{5,1},{6,2},{7,3},{8,12},{9,13},{10,... | collective-permute-start | bytes 1769480 | tf_op jit(solution)/shard_map/ppermute | solution.py:80
  356.9 18.6 %collective-permute-done.31 = bf16[2,1152,128]{2,1,0:T(8,128)(2,1)S(1)} collective-permute-done((bf16[2,1152,128]{2,1,0:T(8,128)(2,1)S(1)}, bf16[2,1152,128]{2,1,0:T(8,128)(2,1)S(1)}, u32[]{:S(2)}, u32[]{:S(2)}) %collective-permute-start.31) | collective-permute-done | bytes 589856 | tf_op jit(solution)/shard_map/ppermute | solution.py:80
  414.3 7.5 %block_backward.4 = (bf16[512,512]{1,0:T(8,128)(2,1)}, bf16[512,128]{1,0:T(8,128)(2,1)}) custom-call(s32[3]{0:T(128)} %pad_add_fusion.place_ref.places_ref, f32[512,512]{1,0:T(8,128)} %get-tuple-element.340.proj_ref, f32[512,128]{1,0:T(8,128)} %get-tuple-element.209.beta_ref, bf16[512,512]{1,0:T(8,128)(2,1)} %get-tuple-element.341.inv_ref, ...), custom_call_target="tpu_custom_call" | custom-call | flops 5000000000 | bytes 4194304 | tf_op jit(solution)/shard_map/block_backward/pallas_call | solution.py:524
  452.4 8.0 %all-gather.11.cloned.1.call-done.branch_ref = bf16[512,1536]{1,0:T(8,128)(2,1)} async-done(((bf16[128,1536]{1,0:T(8,128)(2,1)}), bf16[512,1536]{1,0:T(8,128)(2,1)}) %all-gather.11.cloned.1.call-update) | async-done | bytes 1572880 | tf_op jit(solution)/shard_map/all_gather | solution.py:811
  472.9 7.5 %collective-permute-start.42 = (bf16[128,1536]{1,0:T(8,128)(2,1)S(1)}, bf16[128,1536]{1,0:T(8,128)(2,1)S(1)}, u32[]{:S(2)}, u32[]{:S(2)}) collective-permute-start(bf16[128,1536]{1,0:T(8,128)(2,1)S(1)} %copy-done.42), channel_id=1, source_target_pairs={{0,8},{8,0},{16,24},{24,16},{1,9},{9,1},{17,25},{25,17},{2,10},{10... | collective-permute-start | bytes 1179656 | tf_op jit(solution)/shard_map/ppermute | solution.py:80
  482.9 13.4 %collective-permute-done.42.rest_1_ = bf16[128,1536]{1,0:T(8,128)(2,1)S(1)} collective-permute-done((bf16[128,1536]{1,0:T(8,128)(2,1)S(1)}, bf16[128,1536]{1,0:T(8,128)(2,1)S(1)}, u32[]{:S(2)}, u32[]{:S(2)}) %collective-permute-start.42) | collective-permute-done | bytes 393248 | tf_op jit(solution)/shard_map/ppermute | solution.py:80
  496.3 13.9 %collective-permute-done.43.rest_2_ = bf16[128,1536]{1,0:T(8,128)(2,1)S(1)} collective-permute-done((bf16[128,1536]{1,0:T(8,128)(2,1)S(1)}, bf16[128,1536]{1,0:T(8,128)(2,1)S(1)}, u32[]{:S(2)}, u32[]{:S(2)}) %collective-permute-start.43) | collective-permute-done | bytes 393248 | tf_op jit(solution)/shard_map/ppermute | solution.py:80
  515.4 21.4 %collective-permute-start.46 = (bf16[128,1536]{1,0:T(8,128)(2,1)}, bf16[128,1536]{1,0:T(8,128)(2,1)S(1)}, u32[]{:S(2)}, u32[]{:S(2)}) collective-permute-start(bf16[128,1536]{1,0:T(8,128)(2,1)} %token_grad.1.rest_0_), channel_id=1, source_target_pairs={{0,16},{8,24},{16,0},{24,8},{1,17},{9,25},{17,1},{25,9},{2,18},{10... | collective-permute-start | bytes 1179656 | tf_op jit(solution)/shard_map/ppermute | solution.py:80
  539.4 15.8 %collective-permute-done.46.rest_2_ = bf16[128,1536]{1,0:T(8,128)(2,1)S(1)} collective-permute-done((bf16[128,1536]{1,0:T(8,128)(2,1)}, bf16[128,1536]{1,0:T(8,128)(2,1)S(1)}, u32[]{:S(2)}, u32[]{:S(2)}) %collective-permute-start.46) | collective-permute-done | bytes 393248 | tf_op jit(solution)/shard_map/ppermute | solution.py:80
  (275 shorter events, 244.8 us)
Async XLA Ops:
  7.2 48.8 %all-gather.5.cloned.1.call-start = ((), (), s32[]{:S(2)}) async-start(), calls=%async_computation.2 | async-start | bytes 5750784 | tf_op jit(solution)/shard_map/all_gather | solution.py:648
  12.5 126.3 %all-gather.7.cloned.1.call-start = ((), (), s32[]{:S(2)}) async-start(), calls=%async_computation.3 | async-start | bytes 5308416 | tf_op jit(solution)/shard_map/all_gather | solution.py:652
  56.0 169.0 %all-gather.9.cloned.1.call-start = ((), (), s32[]{:S(2)}) async-start(), calls=%async_computation.4 | async-start | bytes 10616832 | tf_op jit(solution)/shard_map/all_gather | solution.py:716
  89.7 24.8 %collective-permute-start.8 = (bf16[2,1152,128]{2,1,0:T(8,128)(2,1)S(1)}, bf16[2,1152,128]{2,1,0:T(8,128)(2,1)S(1)}, u32[]{:S(2)}, u32[]{:S(2)}) collective-permute-start(bf16[2,1152,128]{2,1,0:T(8,128)(2,1)S(1)} %pad_maximum_fusion.8), channel_id=1, source_target_pairs={{0,4},{1,5},{2,6},{3,7},{4,0},{5,1},{6,2},{7,3},{8,12},{9,13},{10,... | collective-permute-start | bytes 1769480 | tf_op jit(solution)/shard_map/ppermute | solution.py:80
  138.9 270.5 %reduce-scatter.3.cloned.1.call-start = ((), (), s32[]{:S(2)}) async-start(), calls=%async_computation.5 | async-start | bytes 10616832 | tf_op jit(solution)/shard_map/reduce_scatter | solution.py:772
  190.7 34.2 %collective-permute-start.19 = (bf16[128,1536]{1,0:T(8,128)(2,1)}, bf16[128,1536]{1,0:T(8,128)(2,1)S(1)}, u32[]{:S(2)}, u32[]{:S(2)}) collective-permute-start(bf16[128,1536]{1,0:T(8,128)(2,1)} %get-tuple-element.269.rest_0_), channel_id=1, source_target_pairs={{0,16},{8,24},{16,0},{24,8},{1,17},{9,25},{17,1},{25,9},{2,18},{10... | collective-permute-start | bytes 1179656 | tf_op jit(solution)/shard_map/ppermute | solution.py:80
  190.7 34.2 %collective-permute-start.18 = (bf16[128,1536]{1,0:T(8,128)(2,1)}, bf16[128,1536]{1,0:T(8,128)(2,1)S(1)}, u32[]{:S(2)}, u32[]{:S(2)}) collective-permute-start(bf16[128,1536]{1,0:T(8,128)(2,1)} %get-tuple-element.269.rest_0_), channel_id=1, source_target_pairs={{0,8},{8,0},{16,24},{24,16},{1,9},{9,1},{17,25},{25,17},{2,10},{10... | collective-permute-start | bytes 1179656 | tf_op jit(solution)/shard_map/ppermute | solution.py:80
  246.2 30.1 %collective-permute-start.22 = (bf16[128,1536]{1,0:T(8,128)(2,1)}, bf16[128,1536]{1,0:T(8,128)(2,1)S(1)}, u32[]{:S(2)}, u32[]{:S(2)}) collective-permute-start(bf16[128,1536]{1,0:T(8,128)(2,1)} %get-tuple-element.279), channel_id=1, source_target_pairs={{0,16},{8,24},{16,0},{24,8},{1,17},{9,25},{17,1},{25,9},{2,18},{10... | collective-permute-start | bytes 1179656 | tf_op jit(solution)/shard_map/ppermute | solution.py:80
  247.9 28.3 %collective-permute-start.23 = (bf16[128,1536]{1,0:T(8,128)(2,1)}, bf16[128,1536]{1,0:T(8,128)(2,1)S(1)}, u32[]{:S(2)}, u32[]{:S(2)}) collective-permute-start(bf16[128,1536]{1,0:T(8,128)(2,1)} %get-tuple-element.280), channel_id=1, source_target_pairs={{0,24},{8,16},{16,8},{24,0},{1,25},{9,17},{17,9},{25,1},{2,26},{10... | collective-permute-start | bytes 1179656 | tf_op jit(solution)/shard_map/ppermute | solution.py:80
  277.1 183.3 %all-gather.11.cloned.1.call-start = ((), (), s32[]{:S(2)}) async-start(), calls=%async_computation.6 | async-start | bytes 1966080 | tf_op jit(solution)/shard_map/all_gather | solution.py:811
  307.4 29.7 %collective-permute-start.28 = (bf16[4,1152,128]{2,1,0:T(8,128)(2,1)}, bf16[4,1152,128]{2,1,0:T(8,128)(2,1)S(1)}, u32[]{:S(2)}, u32[]{:S(2)}) collective-permute-start(bf16[4,1152,128]{2,1,0:T(8,128)(2,1)} %get-tuple-element.308), channel_id=1, source_target_pairs={{0,1},{1,0},{2,3},{3,2},{4,5},{5,4},{6,7},{7,6},{8,9},{9,8},{10,11... | collective-permute-start | bytes 3538952 | tf_op jit(solution)/shard_map/ppermute | solution.py:80
  307.4 29.7 %collective-permute-start.29 = (bf16[128,1536]{1,0:T(8,128)(2,1)S(1)}, bf16[128,1536]{1,0:T(8,128)(2,1)S(1)}, u32[]{:S(2)}, u32[]{:S(2)}) collective-permute-start(bf16[128,1536]{1,0:T(8,128)(2,1)S(1)} %copy-done.37), channel_id=1, source_target_pairs={{0,16},{8,24},{16,0},{24,8},{1,17},{9,25},{17,1},{25,9},{2,18},{10... | collective-permute-start | bytes 1179656 | tf_op jit(solution)/shard_map/ppermute | solution.py:80
  309.0 47.9 %collective-permute-start.32 = (bf16[128,1536]{1,0:T(8,128)(2,1)}, bf16[128,1536]{1,0:T(8,128)(2,1)S(1)}, u32[]{:S(2)}, u32[]{:S(2)}) collective-permute-start(bf16[128,1536]{1,0:T(8,128)(2,1)} %get-tuple-element.324), channel_id=1, source_target_pairs={{0,24},{8,16},{16,8},{24,0},{1,25},{9,17},{17,9},{25,1},{2,26},{10... | collective-permute-start | bytes 1179656 | tf_op jit(solution)/shard_map/ppermute | solution.py:80
  338.3 37.2 %collective-permute-start.30 = (bf16[4,1152,128]{2,1,0:T(8,128)(2,1)}, bf16[4,1152,128]{2,1,0:T(8,128)(2,1)S(1)}, u32[]{:S(2)}, u32[]{:S(2)}) collective-permute-start(bf16[4,1152,128]{2,1,0:T(8,128)(2,1)} %get-tuple-element.321), channel_id=1, source_target_pairs={{0,1},{1,0},{2,3},{3,2},{4,5},{5,4},{6,7},{7,6},{8,9},{9,8},{10,11... | collective-permute-start | bytes 3538952 | tf_op jit(solution)/shard_map/ppermute | solution.py:80
  339.9 35.6 %collective-permute-start.31 = (bf16[2,1152,128]{2,1,0:T(8,128)(2,1)S(1)}, bf16[2,1152,128]{2,1,0:T(8,128)(2,1)S(1)}, u32[]{:S(2)}, u32[]{:S(2)}) collective-permute-start(bf16[2,1152,128]{2,1,0:T(8,128)(2,1)S(1)} %slice.140), channel_id=1, source_target_pairs={{0,4},{1,5},{2,6},{3,7},{4,0},{5,1},{6,2},{7,3},{8,12},{9,13},{10,... | collective-permute-start | bytes 1769480 | tf_op jit(solution)/shard_map/ppermute | solution.py:80
  377.9 23.8 %collective-permute-start.36 = (bf16[4,1152,128]{2,1,0:T(8,128)(2,1)}, bf16[4,1152,128]{2,1,0:T(8,128)(2,1)S(1)}, u32[]{:S(2)}, u32[]{:S(2)}) collective-permute-start(bf16[4,1152,128]{2,1,0:T(8,128)(2,1)} %get-tuple-element.338), channel_id=1, source_target_pairs={{0,1},{1,0},{2,3},{3,2},{4,5},{5,4},{6,7},{7,6},{8,9},{9,8},{10,11... | collective-permute-start | bytes 3538952 | tf_op jit(solution)/shard_map/ppermute | solution.py:80
  378.3 23.4 %collective-permute-start.35 = (bf16[2,1152,128]{2,1,0:T(8,128)(2,1)S(1)}, bf16[2,1152,128]{2,1,0:T(8,128)(2,1)S(1)}, u32[]{:S(2)}, u32[]{:S(2)}) collective-permute-start(bf16[2,1152,128]{2,1,0:T(8,128)(2,1)S(1)} %slice.144), channel_id=1, source_target_pairs={{0,2},{1,3},{2,0},{3,1},{4,6},{5,7},{6,4},{7,5},{8,10},{9,11},{10,... | collective-permute-start | bytes 1769480 | tf_op jit(solution)/shard_map/ppermute | solution.py:80
  380.4 41.4 %collective-permute-start.38 = (bf16[128,1536]{1,0:T(8,128)(2,1)}, bf16[128,1536]{1,0:T(8,128)(2,1)}, u32[]{:S(2)}, u32[]{:S(2)}) collective-permute-start(bf16[128,1536]{1,0:T(8,128)(2,1)} %add_convert_fusion.6.rest_0_), channel_id=1, source_target_pairs={{0,16},{8,24},{16,0},{24,8},{1,17},{9,25},{17,1},{25,9},{2,18},{10... | collective-permute-start | bytes 1179656 | tf_op jit(solution)/shard_map/ppermute | solution.py:80
  409.4 152.1 %reduce-scatter.5.cloned.1.call-start = ((), (), s32[]{:S(2)}) async-start(), calls=%async_computation.7 | async-start | bytes 7077888 | tf_op jit(solution)/shard_map/reduce_scatter | solution.py:933
  472.9 23.4 %collective-permute-start.42 = (bf16[128,1536]{1,0:T(8,128)(2,1)S(1)}, bf16[128,1536]{1,0:T(8,128)(2,1)S(1)}, u32[]{:S(2)}, u32[]{:S(2)}) collective-permute-start(bf16[128,1536]{1,0:T(8,128)(2,1)S(1)} %copy-done.42), channel_id=1, source_target_pairs={{0,8},{8,0},{16,24},{24,16},{1,9},{9,1},{17,25},{25,17},{2,10},{10... | collective-permute-start | bytes 1179656 | tf_op jit(solution)/shard_map/ppermute | solution.py:80
  480.5 29.8 %collective-permute-start.43 = (bf16[128,1536]{1,0:T(8,128)(2,1)S(1)}, bf16[128,1536]{1,0:T(8,128)(2,1)S(1)}, u32[]{:S(2)}, u32[]{:S(2)}) collective-permute-start(bf16[128,1536]{1,0:T(8,128)(2,1)S(1)} %copy-done.40), channel_id=1, source_target_pairs={{0,16},{8,24},{16,0},{24,8},{1,17},{9,25},{17,1},{25,9},{2,18},{10... | collective-permute-start | bytes 1179656 | tf_op jit(solution)/shard_map/ppermute | solution.py:80
  480.5 29.8 %collective-permute-start.44 = (bf16[128,1536]{1,0:T(8,128)(2,1)S(1)}, bf16[128,1536]{1,0:T(8,128)(2,1)S(1)}, u32[]{:S(2)}, u32[]{:S(2)}) collective-permute-start(bf16[128,1536]{1,0:T(8,128)(2,1)S(1)} %copy-done.39), channel_id=1, source_target_pairs={{0,24},{8,16},{16,8},{24,0},{1,25},{9,17},{17,9},{25,1},{2,26},{10... | collective-permute-start | bytes 1179656 | tf_op jit(solution)/shard_map/ppermute | solution.py:80
  514.3 25.0 %collective-permute-start.47 = (bf16[128,1536]{1,0:T(8,128)(2,1)}, bf16[128,1536]{1,0:T(8,128)(2,1)S(1)}, u32[]{:S(2)}, u32[]{:S(2)}) collective-permute-start(bf16[128,1536]{1,0:T(8,128)(2,1)} %token_grad.1.rest_0_), channel_id=1, source_target_pairs={{0,24},{8,16},{16,8},{24,0},{1,25},{9,17},{17,9},{25,1},{2,26},{10... | collective-permute-start | bytes 1179656 | tf_op jit(solution)/shard_map/ppermute | solution.py:80
  515.4 39.8 %collective-permute-start.46 = (bf16[128,1536]{1,0:T(8,128)(2,1)}, bf16[128,1536]{1,0:T(8,128)(2,1)S(1)}, u32[]{:S(2)}, u32[]{:S(2)}) collective-permute-start(bf16[128,1536]{1,0:T(8,128)(2,1)} %token_grad.1.rest_0_), channel_id=1, source_target_pairs={{0,16},{8,24},{16,0},{24,8},{1,17},{9,25},{17,1},{25,9},{2,18},{10... | collective-permute-start | bytes 1179656 | tf_op jit(solution)/shard_map/ppermute | solution.py:80
  (84 other events, 629.8 us)
Sparse Core Ops, SparseCore 0:
  12.7 43.2 all-gather.4
  58.4 42.5 all-gather.6
  139.0 63.5 all-gather.8
  276.4 98.1 reduce-scatter.2
  409.5 50.8 all-gather.10
  472.1 66.8 reduce-scatter.4

commit v3 on v2

--- a/solution.py
+++ b/solution.py
@@ -10,6 +10,7 @@
 SPAN = 8
 EPSILON = 1e-06
 NEGATIVE = -1e30
+LOG2E = 1.4426950408889634
 LOW = jnp.bfloat16
 WIDE = jnp.float32
 VMEM_BYTES = 60 * 2**20
@@ -128,57 +129,97 @@
     qdir_ref[...] = qdir_two[0]
     solve_ref[...] = solve_two[0]
     allowed = (doc_col_ref[:, 0:1] == doc_row_ref[pl.ds(place_ref[0], 1), :]) & (row >= col)
-    score = jnp.where(allowed, inside * dim**-0.5, NEGATIVE)
+    score = jnp.where(allowed, inside * (LOG2E * dim**-0.5), NEGATIVE)
     score_ref[...] = score
     peak = jnp.max(score, axis=1, keepdims=True)
-    weight = jnp.exp(score - peak)
+    weight = jnp.exp2(score - peak)
     lane = iota((length, 128), 1)
     stat_ref[...] = jnp.where(lane == 0, peak, jnp.sum(weight, axis=1, keepdims=True))
     acc_ref[...] = mm(weight, value)
 
 
+def bring(halves_in, pack_ref, sems):
+    size = halves_in[0].shape[0]
+    copies = [
+        pltpu.make_async_copy(part, pack_ref.at[pl.ds(at * size, size)], sems.at[at]) for at, part in enumerate(halves_in)
+    ]
+    for copy in copies:
+        copy.start()
+    for copy in copies:
+        copy.wait()
+
+
 def slot_of(mask, swapped):
     core, first, second = mask & 1, (mask >> 1) & 1, mask >> 2
     return 4 * core + (2 * first + second if swapped else first + 2 * second)
 
 
 def cross_forward(
-    swapped, place_ref, qm_ref, stat_in_ref, acc_ref, doc_col_ref, doc_row_ref, pack_ref,
-    att_ref, att_x_ref, log_ref, moved_ref, stat_ref,
+    swapped, place_ref, qm_ref, stat_in_ref, acc_ref, doc_col_ref, doc_row_ref, far_ref, core_ref,
+    att_ref, att_x_ref, log_ref, pack_ref, moved_ref, score_ref, peak_ref, sems,
 ):
+    bring((far_ref, core_ref), pack_ref, sems)
     length, dim = qm_ref.shape
     place = place_ref[0]
-    doc_col = doc_col_ref[:, 0:1]
     moved_ref[...] = qm_ref[...]
     att_ref[...] = acc_ref[...]
-    stat_ref[0] = stat_in_ref[:, 0:1]
-    stat_ref[1] = stat_in_ref[:, 1:2]
-
-    def hop(step, carry):
+    own_peak = stat_in_ref[:, 0:1]
+    peak_ref[...] = jnp.broadcast_to(own_peak, (length, 128))
+
+    def look(step, carry):
         at = place - step
         slot = slot_of(place ^ at, swapped)
-        key = pack_ref[slot, 0:length, :]
-        value = pack_ref[slot, length : 2 * length, :]
-        through = pack_ref[slot, 2 * length :, :]
-        allowed = doc_col == doc_row_ref[pl.ds(at, 1), :]
         moved = moved_ref[...]
-        peak = stat_ref[0]
-        score = jnp.where(allowed, mm(moved, key, tb=True) * dim**-0.5, NEGATIVE)
-        new_peak = jnp.maximum(peak, jnp.max(score, axis=1, keepdims=True))
-        rescale = jnp.exp(peak - new_peak)
-        weight = jnp.exp(score - new_peak)
-        stat_ref[0] = new_peak
-        stat_ref[1] = stat_ref[1] * rescale + jnp.sum(weight, axis=1, keepdims=True)
-        att_ref[...] = att_ref[...] * rescale + mm(weight, value)
-        moved_ref[...] = mm(moved, through)
+        score = mm(moved * (LOG2E * dim**-0.5), pack_ref[slot, 0:length, :], tb=True)
+        moved_ref[...] = mm(moved, pack_ref[slot, 2 * length :, :])
+        allowed = doc_col_ref[:, 0:1] == doc_row_ref[pl.ds(at, 1), :]
+        score = jnp.where(allowed, score, NEGATIVE)
+        score_ref[at] = score
+        high = peak_ref[...]
+        for lane in range(0, length, 128):
+            high = jnp.maximum(high, score[:, lane : lane + 128])
+        peak_ref[...] = high
         return carry
 
-    lax.fori_loop(1, place + 1, hop, 0)
-    total = stat_ref[1]
+    def two_looks(pair, carry):
+        look(2 * pair + 1, carry)
+        return look(2 * pair + 2, carry)
+
+    lax.fori_loop(0, place // 2, two_looks, 0)
+    lax.fori_loop(place // 2 * 2 + 1, place + 1, look, 0)
+    peak = jnp.max(peak_ref[...], axis=1, keepdims=True)
+    rescale = jnp.exp2(own_peak - peak)
+    att_ref[...] = att_ref[...] * rescale
+    lanes = iota((length, 128), 1)
+    moved_ref[...] = jnp.where(lanes == 0, stat_in_ref[:, 1:2] * rescale, 0.0)
+
+    def use(at, carry):
+        slot = slot_of(place ^ at, swapped)
+        weight = jnp.exp2(score_ref[at] - peak)
+        sums = moved_ref[...]
+        for lane in range(0, length, 128):
+            sums = sums + weight[:, lane : lane + 128]
+        moved_ref[...] = sums
+        att_ref[...] += mm(weight, pack_ref[slot, length : 2 * length, :])
+        return carry
+
+    def two_uses(pair, carry):
+        use(2 * pair, carry)
+        return use(2 * pair + 1, carry)
+
+    lax.fori_loop(0, place // 2, two_uses, 0)
+    lax.fori_loop(place // 2 * 2, place, use, 0)
+    total = jnp.sum(moved_ref[...], axis=1, keepdims=True)
     attention = att_ref[...] / total
     att_ref[...] = attention
     scatter_rows(att_x_ref, slice(None), attention.astype(LOW), place_ref[1])
-    log_ref[...] = jnp.broadcast_to(stat_ref[0] + jnp.log(total), (length, dim))
+    log_ref[...] = jnp.broadcast_to(peak + jnp.log2(total), (length, 128))
+
+
+def same_document(doc_row_ref, at, place):
+    first = doc_row_ref[pl.ds(at, 1), :][:, 0:1]
+    last = doc_row_ref[pl.ds(place, 1), :][:, doc_row_ref.shape[1] - 1 :]
+    return jnp.sum(last - first) == 0.0
 
 
 def scatter_rows(ref, columns, value, mask, chunk=128):
@@ -187,37 +228,32 @@
         ref[pl.ds(start, chunk), columns] = value[at * chunk : (at + 1) * chunk]
 
 
-def cross_backward(swapped, place_ref, qm_ref, score_ref, att_ref, log_ref, doc_col_ref, doc_row_ref, pack_ref, *rest):
-    *datts, even_ref, odd_ref, dqm_ref, dinside_ref, dval_ref, chain_ref, dchain_ref, datt_ref = rest
+def cross_backward(swapped, place_ref, qm_ref, score_ref, att_ref, log_ref, doc_col_ref, doc_row_ref, far_ref, core_ref, *rest):
+    *datts, even_ref, odd_ref, dqm_ref, dinside_ref, dval_ref = rest[:-7]
+    pack_ref, sums_ref, chain_ref, dchain_ref, datt_ref, turned_ref, sems = rest[-7:]
+    bring((far_ref, core_ref), pack_ref, sems)
     length, dim = qm_ref.shape
     place = place_ref[0]
     chunk = datts[0].shape[0]
     for at, part in enumerate(datts):
         start = pl.multiple_of((place_ref[1] ^ at) * chunk, chunk)
         datt_ref[pl.ds(start, chunk), :] = part[...]
-    doc_col = doc_col_ref[:, 0:1]
     scale = dim**-0.5
     datt = datt_ref[...]
     log_total = log_ref[:, 0:1]
     delta = jnp.sum(datt.astype(WIDE) * att_ref[...], axis=1, keepdims=True)
     value = pack_ref[0, length : 2 * length, :]
-    probs = jnp.exp(score_ref[...] - log_total)
+    probs = jnp.exp2(score_ref[...] - log_total)
     dprob = mm(datt, value, tb=True)
     dinside_ref[...] = (probs * (dprob - delta) * scale).astype(LOW)
     dval_ref[...] = mm(probs, datt, ta=True)
     chain_ref[1] = qm_ref[...]
 
     def put(slot, rows, part):
-        @pl.when(slot < 4)
-        def to_even():
-            even_ref[slot, rows, :] = part.astype(LOW)
-
-        @pl.when(slot >= 4)
-        def to_odd():
-            odd_ref[slot - 4, rows, :] = part.astype(LOW)
+        sums_ref[slot, rows, :] = part.astype(LOW)
 
     def blank(at, carry):
-        put(slot_of(place ^ at, swapped), slice(None), jnp.zeros(even_ref.shape[1:], LOW))
+        put(slot_of(place ^ at, swapped), slice(None), jnp.zeros(sums_ref.shape[1:], LOW))
         return carry
 
     lax.fori_loop(place, SPAN, blank, 0)
@@ -230,17 +266,20 @@
         value = pack_ref[slot, length : 2 * length, :]
         through = pack_ref[slot, 2 * length :, :]
         chain_ref[step + 1] = mm(moved, through)
-        allowed = doc_col == doc_row_ref[pl.ds(at, 1), :]
-        score = jnp.where(allowed, mm(moved, key, tb=True) * scale, NEGATIVE)
-        probs = jnp.exp(score - log_total)
-        dprob = mm(datt, value, tb=True)
-        dscore = probs * (dprob - delta) * scale
-        dchain_ref[step] = mm(dscore, key)
-        put(slot, slice(0, length), mm(dscore, moved, ta=True))
+        allowed = doc_col_ref[:, 0:1] == doc_row_ref[pl.ds(at, 1), :]
+        probs = jnp.exp2(jnp.where(allowed, mm(moved * (LOG2E * scale), key, tb=True), NEGATIVE) - log_total)
+        dscore = (probs * (mm(datt, value, tb=True) - delta)).astype(LOW)
+        dchain_ref[step] = mm(dscore, key) * scale
+        put(slot, slice(0, length), mm(dscore, moved * scale, ta=True))
         put(slot, slice(length, 2 * length), mm(probs, datt, ta=True))
         return carry
 
-    lax.fori_loop(1, place + 1, hop, 0)
+    def two_hops(pair, carry):
+        hop(2 * pair + 1, carry)
+        return hop(2 * pair + 2, carry)
+
+    lax.fori_loop(0, place // 2, two_hops, 0)
+    lax.fori_loop(place // 2 * 2 + 1, place + 1, hop, 0)
 
     def back(count, carry):
         step = place - count
@@ -253,6 +292,8 @@
 
     dqm_ref[...] = jnp.zeros((length, dim), WIDE)
     lax.fori_loop(0, place, back, 0)
+    even_ref[...] = sums_ref[: SPAN // 2]
+    odd_ref[...] = sums_ref[SPAN // 2 :]
 
 
 def block_backward(
@@ -306,13 +347,37 @@
     scatter_rows(dbeta_ref, slice(None), jnp.where(lane == head, dbeta, 0.0).astype(LOW), mask)
 
 
-def prepare(heads, place_ref, tokens_ref, cot_ref, w_ref, mark_ref, *rest):
-    normed_ref, normed_t_ref, tokens_x_ref, cot_x_ref, gains_ref, beta_ref, docs_ref, doc_col_ref, marks_ref = rest
-    for slot in range(SPAN):
-        mask = 2 * (slot & 1) + 4 * ((slot >> 1) & 1) + (slot >> 2)
-        marks_ref[place_ref[0] ^ mask] = mark_ref[slot]
-    span = SPAN
-    small = w_ref[...]
+def pack_heads(heads, *refs):
+    *parts, out_ref = refs
+    dim = parts[0].shape[1] // heads
+    for head in range(heads):
+        for at, part in enumerate(parts):
+            start = (head * len(parts) + at) * dim
+            out_ref[:, start : start + dim] = part[:, head * dim : (head + 1) * dim]
+
+
+def prepare(heads, shard, masks, place_ref, tokens_ref, cot_ref, parts_ref, *rest):
+    normed_ref, normed_t_ref, tokens_x_ref, cot_x_ref, small_ref, gains_ref, beta_ref, docs_ref, doc_col_ref = rest[:9]
+    marks_ref, sems, mark_sems = rest[9:]
+    span = marks_ref.shape[0]
+    copies = []
+    for slot in range(parts_ref.shape[0]):
+        mask = sum(part for at, part in enumerate(masks) if slot >> at & 1)
+        at = pl.multiple_of((place_ref[2] ^ mask) * shard, 16)
+        copies.append(
+            pltpu.make_async_copy(parts_ref.at[slot, pl.ds(0, shard), :], small_ref.at[pl.ds(at, shard), :], sems.at[slot])
+        )
+        if mask < span:
+            copies.append(
+                pltpu.make_async_copy(
+                    parts_ref.at[slot, pl.ds(shard, 16), :], marks_ref.at[place_ref[0] ^ mask], mark_sems.at[mask]
+                )
+            )
+    for copy in copies:
+        copy.start()
+    for copy in copies:
+        copy.wait()
+    small = small_ref[...]
     across = small.astype(WIDE).T
     gains_ref[...] = across[0:8]
     gain = across[heads : heads + 1]
@@ -328,8 +393,12 @@
     for at in range(normed.shape[0] // 128):
         start = pl.multiple_of((mask ^ at) * 128, 128)
         normed_t_ref[:, pl.ds(start, 128)] = normed_wide[at * 128 : (at + 1) * 128].T.astype(LOW)
-    marks = jnp.sum(marks_ref[...].astype(WIDE), axis=1)
-    length = marks.shape[1]
+    all_marks = marks_ref[...].astype(WIDE)
+    line = iota(all_marks.shape, 1)
+    length = tokens_ref.shape[0]
+    marks = jnp.concatenate(
+        [jnp.sum(jnp.where(line == at, all_marks, 0.0), axis=1) for at in range(length // 128)], axis=1
+    )
     upper = jnp.where(iota((length, length), 0) <= iota((length, length), 1), 1.0, 0.0)
     docs = mm(marks, upper)
     row = iota(docs.shape, 0)
@@ -417,8 +486,8 @@
 
 
 def branch_backward(heads, inner, middle_ref, gains_ref, cot_ref, w_out_ref, *rest):
-    ways = (len(rest) - 3) // 2
-    backs, d_middle_ref, d_branch_ref, gain_ref, d_atts = rest[:ways], rest[ways], rest[ways + 1], rest[ways + 2], rest[ways + 3 :]
+    ways = (len(rest) - 4) // 2
+    backs, d_middle_ref, gain_ref, upper_ref, lower_ref, d_atts = rest[:ways], *rest[ways : ways + 4], rest[ways + 4 :]
     grad = total([part[...] for part in backs])
     middle = middle_ref[...]
     scale = lax.rsqrt(jnp.mean(middle * middle, axis=-1, keepdims=True) + EPSILON)
@@ -426,21 +495,22 @@
     d_middle = cot_ref[...].astype(WIDE) + norm_back(grad, middle, scale, gains_ref[heads + 1 : heads + 2])
     d_middle_ref[...] = d_middle
     d_branch = d_middle.astype(LOW)
-    d_branch_ref[...] = d_branch
+    half = upper_ref.shape[0]
+    upper_ref[...] = d_branch[:half]
+    lower_ref[...] = d_branch[half:]
     for at, part in enumerate(d_atts):
         part[...] = mm(d_branch, w_out_ref[:, at * inner : (at + 1) * inner]).astype(LOW)
 
 
-def project_back(heads, tokens_x_ref, w_ref, part_ref, d_proj_ref, *rest):
+def project_back(heads, tokens_x_ref, small_ref, w_ref, gain_two_ref, part_ref, d_proj_ref, *rest):
     d_betas, (gain_ref, d_beta_ref, *outs) = rest[:heads], rest[heads:]
-    cols = d_proj_ref.shape[1]
     d_beta = total([part[...] for part in d_betas]).astype(LOW)
     d_beta_ref[...] = d_beta
-    back = part_ref[...] + mm(d_beta, w_ref[:, heads * cols :], tb=True)
-    back = back + mm(d_proj_ref[...], w_ref[:, (heads - 1) * cols : heads * cols], tb=True)
+    back = part_ref[...] + mm(d_beta, small_ref[...], tb=True) + mm(d_proj_ref[...], w_ref[...], tb=True)
     stream = tokens_x_ref[...].astype(WIDE)
     scale = lax.rsqrt(jnp.mean(stream * stream, axis=-1, keepdims=True) + EPSILON)
-    gain_ref[...] = jnp.broadcast_to(jnp.sum(back * stream * scale, axis=0, keepdims=True), gain_ref.shape)
+    gain = jnp.sum(back * stream * scale, axis=0, keepdims=True)
+    gain_ref[...] = jnp.where(iota(gain_ref.shape, 0) == 0, gain, gain_two_ref[...])
     chunk = outs[0].shape[0]
     for at, part in enumerate(outs):
         part[...] = back[at * chunk : (at + 1) * chunk].astype(LOW)
@@ -466,15 +536,16 @@
     rest[-1][...] = mm(left_ref[...], d_proj_ref[...]).astype(LOW)
 
 
-def out_grads(heads, places_ref, branch_ref, *rest):
-    atts, out_ref, turned_ref = rest[:heads], rest[-2], rest[-1]
+def out_grads(heads, ways, *rest):
+    branches, atts, out_ref, turned_ref = rest[:ways], rest[ways : ways + heads], rest[-2], rest[-1]
     step = pl.program_id(0)
+    chunk = 2 * branches[0].shape[0]
 
     @pl.when(step == 0)
     def turn():
-        for at in range(branch_ref.shape[0] // 128):
-            start = pl.multiple_of((places_ref[1] ^ at) * 128, 128)
-            turned_ref[:, pl.ds(start, 128)] = branch_ref[at * 128 : (at + 1) * 128].astype(WIDE).T.astype(LOW)
+        for at in range(ways // 2):
+            part = jnp.concatenate([branches[2 * at][...], branches[2 * at + 1][...]], axis=0)
+            turned_ref[:, at * chunk : (at + 1) * chunk] = part.astype(WIDE).T.astype(LOW)
 
     for head in range(heads):
 
@@ -483,11 +554,12 @@
             out_ref[...] = mm(turned_ref[...], atts[head][...]).astype(LOW)
 
 
-def small_grads(heads, left_ref, d_beta_ref, gain_one_ref, gain_two_ref, *rest):
-    out_ref, rows_ref = rest[-2:]
+def small_grads(heads, ways, left_ref, d_beta_ref, *rest):
+    gains, out_ref, rows_ref = rest[:ways], rest[-2], rest[-1]
+    gain = total([part[...] for part in gains])
     rows_ref[...] = jnp.zeros_like(rows_ref)
-    rows_ref[heads : heads + 1, :] = gain_one_ref[0:1, :]
-    rows_ref[heads + 1 : heads + 2, :] = gain_two_ref[0:1, :]
+    rows_ref[heads : heads + 1, :] = gain[0:1]
+    rows_ref[heads + 1 : heads + 2, :] = gain[1:2]
     out_ref[...] = (mm(left_ref[...], d_beta_ref[...]) + rows_ref[...].T).astype(LOW)
 
 
@@ -564,32 +636,42 @@
 
 def run_cross_forward(places, q_moved, stats, acc, doc_col, docs, packs, swapped):
     length, dim = q_moved.shape
-    ins = (q_moved, stats, acc, doc_col, docs, packs)
+    ins = (q_moved, stats, acc, doc_col, docs)
     return run(
         functools.partial(cross_forward, swapped),
         "cross_forward",
-        (places, *ins),
-        [SCALARS, *whole(*ins)],
+        (places, *ins, *packs),
+        [SCALARS, *whole(*ins), ANYWHERE, ANYWHERE],
         [((length, dim), WIDE), ((length, dim), LOW), ((length, dim), WIDE)],
-        [pltpu.VMEM((length, dim), WIDE), pltpu.VMEM((2, length, 1), WIDE)],
+        [
+            pltpu.VMEM((SPAN,) + packs[0].shape[1:], LOW),
+            pltpu.VMEM((length, dim), WIDE),
+            pltpu.VMEM((SPAN - 1, length, length), WIDE),
+            pltpu.VMEM((length, 128), WIDE),
+            pltpu.SemaphoreType.DMA((2,)),
+        ],
         flops=10**10,
     )
 
 
 def run_cross_backward(places, q_moved, scores, attention, log_total, doc_col, docs, packs, d_atts, head, swapped):
     length, dim = q_moved.shape
-    half = ((SPAN // 2,) + packs.shape[1:], LOW)
-    ins = (q_moved, scores, attention, log_total, doc_col, docs, packs)
+    ins = (q_moved, scores, attention, log_total, doc_col, docs)
+    both = (SPAN,) + packs[0].shape[1:]
     return run(
         functools.partial(cross_backward, swapped),
         "cross_backward",
-        (places, *ins, *d_atts),
-        [SCALARS, *whole(*ins)] + [column_at((part.shape[0], dim), head) for part in d_atts],
-        [half, half, ((length, dim), WIDE), ((length, length), LOW), ((length, dim), WIDE)],
+        (places, *ins, *packs, *d_atts),
+        [SCALARS, *whole(*ins), ANYWHERE, ANYWHERE] + [column_at((part.shape[0], dim), head) for part in d_atts],
+        [(packs[0].shape, LOW)] * 2 + [((length, dim), WIDE), ((length, length), LOW), ((length, dim), WIDE)],
         [
+            pltpu.VMEM(both, LOW),
+            pltpu.VMEM(both, LOW),
             pltpu.VMEM((SPAN + 1, length, dim), WIDE),
             pltpu.VMEM((SPAN, length, dim), WIDE),
             pltpu.VMEM((length, dim), LOW),
+            pltpu.VMEM((length, length), WIDE),
+            pltpu.SemaphoreType.DMA((2,)),
         ],
         flops=10**10,
     )
@@ -640,36 +722,41 @@
     def over_heads(part):
         return to_heads([part] * ways)
 
-    parts = []
-    for head in range(heads):
-        cut = slice(head * dim, (head + 1) * dim)
-        parts += [w_query[:, cut], w_key[:, cut], w_value[:, cut], w_dir[:, cut]]
-    parts += [w_beta, gain_attn[:, None], gain_mlp[:, None], jnp.zeros((shard, 128 - heads - 2), LOW)]
-    w_in = lax.all_gather(jnp.concatenate(parts, axis=1), "seq", axis=0, tiled=True)
-    marks = doubled(jnp.pad(starts.astype(LOW)[None], ((0, 15), (0, 0))), (2, 4, 1))
+    small = jnp.concatenate([w_beta, gain_attn[:, None], gain_mlp[:, None]], axis=1)
+    small = jnp.pad(small, ((0, 0), (0, 128 - heads - 2)))
+    marks = jnp.pad(starts.astype(LOW).reshape(row_count // 128, 128), ((0, 16 - row_count // 128), (0, 0)))
+    masks = tuple(2 << at for at in range((count // 2).bit_length() - 1)) + (1,)
+    small = doubled(jnp.concatenate([small, marks], axis=0), masks)
+    four = (w_query, w_key, w_value, w_dir)
+    (packed,) = run(functools.partial(pack_heads, heads), "pack_heads", four, whole(*four), [((shard, 4 * inner), LOW)])
+    w_in = lax.all_gather(packed, "seq", axis=0, tiled=True)
     out_parts = jnp.concatenate(over_heads(w_out.T), axis=1)
-    w_in, marks, out_parts = lax.optimization_barrier((w_in, marks, out_parts))
-    w_out_x = lax.all_gather(out_parts, "seq", axis=0, tiled=True)
 
     tall, wide_tall, part_low = (row_count, width), (width, row_count), ((chunk, width), LOW)
-    small_at = heads * 4 * dim // 128
-    normed, normed_x_t, tokens_x, cot_x, gains, beta_raw, docs, doc_col = run(
-        functools.partial(prepare, heads),
+    normed, normed_x_t, tokens_x, cot_x, small_all, gains, beta_raw, docs, doc_col = run(
+        functools.partial(prepare, heads, shard, masks),
         "prepare",
-        (places, tokens, cotangent, w_in, marks),
-        [SCALARS, *whole(tokens, cotangent), column_at((width, 128), small_at), *whole(marks)],
+        (places, tokens, cotangent, small),
+        [SCALARS, *whole(tokens, cotangent), ANYWHERE],
         [
             (tall, LOW),
             (wide_tall, LOW),
             (tall, LOW),
             (tall, LOW),
+            ((width, 128), LOW),
             ((8, width), WIDE),
             ((row_count, 128), WIDE),
             ((SPAN, row_count), WIDE),
             ((row_count, 128), WIDE),
         ],
-        [pltpu.VMEM((SPAN, 16, row_count), LOW)],
-    )
+        [
+            pltpu.VMEM((SPAN, 16, 128), LOW),
+            pltpu.SemaphoreType.DMA((count,)),
+            pltpu.SemaphoreType.DMA((SPAN,)),
+        ],
+    )
+    normed, out_parts = lax.optimization_barrier((normed, out_parts))
+    w_out_x = lax.all_gather(after(out_parts, w_in), "seq", axis=0, tiled=True)
 
     orders = [(4, 2) if head % 2 else (2, 4) for head in range(heads)]
     first, mixed, ready, full = [], [], {}, {}
@@ -679,8 +766,8 @@
 
     def meet(outs, moves):
         outs, arrived = lax.optimization_barrier((outs, [move[2] for move in moves]))
-        for (head, unused, unused_too), part in zip(moves, arrived):
-            ready[head] = jnp.concatenate([ready[head], part], axis=0)
+        for (head, kind, unused), part in zip(moves, arrived):
+            ready[head] = (ready[head], part) if kind == 2 else jnp.concatenate([ready[head], part], axis=0)
         return outs
 
     flying = []
@@ -729,7 +816,7 @@
     )
     two_parts = over_heads(normed_two)
 
-    blocks = 4
+    blocks = 2
     cols = hidden_units // blocks
     all_three, *backs = pl.pallas_call(
         mlp_forward,
@@ -771,44 +858,52 @@
     grad_mlp, mlp_parts, backs = lax.optimization_barrier((grad_mlp, mlp_parts, backs))
     reduced_mlp = lax.psum_scatter(grad_mlp, "seq", scatter_dimension=0, tiled=True)
 
-    d_middle, d_branch, gain_two_sum, *d_atts = run(
+    d_middle, gain_two_sum, upper, lower, *d_atts = run(
         functools.partial(branch_backward, heads, inner),
         "branch_backward",
         (middle, gains, cot_x, w_out_x, *backs),
         [*whole(middle, gains), own_rows, *whole(w_out_x, *backs)],
-        [((chunk, width), WIDE), part_low, ((8, width), WIDE)] + [((chunk, inner), LOW)] * ways,
+        [((chunk, width), WIDE), ((8, width), WIDE)] + [((chunk // 2, width), LOW)] * 2 + [((chunk, inner), LOW)] * ways,
     )
     d_atts = to_heads(d_atts)
 
     def add(left, right):
         return (left.astype(WIDE) + right.astype(WIDE)).astype(LOW)
 
-    second, sums, mlp_terms = [], {}, [mlp_parts[0]]
+    second, low_sums, high_sums, last_sums, branch_parts = [], {}, {}, {}, [upper, lower]
     core, across = {}, {}
+    halves_two = [after(part, *d_atts[1:]) for part in (upper, lower)]
+    branch_moves = [(part, at) for at in range(1, ways) for part in halves_two]
+    shares = [2] + [1] * (2 * heads - 3)
+
+    def branch_next():
+        some = shares.pop(0) if shares else len(branch_moves)
+        out = [xor_move(part, "head", at) for part, at in branch_moves[:some]]
+        del branch_moves[:some]
+        return out
+
     for head in range(heads):
         kept = first[head]
         held = kept[2] if head == 0 else after(kept[2], second[-1][0])
-        flying = [move for move in (core.get(head - 1), across.get(head - 2)) if move is not None]
-        if head + 1 < ways:
-            flying.append(xor_move(mlp_parts[head + 1], "head", head + 1))
+        flying = (core.get(head - 1), across.get(head - 2), branch_next())
         outs = run_cross_backward(
             places, held, kept[3], mixed[head][0], mixed[head][2], doc_col, docs, packs[head], d_atts, head, head % 2 == 1
         )
-        (even, odd, *rest), flying = lax.optimization_barrier((outs, flying))
+        outs, (core_in, across_in, branch_in) = lax.optimization_barrier((outs, flying))
+        even, odd, *rest = outs
         second.append(rest)
-        if head + 1 < ways:
-            mlp_terms.append(flying.pop())
+        branch_parts += branch_in
         if head >= 2:
-            half = add(sums[head - 2][:2], flying.pop())
-            sums[head - 2] = [half[0], half[1]]
+            last_sums[head - 2] = [add(low_sums[head - 2][at], across_in[at]) for at in range(2)]
         if head >= 1:
-            sums[head - 1] = add(sums[head - 1], flying.pop())
-            across[head - 1] = xor_move(sums[head - 1][2:], "seq", orders[head - 1][1])
-        sums[head] = even
+            high_sums[head - 1] = add(low_sums[head - 1][2:], core_in[2:])
+            across[head - 1] = xor_move(high_sums[head - 1], "seq", orders[head - 1][1])
+            low_sums[head - 1] = add(low_sums[head - 1][:2], core_in[:2])
+        low_sums[head] = even
         core[head] = xor_move(odd, "seq", 1)
-    mlp_terms += [xor_move(mlp_parts[at], "head", at) for at in range(heads + 1, ways)]
-    result_own = total(mlp_terms).astype(LOW)
-    d_branch_all = lax.all_gather(after(d_branch, reduced_mlp), "head", axis=0, tiled=True)
+    mlp_rows = jnp.stack(mlp_parts)
+    mlp_rows = jnp.concatenate([lax.dynamic_index_in_dim(mlp_rows, head_place ^ at, 0, False) for at in range(ways)])
+    result = lax.psum(after(mlp_rows, reduced_mlp, second[-1][0]), "head")
 
     cols = 4 * dim
     grad_in = None
@@ -828,14 +923,12 @@
             name=name,
         )(*ins, *given)
 
-    d_projs, d_betas, result_parts = [], [], [result_own]
+    d_projs, d_betas = [], []
     back_part = None
     for head in range(heads):
-        if isinstance(sums[head], list):
-            near_sum, far_sum = sums[head]
-        else:
-            half = add(sums[head][:2], across[head])
-            near_sum, far_sum = half[0], half[1]
+        if head not in last_sums:
+            last_sums[head] = [add(low_sums[head][at], across[head][at]) for at in range(2)]
+        near_sum, far_sum = last_sums[head]
         sent = [near_sum, xor_move(far_sum, "seq", orders[head][0])]
         if head >= 1:
             grad_in = grads_into(
@@ -854,46 +947,45 @@
                 [*whole(d_projs[-1]), column_at((width, cols), head - 1), *whole(*ins[2:])],
                 [(tall, WIDE)],
             )
+            if head == heads - 1:
+                atts = [part[1] for part in mixed]
+                grad_in = grads_into(
+                    functools.partial(out_grads, heads, len(branch_parts)),
+                    (*branch_parts, *atts),
+                    whole(*branch_parts, *atts),
+                    pl.BlockSpec((width, 128), lambda step: (0, heads * cols // 128 + 1 + step)),
+                    heads,
+                    "out_grads",
+                    [pltpu.VMEM(wide_tall, LOW)],
+                )
             grad_in, back_part, sent = lax.optimization_barrier((grad_in, back_part, sent))
-        flying = []
-        if head + 1 < ways:
-            flying.append(xor_move(result_own, "head", head + 1))
-        if head + 1 in across:
-            flying.append(across[head + 1])
         late = heads - 1 if head == 0 and heads - 1 not in across else None
-        if late:
-            flying.append(core[late])
+        flying = (across.get(head + 1), core[late] if late else None, branch_next() if head + 1 < heads else [])
         proj, inverse, carried, qdir, solve = (first[head][at] for at in (0, 4, 5, 6, 7))
+        if head == 0:
+            proj, reduced_mlp = lax.optimization_barrier((proj, reduced_mlp))
         outs = run_block_backward(
             places, proj, beta_raw, (inverse, carried, qdir, solve, *second[head]), sent, head, dim
         )
-        (d_proj, d_beta), flying = lax.optimization_barrier((outs, flying))
+        (d_proj, d_beta), (across_in, core_in, branch_in) = lax.optimization_barrier((outs, flying))
+        branch_parts += branch_in
+        if across_in is not None:
+            across[head + 1] = across_in
         if late:
-            sums[late] = add(sums[late], flying.pop())
-            across[late] = xor_move(sums[late][2:], "seq", orders[late][1])
-        if head + 1 in across and head + 1 != late:
-            across[head + 1] = flying.pop()
-        if head + 1 < ways:
-            result_parts.append(flying.pop())
+            across[late] = xor_move(add(low_sums[late][2:], core_in[2:]), "seq", orders[late][1])
+            low_sums[late] = add(low_sums[late][:2], core_in[:2])
         d_projs.append(d_proj)
         d_betas.append(d_beta)
-    result_parts += [xor_move(result_own, "head", at) for at in range(heads + 1, ways)]
-    atts = [part[1] for part in mixed]
-    grad_in = grads_into(
-        functools.partial(out_grads, heads),
-        (places, d_branch_all, *atts),
-        [SCALARS, *whole(d_branch_all, *atts)],
-        pl.BlockSpec((width, 128), lambda step: (0, heads * cols // 128 + 1 + step)),
-        heads,
-        "out_grads",
-        [pltpu.VMEM(wide_tall, LOW)],
-    )
-    back_ins = (tokens_x, w_in, back_part, d_projs[-1], *d_betas)
-    gain_one_sum, d_beta, *backs = run(
+    back_ins = (tokens_x, small_all, w_in, gain_two_sum, back_part, d_projs[-1], *d_betas)
+    gain_sums, d_beta, *backs = run(
         functools.partial(project_back, heads),
         "project_back",
         back_ins,
-        whole(*back_ins),
+        [
+            *whole(tokens_x, small_all),
+            column_at((width, cols), heads - 1),
+            *whole(*back_ins[3:]),
+        ],
         [((8, width), WIDE), ((row_count, 128), LOW)] + [part_low] * ways,
     )
     backs = to_heads(backs)
@@ -905,13 +997,6 @@
         [part_low],
     )
     token_parts = over_heads(d_tokens_own)
-    (result,) = run(
-        token_join, "result_join", (places, *result_parts), [SCALARS, *whole(*result_parts)], [(tall, LOW)]
-    )
-    (d_tokens,) = run(
-        token_join, "token_join", (places, *token_parts), [SCALARS, *whole(*token_parts)], [(tall, WIDE)]
-    )
-
     grad_in = grads_into(
         weight_grads,
         (normed_x_t, d_projs[-1]),
@@ -920,9 +1005,10 @@
         1,
         "weight_grads",
     )
-    ins = (normed_x_t, d_beta, gain_one_sum, gain_two_sum)
+    gain_parts = over_heads(gain_sums)
+    ins = (normed_x_t, d_beta, *gain_parts)
     grad_in = grads_into(
-        functools.partial(small_grads, heads),
+        functools.partial(small_grads, heads, ways),
         ins,
         whole(*ins),
         column_at((width, 128), heads * cols // 128),
@@ -930,6 +1016,7 @@
         "small_grads",
         [pltpu.VMEM((128, width), WIDE)],
     )
+    grad_in, result = lax.optimization_barrier((grad_in, result))
     reduced_in = lax.psum_scatter(grad_in, "seq", scatter_dimension=0, tiled=True)
     *grads, small_sum, grad_out_t = run(
         functools.partial(grad_join, heads, dim),
@@ -938,16 +1025,18 @@
         whole(reduced_in),
         [((shard, inner), WIDE)] * 4 + [((shard, 128), WIDE), ((shard, inner), WIDE)],
     )
-    gain_sums = total(over_heads(small_sum))
+    (d_tokens,) = run(
+        token_join, "token_join", (places, *token_parts), [SCALARS, *whole(*token_parts)], [(tall, WIDE)]
+    )
     reduced_mlp = reduced_mlp.astype(WIDE)
     return (
         result,
         d_tokens,
-        gain_sums[:, heads],
+        small_sum[:, heads],
         *grads,
         small_sum[:, :heads],
         grad_out_t.T,
-        gain_sums[:, heads + 1],
+        small_sum[:, heads + 1],
         reduced_mlp[:, :hidden_units],
         reduced_mlp[:, hidden_units : 2 * hidden_units],
         reduced_mlp[:, 2 * hidden_units :].T,

time: 591 us -> 551 us (0.932)
  starting transfers between devices: 104 us -> 85.6 us
  local copies, waits for them, and re-layouts: 25.4 us -> 19.3 us
  waiting for transfers between devices: 233 us -> 227 us
    ppermute x51, starting transfers between devices: 103 us -> 85.2 us  [xor_move(): lax.ppermute(value, axis, [(at, at ^ mask) for at in range(lax.axis_size(...]
    ppermute x51, waiting for transfers between devices: 209 us -> 193 us  [xor_move(): lax.ppermute(value, axis, [(at, at ^ mask) for at in range(lax.axis_size(...]
    psum x0 -> x1, waiting for transfers between devices: none -> 12 us  [per_device(): result = lax.psum(after(mlp_rows, reduced_mlp, second[-1][0]), 'head')]
    all_gather x3 -> x2, waiting for transfers between devices: 24.5 us -> 14.5 us  [the longest x1 14.5 us: per_device(): w_in = lax.all_gather(packed, 'seq', axis=0, tiled=True)]
    reduce_scatter x1, waiting for transfers between devices: 0.01 us -> 8.18 us  [per_device(): lax.psum_scatter(grad_mlp, 'seq', scatter_dimension=0, tiled=True)]
    concatenate x9 -> x8, other arithmetic: 7.73 us -> 1.78 us  [the longest x1 1.25 us: per_device(): jnp.concatenate([lax.dynamic_index_in_dim(mlp_rows, head_place ^ at, 0, F...]
    unnamed x106 -> x118, local copies, waits for them, and re-layouts: 14 us -> 14.2 us
  transfers between devices with their start and end apart: 57 -> 57, of which waited for: 31 -> 29; matrix products, arithmetic and copies ran while one was open for 4% -> 3% of each run, Pallas kernels for 26% -> 30%
where the time goes in v3:
time: 551 us; the launch traced here: 545 us
  waiting for transfers between devices  227 us (41%)
  Pallas kernels  184 us (33%)
  starting transfers between devices  85.6 us (16%)
  local copies, waits for them, and re-layouts  19.3 us (4%)
  between operations  15 us (3%)
  other arithmetic  12.9 us (2%)
    ppermute x51, waiting for transfers between devices, xor_move(): lax.ppermute(value, axis, [(at, at ^ mask) for at in range(lax.axis_size(...  193 us
    pallas_call x22, Pallas kernels, run(): pl.pallas_call(kernel, grid=(1,), in_specs=specs, out_specs=[fixed(shape)...  136 us
    ppermute x51, starting transfers between devices, xor_move(): lax.ppermute(value, axis, [(at, at ^ mask) for at in range(lax.axis_size(...  85.2 us
    pallas_call x5, Pallas kernels, grads_into(): pl.pallas_call(kernel, grid=(grid,), in_specs=specs + [ANYWHERE] * len(gi...  18.8 us
    pallas_call x1, Pallas kernels, per_device(): pl.pallas_call(mlp_forward, grid=(blocks,), in_specs=[fixed(tall), pl.Blo...  14.8 us
    pallas_call x1, Pallas kernels, per_device(): pl.pallas_call(mlp_grads, grid=(3 * blocks,), in_specs=[fixed(tall), pl.B...  14.8 us
    all_gather x1, waiting for transfers between devices, per_device(): w_in = lax.all_gather(packed, 'seq', axis=0, tiled=True)  14.5 us
    unnamed x118, local copies, waits for them, and re-layouts  14.2 us
  transfers between devices with their start and end apart: 57, of which 29 were waited for; matrix products, arithmetic and copies ran while one was open for 3% of the time, Pallas kernels for 30%

profile of v3, /device:TPU:0, one launch (start us, length us, event | category | flops | bytes accessed | tf_op | source)
XLA Modules:
  0.0 544.5 jit_solution(15529831039320354317)
XLA Ops:
  30.2 7.6 %prepare.1 = (bf16[512,1536]{1,0:T(8,128)(2,1)}, bf16[1536,512]{1,0:T(8,128)(2,1)}, bf16[512,1536]{1,0:T(8,128)(2,1)}, bf16[512,1536]{1,0:T(8,128)(2,1)}, bf16[1...) custom-call(s32[3]{0:T(128)} %pad_add_fusion.place_ref, ...), custom_call_target="tpu_custom_call" | custom-call | flops 1000000000 | bytes 4194304 | tf_op jit(solution)/shard_map/prepare/pallas_call | solution.py:596
  37.7 14.5 %all-gather.4.cloned.1.call-done.w_ref = bf16[1536,1536]{1,0:T(8,128)(2,1)} async-done(((bf16[192,1536]{1,0:T(8,128)(2,1)}), bf16[1536,1536]{1,0:T(8,128)(2,1)}) %all-gather.4.cloned.1.call-update) | async-done | bytes 4718608 | tf_op jit(solution)/shard_map/all_gather | solution.py:732
  52.5 12.1 %block_forward.3 = (f32[512,512]{1,0:T(8,128)}, bf16[1152,128]{1,0:T(8,128)(2,1)}, f32[512,128]{1,0:T(8,128)}, f32[512,512]{1,0:T(8,128)}, bf16[512,512]{1,0:T(8...) custom-call(s32[3]{0:T(128)} %pad_add_fusion.place_ref, ...), custom_call_target="tpu_custom_call" | custom-call | flops 10000000000 | bytes 4194304 | tf_op jit(solution)/shard_map/block_forward/pallas_call | solution.py:596
  66.1 12.5 %block_forward.4 = (f32[512,512]{1,0:T(8,128)}, bf16[1152,128]{1,0:T(8,128)(2,1)}, f32[512,128]{1,0:T(8,128)}, f32[512,512]{1,0:T(8,128)}, bf16[512,512]{1,0:T(8...) custom-call(s32[3]{0:T(128)} %pad_add_fusion.place_ref, ...), custom_call_target="tpu_custom_call" | custom-call | flops 10000000000 | bytes 4194304 | tf_op jit(solution)/shard_map/block_forward/pallas_call | solution.py:596
  80.8 12.1 %block_forward.5 = (f32[512,512]{1,0:T(8,128)}, bf16[1152,128]{1,0:T(8,128)(2,1)}, f32[512,128]{1,0:T(8,128)}, f32[512,512]{1,0:T(8,128)}, bf16[512,512]{1,0:T(8...) custom-call(s32[3]{0:T(128)} %pad_add_fusion.place_ref, ...), custom_call_target="tpu_custom_call" | custom-call | flops 10000000000 | bytes 4194304 | tf_op jit(solution)/shard_map/block_forward/pallas_call | solution.py:596
  94.7 18.3 %collective-permute-done.8 = bf16[2,1152,128]{2,1,0:T(8,128)(2,1)S(1)} collective-permute-done((bf16[2,1152,128]{2,1,0:T(8,128)(2,1)S(1)}, bf16[2,1152,128]{2,1,0:T(8,128)(2,1)S(1)}, u32[]{:S(2)}, u32[]{:S(2)}) %collective-permute-start.8) | collective-permute-done | bytes 589856 | tf_op jit(solution)/shard_map/ppermute | solution.py:81
  125.7 10.7 %collective-permute-done.11 = bf16[2,1152,128]{2,1,0:T(8,128)(2,1)S(1)} collective-permute-done((bf16[2,1152,128]{2,1,0:T(8,128)(2,1)S(1)}, bf16[2,1152,128]{2,1,0:T(8,128)(2,1)S(1)}, u32[]{:S(2)}, u32[]{:S(2)}) %collective-permute-start.11) | collective-permute-done | bytes 589856 | tf_op jit(solution)/shard_map/ppermute | solution.py:81
  144.2 13.5 %collective-permute-done.13 = bf16[2,1152,128]{2,1,0:T(8,128)(2,1)S(1)} collective-permute-done((bf16[2,1152,128]{2,1,0:T(8,128)(2,1)S(1)}, bf16[2,1152,128]{2,1,0:T(8,128)(2,1)S(1)}, u32[]{:S(2)}, u32[]{:S(2)}) %collective-permute-start.13) | collective-permute-done | bytes 589856 | tf_op jit(solution)/shard_map/ppermute | solution.py:81
  190.8 14.5 %collective-permute-done.18.rest_1_ = bf16[128,1536]{1,0:T(8,128)(2,1)S(1)} collective-permute-done((bf16[128,1536]{1,0:T(8,128)(2,1)}, bf16[128,1536]{1,0:T(8,128)(2,1)S(1)}, u32[]{:S(2)}, u32[]{:S(2)}) %collective-permute-start.18) | collective-permute-done | bytes 393248 | tf_op jit(solution)/shard_map/ppermute | solution.py:81
  205.3 13.1 %collective-permute-done.19.rest_2_ = bf16[128,1536]{1,0:T(8,128)(2,1)S(1)} collective-permute-done((bf16[128,1536]{1,0:T(8,128)(2,1)}, bf16[128,1536]{1,0:T(8,128)(2,1)S(1)}, u32[]{:S(2)}, u32[]{:S(2)}) %collective-permute-start.19) | collective-permute-done | bytes 393248 | tf_op jit(solution)/shard_map/ppermute | solution.py:81
  219.3 14.8 %mlp_forward.1 = (bf16[3,512,1024]{2,1,0:T(8,128)(2,1)}, bf16[128,1536]{1,0:T(8,128)(2,1)}, bf16[128,1536]{1,0:T(8,128)(2,1)}, bf16[128,1536]{1,0:T(8,128)(2,1)}, bf16[128,1536]{1,0:T(8,128)(2,1)}) custom-call(bf16[512,1536]{1,0:T(8,128)(2,1)} %get-tuple-element.276.cot_ref, bf16[1536,3072]{1,0:T(8,128)(2,1)} %all-gather.8.cloned.1.call-done.gate_ref.up_ref.down_ref, ...), custom_call_target="tpu_custom_call" | custom-call | flops 10000000000 | bytes 16777216 | tf_op jit(solution)/shard_map/mlp_forward/pallas_call | solution.py:821
  234.1 7.4 %collective-permute-start.21 = (bf16[128,1536]{1,0:T(8,128)(2,1)}, bf16[128,1536]{1,0:T(8,128)(2,1)S(1)}, u32[]{:S(2)}, u32[]{:S(2)}) collective-permute-start(bf16[128,1536]{1,0:T(8,128)(2,1)} %get-tuple-element.286), channel_id=1, source_target_pairs={{0,8},{8,0},{16,24},{24,16},{1,9},{9,1},{17,25},{25,17},{2,10},{10... | collective-permute-start | bytes 1179656 | tf_op jit(solution)/shard_map/ppermute | solution.py:81
  244.0 14.8 %mlp_grads.1 = (bf16[1536,3072]{1,0:T(8,128)(2,1)}, bf16[128,1536]{1,0:T(8,128)(2,1)}, bf16[128,1536]{1,0:T(8,128)(2,1)}, bf16[128,1536]{1,0:T(8,128)(2,1)}, bf16[128,1536]{1,0:T(8,128)(2,1)}) custom-call(bf16[512,1536]{1,0:T(8,128)(2,1)} %get-tuple-element.276.cot_ref, bf16[3,512,1024]{2,1,0:T(8,128)(2,1)} %get-tuple-element.279.all_ref, ...), custom_call_target="tpu_custom_call" | custom-call | flops 10000000000 | bytes 16777216 | tf_op jit(solution)/shard_map/mlp_grads/pallas_call | solution.py:840
  258.8 12.7 %collective-permute-done.22.rest_2_ = bf16[128,1536]{1,0:T(8,128)(2,1)S(1)} collective-permute-done((bf16[128,1536]{1,0:T(8,128)(2,1)}, bf16[128,1536]{1,0:T(8,128)(2,1)S(1)}, u32[]{:S(2)}, u32[]{:S(2)}) %collective-permute-start.22) | collective-permute-done | bytes 393248 | tf_op jit(solution)/shard_map/ppermute | solution.py:81
  311.1 8.1 %collective-permute-done.30.rest_4_ = bf16[64,1536]{1,0:T(8,128)(2,1)S(1)} collective-permute-done((bf16[64,1536]{1,0:T(8,128)(2,1)S(1)}, bf16[64,1536]{1,0:T(8,128)(2,1)S(1)}, u32[]{:S(2)}, u32[]{:S(2)}) %collective-permute-start.30) | collective-permute-done | bytes 196640 | tf_op jit(solution)/shard_map/ppermute | solution.py:81
  334.9 10.3 %collective-permute-done.32 = bf16[2,1152,128]{2,1,0:T(8,128)(2,1)S(1)} collective-permute-done((bf16[2,1152,128]{2,1,0:T(8,128)(2,1)S(1)}, bf16[2,1152,128]{2,1,0:T(8,128)(2,1)S(1)}, u32[]{:S(2)}, u32[]{:S(2)}) %collective-permute-start.32) | collective-permute-done | bytes 589856 | tf_op jit(solution)/shard_map/ppermute | solution.py:81
  356.8 8.2 %reduce-scatter.3.cloned.1.call-done = bf16[192,3072]{1,0:T(8,128)(2,1)} async-done(((bf16[1536,3072]{1,0:T(8,128)(2,1)}), bf16[192,3072]{1,0:T(8,128)(2,1)}) %reduce-scatter.3.cloned.1.call-update) | async-done | bytes 1179664 | tf_op jit(solution)/shard_map/reduce_scatter | solution.py:859
  413.5 7.4 %block_backward.5 = (bf16[512,512]{1,0:T(8,128)(2,1)}, bf16[512,128]{1,0:T(8,128)(2,1)}) custom-call(s32[3]{0:T(128)} %pad_add_fusion.place_ref, f32[512,512]{1,0:T(8,128)} %get-tuple-element.373.proj_ref, f32[512,128]{1,0:T(8,128)} %get-tuple-element.219.beta_ref, bf16[512,512]{1,0:T(8,128)(2,1)} %get-tuple-element.374.inv_ref, ...), custom_call_target="tpu_custom_call" | custom-call | flops 5000000000 | bytes 4194304 | tf_op jit(solution)/shard_map/block_backward/pallas_call | solution.py:596
  442.0 12.0 %all-reduce.4.cloned.1.call-done = bf16[512,1536]{1,0:T(8,128)(2,1)} async-done(((bf16[512,1536]{1,0:T(8,128)(2,1)}), bf16[512,1536]{1,0:T(8,128)(2,1)}) %all-reduce.4.cloned.1.call-update) | async-done | bytes 1572880 | tf_op jit(solution)/shard_map/psum | solution.py:906
  458.5 13.6 %collective-permute-done.45.rest_1_ = bf16[128,1536]{1,0:T(8,128)(2,1)S(1)} collective-permute-done((bf16[128,1536]{1,0:T(8,128)(2,1)S(1)}, bf16[128,1536]{1,0:T(8,128)(2,1)S(1)}, u32[]{:S(2)}, u32[]{:S(2)}) %collective-permute-start.45) | collective-permute-done | bytes 393248 | tf_op jit(solution)/shard_map/ppermute | solution.py:81
  472.1 11.9 %collective-permute-done.46.rest_2_ = bf16[128,1536]{1,0:T(8,128)(2,1)S(1)} collective-permute-done((bf16[128,1536]{1,0:T(8,128)(2,1)S(1)}, bf16[128,1536]{1,0:T(8,128)(2,1)S(1)}, u32[]{:S(2)}, u32[]{:S(2)}) %collective-permute-start.46) | collective-permute-done | bytes 393248 | tf_op jit(solution)/shard_map/ppermute | solution.py:81
  488.1 7.7 %collective-permute-start.48 = (bf16[128,1536]{1,0:T(8,128)(2,1)}, bf16[128,1536]{1,0:T(8,128)(2,1)S(1)}, u32[]{:S(2)}, u32[]{:S(2)}) collective-permute-start(bf16[128,1536]{1,0:T(8,128)(2,1)} %token_grad.1.rest_0_), channel_id=1, source_target_pairs={{0,8},{8,0},{16,24},{24,16},{1,9},{9,1},{17,25},{25,17},{2,10},{10... | collective-permute-start | bytes 1179656 | tf_op jit(solution)/shard_map/ppermute | solution.py:81
  499.9 10.9 %collective-permute-done.48.rest_1_ = bf16[128,1536]{1,0:T(8,128)(2,1)S(1)} collective-permute-done((bf16[128,1536]{1,0:T(8,128)(2,1)}, bf16[128,1536]{1,0:T(8,128)(2,1)S(1)}, u32[]{:S(2)}, u32[]{:S(2)}) %collective-permute-start.48) | collective-permute-done | bytes 393248 | tf_op jit(solution)/shard_map/ppermute | solution.py:81
  510.8 15.0 %collective-permute-done.49.rest_2_ = bf16[128,1536]{1,0:T(8,128)(2,1)S(1)} collective-permute-done((bf16[128,1536]{1,0:T(8,128)(2,1)}, bf16[128,1536]{1,0:T(8,128)(2,1)S(1)}, u32[]{:S(2)}, u32[]{:S(2)}) %collective-permute-start.49) | collective-permute-done | bytes 393248 | tf_op jit(solution)/shard_map/ppermute | solution.py:81
  (275 shorter events, 246.0 us)
Async XLA Ops:
  7.2 45.0 %all-gather.4.cloned.1.call-start = ((), (), s32[]{:S(2)}) async-start(), calls=%async_computation.2 | async-start | bytes 5308416 | tf_op jit(solution)/shard_map/all_gather | solution.py:732
  9.4 127.0 %all-gather.6.cloned.1.call-start = ((), (), s32[]{:S(2)}) async-start(), calls=%async_computation.3 | async-start | bytes 5308416 | tf_op jit(solution)/shard_map/all_gather | solution.py:759
  52.2 166.2 %all-gather.8.cloned.1.call-start = ((), (), s32[]{:S(2)}) async-start(), calls=%async_computation.4 | async-start | bytes 10616832 | tf_op jit(solution)/shard_map/all_gather | solution.py:803
  79.2 33.8 %collective-permute-start.8 = (bf16[2,1152,128]{2,1,0:T(8,128)(2,1)S(1)}, bf16[2,1152,128]{2,1,0:T(8,128)(2,1)S(1)}, u32[]{:S(2)}, u32[]{:S(2)}) collective-permute-start(bf16[2,1152,128]{2,1,0:T(8,128)(2,1)S(1)} %pad_maximum_fusion.7), channel_id=1, source_target_pairs={{0,4},{1,5},{2,6},{3,7},{4,0},{5,1},{6,2},{7,3},{8,12},{9,13},{10,... | collective-permute-start | bytes 1769480 | tf_op jit(solution)/shard_map/ppermute | solution.py:81
  136.4 228.6 %reduce-scatter.3.cloned.1.call-start = ((), (), s32[]{:S(2)}) async-start(), calls=%async_computation.5 | async-start | bytes 10616832 | tf_op jit(solution)/shard_map/reduce_scatter | solution.py:859
  136.7 21.0 %collective-permute-start.13 = (bf16[2,1152,128]{2,1,0:T(8,128)(2,1)S(1)}, bf16[2,1152,128]{2,1,0:T(8,128)(2,1)S(1)}, u32[]{:S(2)}, u32[]{:S(2)}) collective-permute-start(bf16[2,1152,128]{2,1,0:T(8,128)(2,1)S(1)} %pad_maximum_fusion.9), channel_id=1, source_target_pairs={{0,4},{1,5},{2,6},{3,7},{4,0},{5,1},{6,2},{7,3},{8,12},{9,13},{10,... | collective-permute-start | bytes 1769480 | tf_op jit(solution)/shard_map/ppermute | solution.py:81
  188.4 30.0 %collective-permute-start.19 = (bf16[128,1536]{1,0:T(8,128)(2,1)}, bf16[128,1536]{1,0:T(8,128)(2,1)S(1)}, u32[]{:S(2)}, u32[]{:S(2)}) collective-permute-start(bf16[128,1536]{1,0:T(8,128)(2,1)} %get-tuple-element.278.rest_0_), channel_id=1, source_target_pairs={{0,16},{8,24},{16,0},{24,8},{1,17},{9,25},{17,1},{25,9},{2,18},{10... | collective-permute-start | bytes 1179656 | tf_op jit(solution)/shard_map/ppermute | solution.py:81
  189.3 29.1 %collective-permute-start.20 = (bf16[128,1536]{1,0:T(8,128)(2,1)}, bf16[128,1536]{1,0:T(8,128)(2,1)S(1)}, u32[]{:S(2)}, u32[]{:S(2)}) collective-permute-start(bf16[128,1536]{1,0:T(8,128)(2,1)} %get-tuple-element.278.rest_0_), channel_id=1, source_target_pairs={{0,24},{8,16},{16,8},{24,0},{1,25},{9,17},{17,9},{25,1},{2,26},{10... | collective-permute-start | bytes 1179656 | tf_op jit(solution)/shard_map/ppermute | solution.py:81
  234.1 24.7 %collective-permute-start.21 = (bf16[128,1536]{1,0:T(8,128)(2,1)}, bf16[128,1536]{1,0:T(8,128)(2,1)S(1)}, u32[]{:S(2)}, u32[]{:S(2)}) collective-permute-start(bf16[128,1536]{1,0:T(8,128)(2,1)} %get-tuple-element.286), channel_id=1, source_target_pairs={{0,8},{8,0},{16,24},{24,16},{1,9},{9,1},{17,25},{25,17},{2,10},{10... | collective-permute-start | bytes 1179656 | tf_op jit(solution)/shard_map/ppermute | solution.py:81
  241.5 30.0 %collective-permute-start.22 = (bf16[128,1536]{1,0:T(8,128)(2,1)}, bf16[128,1536]{1,0:T(8,128)(2,1)S(1)}, u32[]{:S(2)}, u32[]{:S(2)}) collective-permute-start(bf16[128,1536]{1,0:T(8,128)(2,1)} %get-tuple-element.287), channel_id=1, source_target_pairs={{0,16},{8,24},{16,0},{24,8},{1,17},{9,25},{17,1},{25,9},{2,18},{10... | collective-permute-start | bytes 1179656 | tf_op jit(solution)/shard_map/ppermute | solution.py:81
  242.6 28.9 %collective-permute-start.23 = (bf16[128,1536]{1,0:T(8,128)(2,1)}, bf16[128,1536]{1,0:T(8,128)(2,1)S(1)}, u32[]{:S(2)}, u32[]{:S(2)}) collective-permute-start(bf16[128,1536]{1,0:T(8,128)(2,1)} %get-tuple-element.288), channel_id=1, source_target_pairs={{0,24},{8,16},{16,8},{24,0},{1,25},{9,17},{17,9},{25,1},{2,26},{10... | collective-permute-start | bytes 1179656 | tf_op jit(solution)/shard_map/ppermute | solution.py:81
  272.5 181.5 %all-reduce.4.cloned.1.call-start = ((), (), s32[]{:S(2)}) async-start(), calls=%async_computation.6 | async-start | bytes 3145728 | tf_op jit(solution)/shard_map/psum | solution.py:906
  305.1 29.9 %collective-permute-start.33 = (bf16[64,1536]{1,0:T(8,128)(2,1)}, bf16[64,1536]{1,0:T(8,128)(2,1)}, u32[]{:S(2)}, u32[]{:S(2)}) collective-permute-start(bf16[64,1536]{1,0:T(8,128)(2,1)} %get-tuple-element.308.rest_1_), channel_id=1, source_target_pairs={{0,16},{8,24},{16,0},{24,8},{1,17},{9,25},{17,1},{25,9},{2,18},{10... | collective-permute-start | bytes 589832 | tf_op jit(solution)/shard_map/ppermute | solution.py:81
  319.9 25.4 %collective-permute-start.31 = (bf16[4,1152,128]{2,1,0:T(8,128)(2,1)}, bf16[4,1152,128]{2,1,0:T(8,128)(2,1)}, u32[]{:S(2)}, u32[]{:S(2)}) collective-permute-start(bf16[4,1152,128]{2,1,0:T(8,128)(2,1)} %get-tuple-element.332), channel_id=1, source_target_pairs={{0,1},{1,0},{2,3},{3,2},{4,5},{5,4},{6,7},{7,6},{8,9},{9,8},{10,11... | collective-permute-start | bytes 3538952 | tf_op jit(solution)/shard_map/ppermute | solution.py:81
  321.4 23.8 %collective-permute-start.32 = (bf16[2,1152,128]{2,1,0:T(8,128)(2,1)S(1)}, bf16[2,1152,128]{2,1,0:T(8,128)(2,1)S(1)}, u32[]{:S(2)}, u32[]{:S(2)}) collective-permute-start(bf16[2,1152,128]{2,1,0:T(8,128)(2,1)S(1)} %get-tuple-element.455), channel_id=1, source_target_pairs={{0,4},{1,5},{2,6},{3,7},{4,0},{5,1},{6,2},{7,3},{8,12},{9,13},{10,... | collective-permute-start | bytes 1769480 | tf_op jit(solution)/shard_map/ppermute | solution.py:81
  350.1 25.8 %collective-permute-start.36 = (bf16[4,1152,128]{2,1,0:T(8,128)(2,1)}, bf16[4,1152,128]{2,1,0:T(8,128)(2,1)}, u32[]{:S(2)}, u32[]{:S(2)}) collective-permute-start(bf16[4,1152,128]{2,1,0:T(8,128)(2,1)} %get-tuple-element.350), channel_id=1, source_target_pairs={{0,1},{1,0},{2,3},{3,2},{4,5},{5,4},{6,7},{7,6},{8,9},{9,8},{10,11... | collective-permute-start | bytes 3538952 | tf_op jit(solution)/shard_map/ppermute | solution.py:81
  351.7 24.2 %collective-permute-start.35 = (bf16[2,1152,128]{2,1,0:T(8,128)(2,1)S(1)}, bf16[2,1152,128]{2,1,0:T(8,128)(2,1)S(1)}, u32[]{:S(2)}, u32[]{:S(2)}) collective-permute-start(bf16[2,1152,128]{2,1,0:T(8,128)(2,1)S(1)} %get-tuple-element.453), channel_id=1, source_target_pairs={{0,2},{1,3},{2,0},{3,1},{4,6},{5,7},{6,4},{7,5},{8,10},{9,11},{10,... | collective-permute-start | bytes 1769480 | tf_op jit(solution)/shard_map/ppermute | solution.py:81
  354.4 42.2 %collective-permute-start.40 = (bf16[64,1536]{1,0:T(8,128)(2,1)}, bf16[64,1536]{1,0:T(8,128)(2,1)}, u32[]{:S(2)}, u32[]{:S(2)}) collective-permute-start(bf16[64,1536]{1,0:T(8,128)(2,1)} %get-tuple-element.308.rest_1_), channel_id=1, source_target_pairs={{0,24},{8,16},{16,8},{24,0},{1,25},{9,17},{17,9},{25,1},{2,26},{10... | collective-permute-start | bytes 589832 | tf_op jit(solution)/shard_map/ppermute | solution.py:81
  380.4 150.1 %reduce-scatter.5.cloned.1.call-start = ((), (), s32[]{:S(2)}) async-start(), calls=%async_computation.7 | async-start | bytes 7077888 | tf_op jit(solution)/shard_map/reduce_scatter | solution.py:1020
  454.1 29.8 %collective-permute-start.46 = (bf16[128,1536]{1,0:T(8,128)(2,1)S(1)}, bf16[128,1536]{1,0:T(8,128)(2,1)S(1)}, u32[]{:S(2)}, u32[]{:S(2)}) collective-permute-start(bf16[128,1536]{1,0:T(8,128)(2,1)S(1)} %copy-done.45), channel_id=1, source_target_pairs={{0,16},{8,24},{16,0},{24,8},{1,17},{9,25},{17,1},{25,9},{2,18},{10... | collective-permute-start | bytes 1179656 | tf_op jit(solution)/shard_map/ppermute | solution.py:81
  455.8 28.2 %collective-permute-start.47 = (bf16[128,1536]{1,0:T(8,128)(2,1)S(1)}, bf16[128,1536]{1,0:T(8,128)(2,1)S(1)}, u32[]{:S(2)}, u32[]{:S(2)}) collective-permute-start(bf16[128,1536]{1,0:T(8,128)(2,1)S(1)} %copy-done.44), channel_id=1, source_target_pairs={{0,24},{8,16},{16,8},{24,0},{1,25},{9,17},{17,9},{25,1},{2,26},{10... | collective-permute-start | bytes 1179656 | tf_op jit(solution)/shard_map/ppermute | solution.py:81
  488.1 22.7 %collective-permute-start.48 = (bf16[128,1536]{1,0:T(8,128)(2,1)}, bf16[128,1536]{1,0:T(8,128)(2,1)S(1)}, u32[]{:S(2)}, u32[]{:S(2)}) collective-permute-start(bf16[128,1536]{1,0:T(8,128)(2,1)} %token_grad.1.rest_0_), channel_id=1, source_target_pairs={{0,8},{8,0},{16,24},{24,16},{1,9},{9,1},{17,25},{25,17},{2,10},{10... | collective-permute-start | bytes 1179656 | tf_op jit(solution)/shard_map/ppermute | solution.py:81
  495.8 30.0 %collective-permute-start.49 = (bf16[128,1536]{1,0:T(8,128)(2,1)}, bf16[128,1536]{1,0:T(8,128)(2,1)S(1)}, u32[]{:S(2)}, u32[]{:S(2)}) collective-permute-start(bf16[128,1536]{1,0:T(8,128)(2,1)} %token_grad.1.rest_0_), channel_id=1, source_target_pairs={{0,16},{8,24},{16,0},{24,8},{1,17},{9,25},{17,1},{25,9},{2,18},{10... | collective-permute-start | bytes 1179656 | tf_op jit(solution)/shard_map/ppermute | solution.py:81
  495.9 29.9 %collective-permute-start.50 = (bf16[128,1536]{1,0:T(8,128)(2,1)}, bf16[128,1536]{1,0:T(8,128)(2,1)S(1)}, u32[]{:S(2)}, u32[]{:S(2)}) collective-permute-start(bf16[128,1536]{1,0:T(8,128)(2,1)} %token_grad.1.rest_0_), channel_id=1, source_target_pairs={{0,24},{8,16},{16,8},{24,0},{1,25},{9,17},{17,9},{25,1},{2,26},{10... | collective-permute-start | bytes 1179656 | tf_op jit(solution)/shard_map/ppermute | solution.py:81
  (90 other events, 669.2 us)
Sparse Core Ops, SparseCore 0:
  10.5 41.6 all-gather.3
  54.7 55.0 all-gather.5
  136.5 63.4 all-gather.7
  271.7 93.2 reduce-scatter.2
  380.5 73.3 all-reduce.3
  457.2 60.6 reduce-scatter.4

commit v4 on v3

--- a/solution.py
+++ b/solution.py
@@ -453,7 +453,7 @@
             part[...] = acc_ref[at * chunk : (at + 1) * chunk, :].astype(LOW)
 
 
-def mlp_grads(cot_ref, all_ref, down_ref, middle_ref, *rest):
+def mlp_grads(cot_ref, near_ref, far_ref, down_ref, middle_ref, *rest):
     ways = (len(rest) - 3) // 2
     pieces, grad_ref, outs, left_ref, acc_ref = rest[:ways], rest[ways], rest[ways + 1 : -2], rest[-2], rest[-1]
     step, third = pl.program_id(0), pl.num_programs(0) // 3
@@ -472,7 +472,7 @@
             part = cot_ref[at * chunk : (at + 1) * chunk, :]
             left_ref[:, at * chunk : (at + 1) * chunk] = part.astype(WIDE).T.astype(LOW)
 
-    right = all_ref[0]
+    right = jnp.concatenate([near_ref[0], far_ref[0]], axis=0)
     grad_ref[...] = mm(left_ref[...], right).astype(LOW)
 
     @pl.when(step >= 2 * third)
@@ -758,7 +758,7 @@
     normed, out_parts = lax.optimization_barrier((normed, out_parts))
     w_out_x = lax.all_gather(after(out_parts, w_in), "seq", axis=0, tiled=True)
 
-    orders = [(4, 2) if head % 2 else (2, 4) for head in range(heads)]
+    orders = [(2, 4)] * heads
     first, mixed, ready, full = [], [], {}, {}
 
     def step(kind, head):
@@ -792,7 +792,7 @@
             held = kept[2]
         else:
             held = after(kept[2], mixed[-1][0])
-        outs = run_cross_forward(places, held, kept[8], kept[9], doc_col, docs, ready[head], head % 2 == 1)
+        outs = run_cross_forward(places, held, kept[8], kept[9], doc_col, docs, ready[head], False)
         mixed.append(meet(outs, flying))
         flying = []
         for later in range(head + 1, heads):
@@ -818,31 +818,42 @@
 
     blocks = 2
     cols = hidden_units // blocks
-    all_three, *backs = pl.pallas_call(
-        mlp_forward,
-        grid=(blocks,),
-        in_specs=[
-            fixed(tall),
-            pl.BlockSpec((width, cols), lambda step: (0, step)),
-            pl.BlockSpec((width, cols), lambda step: (0, blocks + step)),
-            pl.BlockSpec((width, cols), lambda step: (0, 2 * blocks + step)),
-            *whole(*two_parts),
-        ],
-        out_specs=[pl.BlockSpec((3, row_count, cols), lambda step: (0, 0, step))] + [fixed((chunk, width))] * ways,
-        out_shape=[jax.ShapeDtypeStruct((3, row_count, hidden_units), LOW)]
-        + [jax.ShapeDtypeStruct((chunk, width), LOW)] * ways,
-        scratch_shapes=[pltpu.VMEM(tall, LOW), pltpu.VMEM(tall, WIDE)],
-        compiler_params=pltpu.CompilerParams(vmem_limit_bytes=VMEM_BYTES),
-        cost_estimate=pl.CostEstimate(flops=10**10, bytes_accessed=2**24, transcendentals=2**19),
-        name="mlp_forward",
-    )(cot_x, w_rest, w_rest, w_rest, *two_parts)
-    backs = to_heads(backs)
+
+    def mlp_half(parts, at):
+        rows = chunk * len(parts)
+        return pl.pallas_call(
+            mlp_forward,
+            grid=(blocks,),
+            in_specs=[
+                pl.BlockSpec((rows, width), lambda step: (at, 0)),
+                pl.BlockSpec((width, cols), lambda step: (0, step)),
+                pl.BlockSpec((width, cols), lambda step: (0, blocks + step)),
+                pl.BlockSpec((width, cols), lambda step: (0, 2 * blocks + step)),
+                *whole(*parts),
+            ],
+            out_specs=[pl.BlockSpec((3, rows, cols), lambda step: (0, 0, step))] + [fixed((chunk, width))] * len(parts),
+            out_shape=[jax.ShapeDtypeStruct((3, rows, hidden_units), LOW)]
+            + [jax.ShapeDtypeStruct((chunk, width), LOW)] * len(parts),
+            scratch_shapes=[pltpu.VMEM((rows, width), LOW), pltpu.VMEM((rows, width), WIDE)],
+            compiler_params=pltpu.CompilerParams(vmem_limit_bytes=VMEM_BYTES),
+            cost_estimate=pl.CostEstimate(flops=5 * 10**9, bytes_accessed=2**24, transcendentals=2**19),
+            name="mlp_forward",
+        )(cot_x, w_rest, w_rest, w_rest, *parts)
+
+    near_all, *near_backs = mlp_half(two_parts[: ways // 2], 0)
+    (near_all, near_backs), far_two = lax.optimization_barrier(((near_all, near_backs), two_parts[ways // 2 :]))
+    near_moves = [xor_move(part, "head", at) if at else part for at, part in enumerate(near_backs)]
+    far_all, *far_backs = mlp_half([after(part, near_all) for part in far_two], 1)
+    (far_all, far_backs), near_moves = lax.optimization_barrier(((far_all, far_backs), near_moves))
+    two_parts = two_parts[: ways // 2] + list(far_two)
+    backs = near_moves + [xor_move(part, "head", ways // 2 + at) for at, part in enumerate(far_backs)]
     grad_mlp, *mlp_parts = pl.pallas_call(
         mlp_grads,
         grid=(3 * blocks,),
         in_specs=[
             fixed(tall),
-            pl.BlockSpec((1, row_count, cols), lambda step: (step // blocks, 0, step % blocks)),
+            pl.BlockSpec((1, row_count // 2, cols), lambda step: (step // blocks, 0, step % blocks)),
+            pl.BlockSpec((1, row_count // 2, cols), lambda step: (step // blocks, 0, step % blocks)),
             pl.BlockSpec((width, cols), lambda step: (0, jnp.maximum(step, 2 * blocks))),
             fixed((chunk, width)),
             *whole(*two_parts),
@@ -854,7 +865,7 @@
         compiler_params=pltpu.CompilerParams(vmem_limit_bytes=VMEM_BYTES),
         cost_estimate=pl.CostEstimate(flops=10**10, bytes_accessed=2**24, transcendentals=0),
         name="mlp_grads",
-    )(cot_x, all_three, w_rest, middle, *two_parts)
+    )(cot_x, near_all, far_all, w_rest, middle, *two_parts)
     grad_mlp, mlp_parts, backs = lax.optimization_barrier((grad_mlp, mlp_parts, backs))
     reduced_mlp = lax.psum_scatter(grad_mlp, "seq", scatter_dimension=0, tiled=True)
 
@@ -887,7 +898,7 @@
         held = kept[2] if head == 0 else after(kept[2], second[-1][0])
         flying = (core.get(head - 1), across.get(head - 2), branch_next())
         outs = run_cross_backward(
-            places, held, kept[3], mixed[head][0], mixed[head][2], doc_col, docs, packs[head], d_atts, head, head % 2 == 1
+            places, held, kept[3], mixed[head][0], mixed[head][2], doc_col, docs, packs[head], d_atts, head, False
         )
         outs, (core_in, across_in, branch_in) = lax.optimization_barrier((outs, flying))
         even, odd, *rest = outs
@@ -1025,21 +1036,31 @@
         whole(reduced_in),
         [((shard, inner), WIDE)] * 4 + [((shard, 128), WIDE), ((shard, inner), WIDE)],
     )
+    reduced_mlp = reduced_mlp.astype(WIDE)
+    finished = (
+        *grads,
+        small_sum,
+        grad_out_t.T,
+        reduced_mlp[:, :hidden_units],
+        reduced_mlp[:, hidden_units : 2 * hidden_units],
+        reduced_mlp[:, 2 * hidden_units :].T,
+    )
+    finished, token_parts = lax.optimization_barrier((finished, token_parts))
+    *grads, small_sum, grad_out, grad_gate, grad_up, grad_down = finished
     (d_tokens,) = run(
         token_join, "token_join", (places, *token_parts), [SCALARS, *whole(*token_parts)], [(tall, WIDE)]
     )
-    reduced_mlp = reduced_mlp.astype(WIDE)
     return (
         result,
         d_tokens,
         small_sum[:, heads],
         *grads,
         small_sum[:, :heads],
-        grad_out_t.T,
+        grad_out,
         small_sum[:, heads + 1],
-        reduced_mlp[:, :hidden_units],
-        reduced_mlp[:, hidden_units : 2 * hidden_units],
-        reduced_mlp[:, 2 * hidden_units :].T,
+        grad_gate,
+        grad_up,
+        grad_down,
     )
 
 

time: 551 us -> 530 us (0.962)
  waiting for transfers between devices: 227 us -> 194 us
  starting transfers between devices: 85.6 us -> 94.2 us
    ppermute x51, waiting for transfers between devices: 193 us -> 148 us  [xor_move(): lax.ppermute(value, axis, [(at, at ^ mask) for at in range(lax.axis_size(...]
    reduce_scatter x1, waiting for transfers between devices: 0.01 us -> 18.9 us  [per_device(): lax.psum_scatter(grad_in, 'seq', scatter_dimension=0, tiled=True)]
    ppermute x51, starting transfers between devices: 85.2 us -> 93.8 us  [xor_move(): lax.ppermute(value, axis, [(at, at ^ mask) for at in range(lax.axis_size(...]
    reduce_scatter x1, waiting for transfers between devices: 8.18 us -> 0.01 us  [per_device(): lax.psum_scatter(grad_mlp, 'seq', scatter_dimension=0, tiled=True)]
    pallas_call x1 -> x2, Pallas kernels: 14.8 us -> 19 us  [mlp_half(): pl.pallas_call(mlp_forward, grid=(blocks,), in_specs=[pl.BlockSpec((rows,...]
    unnamed x118 -> x102, local copies, waits for them, and re-layouts: 14.2 us -> 11.7 us
  transfers between devices with their start and end apart: 57 -> 57, of which waited for: 29 -> 27; matrix products, arithmetic and copies ran while one was open for 3% -> 3% of each run, Pallas kernels for 30% -> 35%
where the time goes in v4:
time: 530 us; the launch traced here: 521 us
  waiting for transfers between devices  194 us (37%)
  Pallas kernels  188 us (35%)
  starting transfers between devices  94.2 us (18%)
  local copies, waits for them, and re-layouts  16.8 us (3%)
  between operations  14.8 us (3%)
  other arithmetic  13 us (2%)
    ppermute x51, waiting for transfers between devices, xor_move(): lax.ppermute(value, axis, [(at, at ^ mask) for at in range(lax.axis_size(...  148 us
    pallas_call x22, Pallas kernels, run(): pl.pallas_call(kernel, grid=(1,), in_specs=specs, out_specs=[fixed(shape)...  136 us
    ppermute x51, starting transfers between devices, xor_move(): lax.ppermute(value, axis, [(at, at ^ mask) for at in range(lax.axis_size(...  93.8 us
    pallas_call x2, Pallas kernels, mlp_half(): pl.pallas_call(mlp_forward, grid=(blocks,), in_specs=[pl.BlockSpec((rows,...  19 us
    reduce_scatter x1, waiting for transfers between devices, per_device(): lax.psum_scatter(grad_in, 'seq', scatter_dimension=0, tiled=True)  18.9 us
    pallas_call x5, Pallas kernels, grads_into(): pl.pallas_call(kernel, grid=(grid,), in_specs=specs + [ANYWHERE] * len(gi...  18.8 us
    pallas_call x1, Pallas kernels, per_device(): pl.pallas_call(mlp_grads, grid=(3 * blocks,), in_specs=[fixed(tall), pl.B...  14.9 us
    all_gather x1, waiting for transfers between devices, per_device(): w_in = lax.all_gather(packed, 'seq', axis=0, tiled=True)  14.5 us
  transfers between devices with their start and end apart: 57, of which 27 were waited for; matrix products, arithmetic and copies ran while one was open for 3% of the time, Pallas kernels for 35%

profile of v4, /device:TPU:0, one launch (start us, length us, event | category | flops | bytes accessed | tf_op | source)
XLA Modules:
  0.0 521.1 jit_solution(159110897587998874)
XLA Ops:
  30.2 7.6 %prepare.1 = (bf16[512,1536]{1,0:T(8,128)(2,1)}, bf16[1536,512]{1,0:T(8,128)(2,1)}, bf16[512,1536]{1,0:T(8,128)(2,1)}, bf16[512,1536]{1,0:T(8,128)(2,1)}, bf16[1...) custom-call(s32[3]{0:T(128)} %pad_add_fusion.place_ref, ...), custom_call_target="tpu_custom_call" | custom-call | flops 1000000000 | bytes 4194304 | tf_op jit(solution)/shard_map/prepare/pallas_call | solution.py:596
  37.7 14.5 %all-gather.4.cloned.1.call-done.w_ref = bf16[1536,1536]{1,0:T(8,128)(2,1)} async-done(((bf16[192,1536]{1,0:T(8,128)(2,1)}), bf16[1536,1536]{1,0:T(8,128)(2,1)}) %all-gather.4.cloned.1.call-update) | async-done | bytes 4718608 | tf_op jit(solution)/shard_map/all_gather | solution.py:732
  52.5 12.1 %block_forward.3 = (f32[512,512]{1,0:T(8,128)}, bf16[1152,128]{1,0:T(8,128)(2,1)}, f32[512,128]{1,0:T(8,128)}, f32[512,512]{1,0:T(8,128)}, bf16[512,512]{1,0:T(8...) custom-call(s32[3]{0:T(128)} %pad_add_fusion.place_ref, ...), custom_call_target="tpu_custom_call" | custom-call | flops 10000000000 | bytes 4194304 | tf_op jit(solution)/shard_map/block_forward/pallas_call | solution.py:596
  66.0 12.5 %block_forward.4 = (f32[512,512]{1,0:T(8,128)}, bf16[1152,128]{1,0:T(8,128)(2,1)}, f32[512,128]{1,0:T(8,128)}, f32[512,512]{1,0:T(8,128)}, bf16[512,512]{1,0:T(8...) custom-call(s32[3]{0:T(128)} %pad_add_fusion.place_ref, ...), custom_call_target="tpu_custom_call" | custom-call | flops 10000000000 | bytes 4194304 | tf_op jit(solution)/shard_map/block_forward/pallas_call | solution.py:596
  80.6 12.2 %block_forward.5 = (f32[512,512]{1,0:T(8,128)}, bf16[1152,128]{1,0:T(8,128)(2,1)}, f32[512,128]{1,0:T(8,128)}, f32[512,512]{1,0:T(8,128)}, bf16[512,512]{1,0:T(8...) custom-call(s32[3]{0:T(128)} %pad_add_fusion.place_ref, ...), custom_call_target="tpu_custom_call" | custom-call | flops 10000000000 | bytes 4194304 | tf_op jit(solution)/shard_map/block_forward/pallas_call | solution.py:596
  93.6 13.3 %collective-permute-done.8 = bf16[2,1152,128]{2,1,0:T(8,128)(2,1)S(1)} collective-permute-done((bf16[2,1152,128]{2,1,0:T(8,128)(2,1)S(1)}, bf16[2,1152,128]{2,1,0:T(8,128)(2,1)S(1)}, u32[]{:S(2)}, u32[]{:S(2)}) %collective-permute-start.8) | collective-permute-done | bytes 589856 | tf_op jit(solution)/shard_map/ppermute | solution.py:81
  117.6 7.6 %collective-permute-done.11 = bf16[2,1152,128]{2,1,0:T(8,128)(2,1)S(1)} collective-permute-done((bf16[2,1152,128]{2,1,0:T(8,128)(2,1)S(1)}, bf16[2,1152,128]{2,1,0:T(8,128)(2,1)S(1)}, u32[]{:S(2)}, u32[]{:S(2)}) %collective-permute-start.11) | collective-permute-done | bytes 589856 | tf_op jit(solution)/shard_map/ppermute | solution.py:81
  132.9 13.7 %collective-permute-done.13 = bf16[2,1152,128]{2,1,0:T(8,128)(2,1)S(1)} collective-permute-done((bf16[2,1152,128]{2,1,0:T(8,128)(2,1)S(1)}, bf16[2,1152,128]{2,1,0:T(8,128)(2,1)S(1)}, u32[]{:S(2)}, u32[]{:S(2)}) %collective-permute-start.13) | collective-permute-done | bytes 589856 | tf_op jit(solution)/shard_map/ppermute | solution.py:81
  179.7 14.6 %collective-permute-done.18.rest_1_ = bf16[128,1536]{1,0:T(8,128)(2,1)S(1)} collective-permute-done((bf16[128,1536]{1,0:T(8,128)(2,1)}, bf16[128,1536]{1,0:T(8,128)(2,1)S(1)}, u32[]{:S(2)}, u32[]{:S(2)}) %collective-permute-start.18) | collective-permute-done | bytes 393248 | tf_op jit(solution)/shard_map/ppermute | solution.py:81
  195.0 9.5 %mlp_forward.2 = (bf16[3,256,1024]{2,1,0:T(8,128)(2,1)}, bf16[128,1536]{1,0:T(8,128)(2,1)}, bf16[128,1536]{1,0:T(8,128)(2,1)}) custom-call(bf16[512,1536]{1,0:T(8,128)(2,1)} %get-tuple-element.302.cot_ref, bf16[1536,3072]{1,0:T(8,128)(2,1)} %all-gather.8.cloned.1.call-done.gate_ref.up_ref.down_ref, ...), custom_call_target="tpu_custom_call" | custom-call | flops 5000000000 | bytes 16777216 | tf_op jit(solution)/shard_map/mlp_forward/pallas_call | solution.py:824
  207.3 7.6 %collective-permute-start.21 = (bf16[128,1536]{1,0:T(8,128)(2,1)}, bf16[128,1536]{1,0:T(8,128)(2,1)S(1)}, u32[]{:S(2)}, u32[]{:S(2)}) collective-permute-start(bf16[128,1536]{1,0:T(8,128)(2,1)} %get-tuple-element.317), channel_id=1, source_target_pairs={{0,8},{8,0},{16,24},{24,16},{1,9},{9,1},{17,25},{25,17},{2,10},{10... | collective-permute-start | bytes 1179656 | tf_op jit(solution)/shard_map/ppermute | solution.py:81
  214.9 9.6 %mlp_forward.3 = (bf16[3,256,1024]{2,1,0:T(8,128)(2,1)}, bf16[128,1536]{1,0:T(8,128)(2,1)}, bf16[128,1536]{1,0:T(8,128)(2,1)}) custom-call(bf16[512,1536]{1,0:T(8,128)(2,1)} %get-tuple-element.302.cot_ref, bf16[1536,3072]{1,0:T(8,128)(2,1)} %all-gather.8.cloned.1.call-done.gate_ref.up_ref.down_ref, ...), custom_call_target="tpu_custom_call" | custom-call | flops 5000000000 | bytes 16777216 | tf_op jit(solution)/shard_map/mlp_forward/pallas_call | solution.py:824
  227.6 14.9 %mlp_grads.1 = (bf16[1536,3072]{1,0:T(8,128)(2,1)}, bf16[128,1536]{1,0:T(8,128)(2,1)}, bf16[128,1536]{1,0:T(8,128)(2,1)}, bf16[128,1536]{1,0:T(8,128)(2,1)}, bf16[128,1536]{1,0:T(8,128)(2,1)}) custom-call(bf16[512,1536]{1,0:T(8,128)(2,1)} %get-tuple-element.302.cot_ref, bf16[3,256,1024]{2,1,0:T(8,128)(2,1)} %get-tuple-element.308.near_ref, ...), custom_call_target="tpu_custom_call" | custom-call | flops 10000000000 | bytes 16777216 | tf_op jit(solution)/shard_map/mlp_grads/pallas_call | solution.py:850
  242.5 10.0 %collective-permute-done.22.rest_2_ = bf16[128,1536]{1,0:T(8,128)(2,1)S(1)} collective-permute-done((bf16[128,1536]{1,0:T(8,128)(2,1)}, bf16[128,1536]{1,0:T(8,128)(2,1)S(1)}, u32[]{:S(2)}, u32[]{:S(2)}) %collective-permute-start.22) | collective-permute-done | bytes 393248 | tf_op jit(solution)/shard_map/ppermute | solution.py:81
  258.9 8.3 %collective-permute-start.24 = (bf16[128,384]{1,0:T(8,128)(2,1)}, bf16[128,384]{1,0:T(8,128)(2,1)S(1)}, u32[]{:S(2)}, u32[]{:S(2)}) collective-permute-start(bf16[128,384]{1,0:T(8,128)(2,1)} %get-tuple-element.338), channel_id=1, source_target_pairs={{0,8},{8,0},{16,24},{24,16},{1,9},{9,1},{17,25},{25,17},{2,10},{10... | collective-permute-start | bytes 294920 | tf_op jit(solution)/shard_map/ppermute | solution.py:81
  296.9 8.2 %collective-permute-done.30.rest_4_ = bf16[64,1536]{1,0:T(8,128)(2,1)S(1)} collective-permute-done((bf16[64,1536]{1,0:T(8,128)(2,1)S(1)}, bf16[64,1536]{1,0:T(8,128)(2,1)S(1)}, u32[]{:S(2)}, u32[]{:S(2)}) %collective-permute-start.30) | collective-permute-done | bytes 196640 | tf_op jit(solution)/shard_map/ppermute | solution.py:81
  319.7 10.3 %collective-permute-done.32 = bf16[2,1152,128]{2,1,0:T(8,128)(2,1)S(1)} collective-permute-done((bf16[2,1152,128]{2,1,0:T(8,128)(2,1)S(1)}, bf16[2,1152,128]{2,1,0:T(8,128)(2,1)S(1)}, u32[]{:S(2)}, u32[]{:S(2)}) %collective-permute-start.32) | collective-permute-done | bytes 589856 | tf_op jit(solution)/shard_map/ppermute | solution.py:81
  330.9 7.5 %collective-permute-start.34 = (bf16[1152,128]{1,0:T(8,128)(2,1)S(1)}, bf16[1152,128]{1,0:T(8,128)(2,1)}, u32[]{:S(2)}, u32[]{:S(2)}) collective-permute-start(bf16[1152,128]{1,0:T(8,128)(2,1)S(1)} %get-tuple-element.518), channel_id=1, source_target_pairs={{0,2},{1,3},{2,0},{3,1},{4,6},{5,7},{6,4},{7,5},{8,10},{9,11},{10,... | collective-permute-start | bytes 884744 | tf_op jit(solution)/shard_map/ppermute | solution.py:81
  394.3 7.4 %block_backward.5 = (bf16[512,512]{1,0:T(8,128)(2,1)}, bf16[512,128]{1,0:T(8,128)(2,1)}) custom-call(s32[3]{0:T(128)} %pad_add_fusion.place_ref, f32[512,512]{1,0:T(8,128)} %get-tuple-element.412.proj_ref, f32[512,128]{1,0:T(8,128)} %get-tuple-element.245.beta_ref, bf16[512,512]{1,0:T(8,128)(2,1)} %get-tuple-element.413.inv_ref, ...), custom_call_target="tpu_custom_call" | custom-call | flops 5000000000 | bytes 4194304 | tf_op jit(solution)/shard_map/block_backward/pallas_call | solution.py:596
  422.7 12.2 %all-reduce.4.cloned.1.call-done = bf16[512,1536]{1,0:T(8,128)(2,1)} async-done(((bf16[512,1536]{1,0:T(8,128)(2,1)}), bf16[512,1536]{1,0:T(8,128)(2,1)}) %all-reduce.4.cloned.1.call-update) | async-done | bytes 1572880 | tf_op jit(solution)/shard_map/psum | solution.py:917
  439.7 13.6 %collective-permute-done.45.rest_1_ = bf16[128,1536]{1,0:T(8,128)(2,1)S(1)} collective-permute-done((bf16[128,1536]{1,0:T(8,128)(2,1)}, bf16[128,1536]{1,0:T(8,128)(2,1)S(1)}, u32[]{:S(2)}, u32[]{:S(2)}) %collective-permute-start.45) | collective-permute-done | bytes 393248 | tf_op jit(solution)/shard_map/ppermute | solution.py:81
  453.3 11.9 %collective-permute-done.46.rest_2_ = bf16[128,1536]{1,0:T(8,128)(2,1)} collective-permute-done((bf16[128,1536]{1,0:T(8,128)(2,1)}, bf16[128,1536]{1,0:T(8,128)(2,1)}, u32[]{:S(2)}, u32[]{:S(2)}) %collective-permute-start.46) | collective-permute-done | bytes 393248 | tf_op jit(solution)/shard_map/ppermute | solution.py:81
  468.4 7.7 %collective-permute-start.48 = (bf16[128,1536]{1,0:T(8,128)(2,1)}, bf16[128,1536]{1,0:T(8,128)(2,1)}, u32[]{:S(2)}, u32[]{:S(2)}) collective-permute-start(bf16[128,1536]{1,0:T(8,128)(2,1)} %token_grad.1.rest_0_), channel_id=1, source_target_pairs={{0,8},{8,0},{16,24},{24,16},{1,9},{9,1},{17,25},{25,17},{2,10},{10... | collective-permute-start | bytes 1179656 | tf_op jit(solution)/shard_map/ppermute | solution.py:81
  480.0 18.9 %reduce-scatter.5.cloned.1.call-done.in_ref = bf16[192,2048]{1,0:T(8,128)(2,1)} async-done(((bf16[1536,2048]{1,0:T(8,128)(2,1)}), bf16[192,2048]{1,0:T(8,128)(2,1)}) %reduce-scatter.5.cloned.1.call-update) | async-done | bytes 786448 | tf_op jit(solution)/shard_map/reduce_scatter | solution.py:1031
  (260 shorter events, 240.8 us)
Async XLA Ops:
  7.2 45.0 %all-gather.4.cloned.1.call-start = ((), (), s32[]{:S(2)}) async-start(), calls=%async_computation.2 | async-start | bytes 5308416 | tf_op jit(solution)/shard_map/all_gather | solution.py:732
  9.4 115.8 %all-gather.6.cloned.1.call-start = ((), (), s32[]{:S(2)}) async-start(), calls=%async_computation.3 | async-start | bytes 5308416 | tf_op jit(solution)/shard_map/all_gather | solution.py:759
  52.2 142.0 %all-gather.8.cloned.1.call-start = ((), (), s32[]{:S(2)}) async-start(), calls=%async_computation.4 | async-start | bytes 10616832 | tf_op jit(solution)/shard_map/all_gather | solution.py:803
  79.2 27.6 %collective-permute-start.8 = (bf16[2,1152,128]{2,1,0:T(8,128)(2,1)S(1)}, bf16[2,1152,128]{2,1,0:T(8,128)(2,1)S(1)}, u32[]{:S(2)}, u32[]{:S(2)}) collective-permute-start(bf16[2,1152,128]{2,1,0:T(8,128)(2,1)S(1)} %pad_maximum_fusion.7), channel_id=1, source_target_pairs={{0,4},{1,5},{2,6},{3,7},{4,0},{5,1},{6,2},{7,3},{8,12},{9,13},{10,... | collective-permute-start | bytes 1769480 | tf_op jit(solution)/shard_map/ppermute | solution.py:81
  125.3 222.4 %reduce-scatter.3.cloned.1.call-start = ((), (), s32[]{:S(2)}) async-start(), calls=%async_computation.5 | async-start | bytes 10616832 | tf_op jit(solution)/shard_map/reduce_scatter | solution.py:870
  125.6 21.0 %collective-permute-start.13 = (bf16[2,1152,128]{2,1,0:T(8,128)(2,1)S(1)}, bf16[2,1152,128]{2,1,0:T(8,128)(2,1)S(1)}, u32[]{:S(2)}, u32[]{:S(2)}) collective-permute-start(bf16[2,1152,128]{2,1,0:T(8,128)(2,1)S(1)} %pad_maximum_fusion.9), channel_id=1, source_target_pairs={{0,4},{1,5},{2,6},{3,7},{4,0},{5,1},{6,2},{7,3},{8,12},{9,13},{10,... | collective-permute-start | bytes 1769480 | tf_op jit(solution)/shard_map/ppermute | solution.py:81
  175.0 19.2 %collective-permute-start.18 = (bf16[128,1536]{1,0:T(8,128)(2,1)}, bf16[128,1536]{1,0:T(8,128)(2,1)S(1)}, u32[]{:S(2)}, u32[]{:S(2)}) collective-permute-start(bf16[128,1536]{1,0:T(8,128)(2,1)} %get-tuple-element.304.rest_0_), channel_id=1, source_target_pairs={{0,8},{8,0},{16,24},{24,16},{1,9},{9,1},{17,25},{25,17},{2,10},{10... | collective-permute-start | bytes 1179656 | tf_op jit(solution)/shard_map/ppermute | solution.py:81
  177.3 30.0 %collective-permute-start.19 = (bf16[128,1536]{1,0:T(8,128)(2,1)}, bf16[128,1536]{1,0:T(8,128)(2,1)S(1)}, u32[]{:S(2)}, u32[]{:S(2)}) collective-permute-start(bf16[128,1536]{1,0:T(8,128)(2,1)} %get-tuple-element.304.rest_0_), channel_id=1, source_target_pairs={{0,16},{8,24},{16,0},{24,8},{1,17},{9,25},{17,1},{25,9},{2,18},{10... | collective-permute-start | bytes 1179656 | tf_op jit(solution)/shard_map/ppermute | solution.py:81
  178.3 29.1 %collective-permute-start.20 = (bf16[128,1536]{1,0:T(8,128)(2,1)}, bf16[128,1536]{1,0:T(8,128)(2,1)S(1)}, u32[]{:S(2)}, u32[]{:S(2)}) collective-permute-start(bf16[128,1536]{1,0:T(8,128)(2,1)} %get-tuple-element.304.rest_0_), channel_id=1, source_target_pairs={{0,24},{8,16},{16,8},{24,0},{1,25},{9,17},{17,9},{25,1},{2,26},{10... | collective-permute-start | bytes 1179656 | tf_op jit(solution)/shard_map/ppermute | solution.py:81
  224.5 28.1 %collective-permute-start.22 = (bf16[128,1536]{1,0:T(8,128)(2,1)}, bf16[128,1536]{1,0:T(8,128)(2,1)S(1)}, u32[]{:S(2)}, u32[]{:S(2)}) collective-permute-start(bf16[128,1536]{1,0:T(8,128)(2,1)} %get-tuple-element.326), channel_id=1, source_target_pairs={{0,16},{8,24},{16,0},{24,8},{1,17},{9,25},{17,1},{25,9},{2,18},{10... | collective-permute-start | bytes 1179656 | tf_op jit(solution)/shard_map/ppermute | solution.py:81
  226.2 26.4 %collective-permute-start.23 = (bf16[128,1536]{1,0:T(8,128)(2,1)}, bf16[128,1536]{1,0:T(8,128)(2,1)S(1)}, u32[]{:S(2)}, u32[]{:S(2)}) collective-permute-start(bf16[128,1536]{1,0:T(8,128)(2,1)} %get-tuple-element.327), channel_id=1, source_target_pairs={{0,24},{8,16},{16,8},{24,0},{1,25},{9,17},{17,9},{25,1},{2,26},{10... | collective-permute-start | bytes 1179656 | tf_op jit(solution)/shard_map/ppermute | solution.py:81
  253.4 181.5 %all-reduce.4.cloned.1.call-start = ((), (), s32[]{:S(2)}) async-start(), calls=%async_computation.6 | async-start | bytes 3145728 | tf_op jit(solution)/shard_map/psum | solution.py:917
  290.9 28.8 %collective-permute-start.33 = (bf16[64,1536]{1,0:T(8,128)(2,1)}, bf16[64,1536]{1,0:T(8,128)(2,1)}, u32[]{:S(2)}, u32[]{:S(2)}) collective-permute-start(bf16[64,1536]{1,0:T(8,128)(2,1)} %get-tuple-element.347.rest_1_), channel_id=1, source_target_pairs={{0,16},{8,24},{16,0},{24,8},{1,17},{9,25},{17,1},{25,9},{2,18},{10... | collective-permute-start | bytes 589832 | tf_op jit(solution)/shard_map/ppermute | solution.py:81
  305.8 24.3 %collective-permute-start.31 = (bf16[4,1152,128]{2,1,0:T(8,128)(2,1)}, bf16[4,1152,128]{2,1,0:T(8,128)(2,1)}, u32[]{:S(2)}, u32[]{:S(2)}) collective-permute-start(bf16[4,1152,128]{2,1,0:T(8,128)(2,1)} %get-tuple-element.371), channel_id=1, source_target_pairs={{0,1},{1,0},{2,3},{3,2},{4,5},{5,4},{6,7},{7,6},{8,9},{9,8},{10,11... | collective-permute-start | bytes 3538952 | tf_op jit(solution)/shard_map/ppermute | solution.py:81
  307.3 22.7 %collective-permute-start.32 = (bf16[2,1152,128]{2,1,0:T(8,128)(2,1)S(1)}, bf16[2,1152,128]{2,1,0:T(8,128)(2,1)S(1)}, u32[]{:S(2)}, u32[]{:S(2)}) collective-permute-start(bf16[2,1152,128]{2,1,0:T(8,128)(2,1)S(1)} %get-tuple-element.507), channel_id=1, source_target_pairs={{0,4},{1,5},{2,6},{3,7},{4,0},{5,1},{6,2},{7,3},{8,12},{9,13},{10,... | collective-permute-start | bytes 1769480 | tf_op jit(solution)/shard_map/ppermute | solution.py:81
  338.5 18.1 %collective-permute-start.36 = (bf16[4,1152,128]{2,1,0:T(8,128)(2,1)}, bf16[4,1152,128]{2,1,0:T(8,128)(2,1)}, u32[]{:S(2)}, u32[]{:S(2)}) collective-permute-start(bf16[4,1152,128]{2,1,0:T(8,128)(2,1)} %get-tuple-element.389), channel_id=1, source_target_pairs={{0,1},{1,0},{2,3},{3,2},{4,5},{5,4},{6,7},{7,6},{8,9},{9,8},{10,11... | collective-permute-start | bytes 3538952 | tf_op jit(solution)/shard_map/ppermute | solution.py:81
  344.3 33.3 %collective-permute-start.40 = (bf16[64,1536]{1,0:T(8,128)(2,1)}, bf16[64,1536]{1,0:T(8,128)(2,1)}, u32[]{:S(2)}, u32[]{:S(2)}) collective-permute-start(bf16[64,1536]{1,0:T(8,128)(2,1)} %get-tuple-element.347.rest_1_), channel_id=1, source_target_pairs={{0,24},{8,16},{16,8},{24,0},{1,25},{9,17},{17,9},{25,1},{2,26},{10... | collective-permute-start | bytes 589832 | tf_op jit(solution)/shard_map/ppermute | solution.py:81
  361.5 137.4 %reduce-scatter.5.cloned.1.call-start = ((), (), s32[]{:S(2)}) async-start(), calls=%async_computation.7 | async-start | bytes 7077888 | tf_op jit(solution)/shard_map/reduce_scatter | solution.py:1031
  435.0 18.3 %collective-permute-start.45 = (bf16[128,1536]{1,0:T(8,128)(2,1)}, bf16[128,1536]{1,0:T(8,128)(2,1)S(1)}, u32[]{:S(2)}, u32[]{:S(2)}) collective-permute-start(bf16[128,1536]{1,0:T(8,128)(2,1)} %get-tuple-element.445), channel_id=1, source_target_pairs={{0,8},{8,0},{16,24},{24,16},{1,9},{9,1},{17,25},{25,17},{2,10},{10... | collective-permute-start | bytes 1179656 | tf_op jit(solution)/shard_map/ppermute | solution.py:81
  435.0 30.2 %collective-permute-start.46 = (bf16[128,1536]{1,0:T(8,128)(2,1)}, bf16[128,1536]{1,0:T(8,128)(2,1)}, u32[]{:S(2)}, u32[]{:S(2)}) collective-permute-start(bf16[128,1536]{1,0:T(8,128)(2,1)} %get-tuple-element.446), channel_id=1, source_target_pairs={{0,16},{8,24},{16,0},{24,8},{1,17},{9,25},{17,1},{25,9},{2,18},{10... | collective-permute-start | bytes 1179656 | tf_op jit(solution)/shard_map/ppermute | solution.py:81
  436.8 28.4 %collective-permute-start.47 = (bf16[128,1536]{1,0:T(8,128)(2,1)}, bf16[128,1536]{1,0:T(8,128)(2,1)}, u32[]{:S(2)}, u32[]{:S(2)}) collective-permute-start(bf16[128,1536]{1,0:T(8,128)(2,1)} %get-tuple-element.447), channel_id=1, source_target_pairs={{0,24},{8,16},{16,8},{24,0},{1,25},{9,17},{17,9},{25,1},{2,26},{10... | collective-permute-start | bytes 1179656 | tf_op jit(solution)/shard_map/ppermute | solution.py:81
  468.4 32.8 %collective-permute-start.48 = (bf16[128,1536]{1,0:T(8,128)(2,1)}, bf16[128,1536]{1,0:T(8,128)(2,1)}, u32[]{:S(2)}, u32[]{:S(2)}) collective-permute-start(bf16[128,1536]{1,0:T(8,128)(2,1)} %token_grad.1.rest_0_), channel_id=1, source_target_pairs={{0,8},{8,0},{16,24},{24,16},{1,9},{9,1},{17,25},{25,17},{2,10},{10... | collective-permute-start | bytes 1179656 | tf_op jit(solution)/shard_map/ppermute | solution.py:81
  476.1 30.1 %collective-permute-start.49 = (bf16[128,1536]{1,0:T(8,128)(2,1)}, bf16[128,1536]{1,0:T(8,128)(2,1)}, u32[]{:S(2)}, u32[]{:S(2)}) collective-permute-start(bf16[128,1536]{1,0:T(8,128)(2,1)} %token_grad.1.rest_0_), channel_id=1, source_target_pairs={{0,16},{8,24},{16,0},{24,8},{1,17},{9,25},{17,1},{25,9},{2,18},{10... | collective-permute-start | bytes 1179656 | tf_op jit(solution)/shard_map/ppermute | solution.py:81
  476.3 30.0 %collective-permute-start.50 = (bf16[128,1536]{1,0:T(8,128)(2,1)}, bf16[128,1536]{1,0:T(8,128)(2,1)}, u32[]{:S(2)}, u32[]{:S(2)}) collective-permute-start(bf16[128,1536]{1,0:T(8,128)(2,1)} %token_grad.1.rest_0_), channel_id=1, source_target_pairs={{0,24},{8,16},{16,8},{24,0},{1,25},{9,17},{17,9},{25,1},{2,26},{10... | collective-permute-start | bytes 1179656 | tf_op jit(solution)/shard_map/ppermute | solution.py:81
  (82 other events, 619.6 us)
Sparse Core Ops, SparseCore 0:
  10.5 41.6 all-gather.3
  54.7 55.3 all-gather.5
  125.4 63.4 all-gather.7
  252.7 89.1 reduce-scatter.2
  361.6 73.2 all-reduce.3
  438.2 60.6 reduce-scatter.4

commit v5 on v4

--- a/solution.py
+++ b/solution.py
@@ -13,7 +13,7 @@
 LOG2E = 1.4426950408889634
 LOW = jnp.bfloat16
 WIDE = jnp.float32
-VMEM_BYTES = 60 * 2**20
+VMEM_BYTES = 40 * 2**20
 
 
 def mm(left, right, ta=False, tb=False):
@@ -97,14 +97,15 @@
 
 
 def block_forward(
-    head, place_ref, normed_ref, w_ref, beta_ref, doc_col_ref, doc_row_ref,
+    place_ref, normed_ref, w_ref, beta_ref, doc_col_ref, doc_row_ref,
     proj_ref, pack_ref, qm_ref, score_ref, inv_ref, carried_ref, qdir_ref, solve_ref, stat_ref, acc_ref,
 ):
     proj_ref[...] = mm(normed_ref[...], w_ref[...])
     length, dim = qm_ref.shape
     query, key = proj_ref[:, 0:dim], proj_ref[:, dim : 2 * dim]
     value, dirs = proj_ref[:, 2 * dim : 3 * dim].astype(LOW), proj_ref[:, 3 * dim :]
-    beta = 2.0 * jax.nn.sigmoid(beta_ref[:, head : head + 1])
+    head = place_ref[3]
+    beta = 2.0 * jax.nn.sigmoid(jnp.sum(jnp.where(iota((length, 128), 1) == head, beta_ref[...], 0.0), axis=1, keepdims=True))
     unit = dirs * lax.rsqrt(jnp.sum(dirs * dirs, axis=-1, keepdims=True) + EPSILON)
     row, col = iota((length, length), 0), iota((length, length), 1)
     unit_two = halves(unit)
@@ -297,12 +298,13 @@
 
 
 def block_backward(
-    head, place_ref, proj_ref, beta_ref, inv_ref, carried_ref, qdir_ref, solve_ref, dqm_ref, dinside_ref, dval_ref, *rest
+    place_ref, proj_ref, beta_ref, inv_ref, carried_ref, qdir_ref, solve_ref, dqm_ref, dinside_ref, dval_ref, *rest
 ):
     *dpacks, dproj_ref, dbeta_ref = rest
     length, dim = dqm_ref.shape
     query, key, dirs = proj_ref[:, 0:dim], proj_ref[:, dim : 2 * dim], proj_ref[:, 3 * dim :]
-    beta = 2.0 * jax.nn.sigmoid(beta_ref[:, head : head + 1])
+    head = place_ref[3]
+    beta = 2.0 * jax.nn.sigmoid(jnp.sum(jnp.where(iota((length, 128), 1) == head, beta_ref[...], 0.0), axis=1, keepdims=True))
     norm = lax.rsqrt(jnp.sum(dirs * dirs, axis=-1, keepdims=True) + EPSILON)
     unit = dirs * norm
     low_unit, low_key, low_query = unit.astype(LOW), key.astype(LOW), query.astype(LOW)
@@ -614,7 +616,7 @@
     length, width = normed.shape
     square, tall = (length, length), (length, dim)
     return run(
-        functools.partial(block_forward, head),
+        block_forward,
         "block_forward",
         (places, normed, w_in, beta_raw, doc_col, doc_row),
         [SCALARS, *whole(normed), column_at((width, 4 * dim), at), *whole(beta_raw, doc_col, doc_row)],
@@ -681,7 +683,7 @@
     length = proj.shape[0]
     ins = (proj, beta_raw, *kept, *d_packs)
     return run(
-        functools.partial(block_backward, head),
+        block_backward,
         "block_backward",
         (places, *ins),
         [SCALARS, *whole(*ins)],
@@ -715,6 +717,7 @@
     chunk = row_count // ways
     seq_place, head_place = lax.axis_index("seq"), lax.axis_index("head")
     places = jnp.stack([seq_place % SPAN, head_place, seq_place]).astype(jnp.int32)
+    places_of = [jnp.concatenate([places, jnp.full((1,), head, jnp.int32)]) for head in range(heads)]
 
     def to_heads(parts):
         return [xor_move(part, "head", at) if at else part for at, part in enumerate(parts)]
@@ -773,7 +776,7 @@
     flying = []
     for head in range(heads):
         held = normed if head == 0 else after(normed, first[-1][2])
-        outs = run_block_forward(places, held, w_in, head, beta_raw, doc_col, docs, dim, head)
+        outs = run_block_forward(places_of[head], held, w_in, head, beta_raw, doc_col, docs, dim, head)
         first.append(meet(outs, flying))
         ready[head] = first[head][1][None]
         flying = [step(at, head - at) for at in range(max(0, head - 2), head + 1)]
@@ -976,7 +979,7 @@
         if head == 0:
             proj, reduced_mlp = lax.optimization_barrier((proj, reduced_mlp))
         outs = run_block_backward(
-            places, proj, beta_raw, (inverse, carried, qdir, solve, *second[head]), sent, head, dim
+            places_of[head], proj, beta_raw, (inverse, carried, qdir, solve, *second[head]), sent, head, dim
         )
         (d_proj, d_beta), (across_in, core_in, branch_in) = lax.optimization_barrier((outs, flying))
         branch_parts += branch_in

time: 530 us -> 519 us (0.979)
  Pallas kernels: 188 us -> 107 us
  local copies, waits for them, and re-layouts: 16.8 us -> 82.8 us
  waiting for transfers between devices: 194 us -> 200 us
    unnamed x102 -> x398, local copies, waits for them, and re-layouts: 11.7 us -> 80.2 us
    pallas_call x22, Pallas kernels: 136 us -> 73.9 us  [run(): pl.pallas_call(kernel, grid=(1,), in_specs=specs, out_specs=[fixed(shape)...]
    pallas_call x5, Pallas kernels: 18.8 us -> 7.26 us  [grads_into(): pl.pallas_call(kernel, grid=(grid,), in_specs=specs + [ANYWHERE] * len(gi...]
    psum x1, waiting for transfers between devices: 12.2 us -> 21.1 us  [per_device(): result = lax.psum(after(mlp_rows, reduced_mlp, second[-1][0]), 'head')]
    pallas_call x2, Pallas kernels: 19 us -> 13.3 us  [mlp_half(): pl.pallas_call(mlp_forward, grid=(blocks,), in_specs=[pl.BlockSpec((rows,...]
  transfers between devices with their start and end apart: 57 -> 57, of which waited for: 27 -> 29; matrix products, arithmetic and copies ran while one was open for 3% -> 3% of each run, Pallas kernels for 35% -> 20%
where the time goes in v5:
time: 519 us; the launch traced here: 510 us
  waiting for transfers between devices  200 us (39%)
  Pallas kernels  107 us (21%)
  starting transfers between devices  89.6 us (17%)
  local copies, waits for them, and re-layouts  82.8 us (16%)
  between operations  16.2 us (3%)
  other arithmetic  14.2 us (3%)
    ppermute x51, waiting for transfers between devices, xor_move(): lax.ppermute(value, axis, [(at, at ^ mask) for at in range(lax.axis_size(...  145 us
    ppermute x51, starting transfers between devices, xor_move(): lax.ppermute(value, axis, [(at, at ^ mask) for at in range(lax.axis_size(...  88.6 us
    unnamed x398, local copies, waits for them, and re-layouts  80.2 us
    pallas_call x22, Pallas kernels, run(): pl.pallas_call(kernel, grid=(1,), in_specs=specs, out_specs=[fixed(shape)...  73.9 us
    reduce_scatter x1, waiting for transfers between devices, per_device(): lax.psum_scatter(grad_in, 'seq', scatter_dimension=0, tiled=True)  21.3 us
    psum x1, waiting for transfers between devices, per_device(): result = lax.psum(after(mlp_rows, reduced_mlp, second[-1][0]), 'head')  21.1 us
    pallas_call x2, Pallas kernels, mlp_half(): pl.pallas_call(mlp_forward, grid=(blocks,), in_specs=[pl.BlockSpec((rows,...  13.3 us
    pallas_call x1, Pallas kernels, per_device(): pl.pallas_call(mlp_grads, grid=(3 * blocks,), in_specs=[fixed(tall), pl.B...  12.9 us
  transfers between devices with their start and end apart: 57, of which 29 were waited for; matrix products, arithmetic and copies ran while one was open for 3% of the time, Pallas kernels for 20%

profile of v5, /device:TPU:0, one launch (start us, length us, event | category | flops | bytes accessed | tf_op | source)
XLA Modules:
  0.0 510.3 jit_solution(1301029159209869259)
XLA Ops:
  24.4 6.5 %collective-permute-done.4 = bf16[192,384]{1,0:T(8,128)(2,1)S(1)} collective-permute-done((bf16[192,384]{1,0:T(8,128)(2,1)S(1)}, bf16[192,384]{1,0:T(8,128)(2,1)S(1)}, u32[]{:S(2)}, u32[]{:S(2)}) %collective-permute-start.4) | collective-permute-done | bytes 147488 | tf_op jit(solution)/shard_map/ppermute | solution.py:81
  41.1 12.5 %all-gather.4.cloned.1.call-done.w_ref = bf16[1536,1536]{1,0:T(8,128)(2,1)} async-done(((bf16[192,1536]{1,0:T(8,128)(2,1)}), bf16[1536,1536]{1,0:T(8,128)(2,1)}) %all-gather.4.cloned.1.call-update) | async-done | bytes 4718608 | tf_op jit(solution)/shard_map/all_gather | solution.py:735
  57.8 9.2 %block_forward.3 = (f32[512,512]{1,0:T(8,128)S(1)}, bf16[1152,128]{1,0:T(8,128)(2,1)S(1)}, f32[512,128]{1,0:T(8,128)S(1)}, f32[512,512]{1,0:T(8,128)S(1)}, bf16[...) custom-call(s32[4]{0:T(128)S(1)} %get-tuple-element.527.place_ref, ...), custom_call_target="tpu_custom_call" | custom-call | flops 10000000000 | bytes 4194304 | tf_op jit(solution)/shard_map/block_forward/pallas_call | solution.py:598
  74.9 9.6 %block_forward.4 = (f32[512,512]{1,0:T(8,128)S(1)}, bf16[1152,128]{1,0:T(8,128)(2,1)S(1)}, f32[512,128]{1,0:T(8,128)S(1)}, f32[512,512]{1,0:T(8,128)S(1)}, bf16[...) custom-call(s32[4]{0:T(128)S(1)} %get-tuple-element.502.place_ref, ...), custom_call_target="tpu_custom_call" | custom-call | flops 10000000000 | bytes 4194304 | tf_op jit(solution)/shard_map/block_forward/pallas_call | solution.py:598
  90.7 9.2 %block_forward.5 = (f32[512,512]{1,0:T(8,128)S(1)}, bf16[1152,128]{1,0:T(8,128)(2,1)S(1)}, f32[512,128]{1,0:T(8,128)S(1)}, f32[512,512]{1,0:T(8,128)S(1)}, bf16[...) custom-call(s32[4]{0:T(128)S(1)} %get-tuple-element.526.place_ref, ...), custom_call_target="tpu_custom_call" | custom-call | flops 10000000000 | bytes 4194304 | tf_op jit(solution)/shard_map/block_forward/pallas_call | solution.py:598
  118.1 8.0 %collective-permute-done.11 = bf16[2,1152,128]{2,1,0:T(8,128)(2,1)} collective-permute-done((bf16[2,1152,128]{2,1,0:T(8,128)(2,1)S(1)}, bf16[2,1152,128]{2,1,0:T(8,128)(2,1)}, u32[]{:S(2)}, u32[]{:S(2)}) %collective-permute-start.11) | collective-permute-done | bytes 589856 | tf_op jit(solution)/shard_map/ppermute | solution.py:81
  133.8 17.2 %collective-permute-done.13 = bf16[2,1152,128]{2,1,0:T(8,128)(2,1)S(1)} collective-permute-done((bf16[2,1152,128]{2,1,0:T(8,128)(2,1)S(1)}, bf16[2,1152,128]{2,1,0:T(8,128)(2,1)S(1)}, u32[]{:S(2)}, u32[]{:S(2)}) %collective-permute-start.13) | collective-permute-done | bytes 589856 | tf_op jit(solution)/shard_map/ppermute | solution.py:81
  161.6 6.7 %collective-permute-done.16.rest_2_ = bf16[128,384]{1,0:T(8,128)(2,1)S(1)} collective-permute-done((bf16[128,384]{1,0:T(8,128)(2,1)S(1)}, bf16[128,384]{1,0:T(8,128)(2,1)S(1)}, u32[]{:S(2)}, u32[]{:S(2)}) %collective-permute-start.16) | collective-permute-done | bytes 98336 | tf_op jit(solution)/shard_map/ppermute | solution.py:81
  176.4 14.5 %collective-permute-done.18.rest_1_ = bf16[128,1536]{1,0:T(8,128)(2,1)S(1)} collective-permute-done((bf16[128,1536]{1,0:T(8,128)(2,1)}, bf16[128,1536]{1,0:T(8,128)(2,1)S(1)}, u32[]{:S(2)}, u32[]{:S(2)}) %collective-permute-start.18) | collective-permute-done | bytes 393248 | tf_op jit(solution)/shard_map/ppermute | solution.py:81
  197.7 6.7 %mlp_forward.2 = (bf16[3,256,1024]{2,1,0:T(8,128)(2,1)S(1)}, bf16[128,1536]{1,0:T(8,128)(2,1)S(1)}, bf16[128,1536]{1,0:T(8,128)(2,1)S(1)}) custom-call(bf16[512,1536]{1,0:T(8,128)(2,1)S(1)} %copy-done.12, bf16[1536,3072]{1,0:T(8,128)(2,1)S(1)} %copy-done, bf16[1536,3072]{1,0:T(8,128)(2,1)S(1)} %copy-done, bf16[1536,3072]{1,0:T(8,128)(2,1)S(1)} %copy-done, ...), custom_call_target="tpu_custom_call" | custom-call | flops 5000000000 | bytes 16777216 | tf_op jit(solution)/shard_map/mlp_forward/pallas_call | solution.py:827
  205.2 6.5 %collective-permute-start.21 = (bf16[128,1536]{1,0:T(8,128)(2,1)}, bf16[128,1536]{1,0:T(8,128)(2,1)S(1)}, u32[]{:S(2)}, u32[]{:S(2)}) collective-permute-start(bf16[128,1536]{1,0:T(8,128)(2,1)} %copy-done.76), channel_id=1, source_target_pairs={{0,8},{8,0},{16,24},{24,16},{1,9},{9,1},{17,25},{25,17},{2,10},{10... | collective-permute-start | bytes 1179656 | tf_op jit(solution)/shard_map/ppermute | solution.py:81
  211.6 6.6 %mlp_forward.3 = (bf16[3,256,1024]{2,1,0:T(8,128)(2,1)S(1)}, bf16[128,1536]{1,0:T(8,128)(2,1)S(1)}, bf16[128,1536]{1,0:T(8,128)(2,1)S(1)}) custom-call(bf16[512,1536]{1,0:T(8,128)(2,1)S(1)} %copy-done.12, bf16[1536,3072]{1,0:T(8,128)(2,1)S(1)} %copy-done.1, bf16[1536,3072]{1,0:T(8,128)(2,1)S(1)} %copy-done.1, bf16[1536,3072]{1,0:T(8,128)(2,1)S(1)} %copy-done.1, ...), custom_call_target="tpu_custom_call" | custom-call | flops 5000000000 | bytes 16777216 | tf_op jit(solution)/shard_map/mlp_forward/pallas_call | solution.py:827
  223.9 12.9 %mlp_grads.1 = (bf16[1536,3072]{1,0:T(8,128)(2,1)}, bf16[128,1536]{1,0:T(8,128)(2,1)S(1)}, bf16[128,1536]{1,0:T(8,128)(2,1)S(1)}, bf16[128,1536]{1,0:T(8,128)(2,1)S(1)}, bf16[128,1536]{1,0:T(8,128)(2,1)S(1)}) custom-call(bf16[512,1536]{1,0:T(8,128)(2,1)S(1)} %copy-done.12, bf16[3,256,1024]{2,1,0:T(8,128)(2,1)S(1)} %get-tuple-element.308.near_ref, ...), custom_call_target="tpu_custom_call" | custom-call | flops 10000000000 | bytes 16777216 | tf_op jit(solution)/shard_map/mlp_grads/pallas_call | solution.py:853
  239.8 7.8 %collective-permute-done.22.rest_2_ = bf16[128,1536]{1,0:T(8,128)(2,1)S(1)} collective-permute-done((bf16[128,1536]{1,0:T(8,128)(2,1)S(1)}, bf16[128,1536]{1,0:T(8,128)(2,1)S(1)}, u32[]{:S(2)}, u32[]{:S(2)}) %collective-permute-start.22) | collective-permute-done | bytes 393248 | tf_op jit(solution)/shard_map/ppermute | solution.py:81
  258.7 7.4 %collective-permute-start.24 = (bf16[128,384]{1,0:T(8,128)(2,1)S(1)}, bf16[128,384]{1,0:T(8,128)(2,1)S(1)}, u32[]{:S(2)}, u32[]{:S(2)}) collective-permute-start(bf16[128,384]{1,0:T(8,128)(2,1)S(1)} %get-tuple-element.338), channel_id=1, source_target_pairs={{0,8},{8,0},{16,24},{24,16},{1,9},{9,1},{17,25},{25,17},{2,10},{10... | collective-permute-start | bytes 294920 | tf_op jit(solution)/shard_map/ppermute | solution.py:81
  269.6 6.1 %collective-permute-done.25.rest_2_ = bf16[128,384]{1,0:T(8,128)(2,1)S(1)} collective-permute-done((bf16[128,384]{1,0:T(8,128)(2,1)S(1)}, bf16[128,384]{1,0:T(8,128)(2,1)S(1)}, u32[]{:S(2)}, u32[]{:S(2)}) %collective-permute-start.25) | collective-permute-done | bytes 98336 | tf_op jit(solution)/shard_map/ppermute | solution.py:81
  291.4 11.8 %collective-permute-done.30.rest_4_ = bf16[64,1536]{1,0:T(8,128)(2,1)S(1)} collective-permute-done((bf16[64,1536]{1,0:T(8,128)(2,1)S(1)}, bf16[64,1536]{1,0:T(8,128)(2,1)S(1)}, u32[]{:S(2)}, u32[]{:S(2)}) %collective-permute-start.30) | collective-permute-done | bytes 196640 | tf_op jit(solution)/shard_map/ppermute | solution.py:81
  311.1 14.3 %collective-permute-done.32 = bf16[2,1152,128]{2,1,0:T(8,128)(2,1)S(1)} collective-permute-done((bf16[2,1152,128]{2,1,0:T(8,128)(2,1)S(1)}, bf16[2,1152,128]{2,1,0:T(8,128)(2,1)S(1)}, u32[]{:S(2)}, u32[]{:S(2)}) %collective-permute-start.32) | collective-permute-done | bytes 589856 | tf_op jit(solution)/shard_map/ppermute | solution.py:81
  366.8 5.3 %block_backward.4 = (bf16[512,512]{1,0:T(8,128)(2,1)S(1)}, bf16[512,128]{1,0:T(8,128)(2,1)S(1)}) custom-call(s32[4]{0:T(128)S(1)} %get-tuple-element.502.place_ref, f32[512,512]{1,0:T(8,128)S(1)} %copy-done.94, f32[512,128]{1,0:T(8,128)S(1)} %copy-done.85, bf16[512,512]{1,0:T(8,128)(2,1)S(1)} %copy-done.104, bf16[512,512]{1,0:T(8,128)(2,1)S(1)} %copy-done.106, ...), custom_call_target="tpu_custom_call" | custom-call | flops 5000000000 | bytes 4194304 | tf_op jit(solution)/shard_map/block_backward/pallas_call | solution.py:598
  408.4 21.1 %all-reduce.4.cloned.1.call-done = bf16[512,1536]{1,0:T(8,128)(2,1)} async-done(((bf16[512,1536]{1,0:T(8,128)(2,1)}), bf16[512,1536]{1,0:T(8,128)(2,1)}) %all-reduce.4.cloned.1.call-update) | async-done | bytes 1572880 | tf_op jit(solution)/shard_map/psum | solution.py:920
  434.3 14.2 %collective-permute-done.45.rest_1_ = bf16[128,1536]{1,0:T(8,128)(2,1)S(1)} collective-permute-done((bf16[128,1536]{1,0:T(8,128)(2,1)S(1)}, bf16[128,1536]{1,0:T(8,128)(2,1)S(1)}, u32[]{:S(2)}, u32[]{:S(2)}) %collective-permute-start.45) | collective-permute-done | bytes 393248 | tf_op jit(solution)/shard_map/ppermute | solution.py:81
  448.4 11.1 %collective-permute-done.46.rest_2_ = bf16[128,1536]{1,0:T(8,128)(2,1)S(1)} collective-permute-done((bf16[128,1536]{1,0:T(8,128)(2,1)S(1)}, bf16[128,1536]{1,0:T(8,128)(2,1)S(1)}, u32[]{:S(2)}, u32[]{:S(2)}) %collective-permute-start.46) | collective-permute-done | bytes 393248 | tf_op jit(solution)/shard_map/ppermute | solution.py:81
  460.3 8.1 %collective-permute-start.48 = (bf16[128,1536]{1,0:T(8,128)(2,1)S(1)}, bf16[128,1536]{1,0:T(8,128)(2,1)S(1)}, u32[]{:S(2)}, u32[]{:S(2)}) collective-permute-start(bf16[128,1536]{1,0:T(8,128)(2,1)S(1)} %token_grad.1.rest_0_), channel_id=1, source_target_pairs={{0,8},{8,0},{16,24},{24,16},{1,9},{9,1},{17,25},{25,17},{2,10},{10... | collective-permute-start | bytes 1179656 | tf_op jit(solution)/shard_map/ppermute | solution.py:81
  472.3 21.3 %reduce-scatter.5.cloned.1.call-done.in_ref = bf16[192,2048]{1,0:T(8,128)(2,1)} async-done(((bf16[1536,2048]{1,0:T(8,128)(2,1)}), bf16[192,2048]{1,0:T(8,128)(2,1)}) %reduce-scatter.5.cloned.1.call-update) | async-done | bytes 786448 | tf_op jit(solution)/shard_map/reduce_scatter | solution.py:1034
  (560 shorter events, 239.7 us)
Async XLA Ops:
  7.2 46.5 %all-gather.4.cloned.1.call-start = ((), (), s32[]{:S(2)}) async-start(), calls=%async_computation.2 | async-start | bytes 5308416 | tf_op jit(solution)/shard_map/all_gather | solution.py:735
  11.8 114.2 %all-gather.6.cloned.1.call-start = ((), (), s32[]{:S(2)}) async-start(), calls=%async_computation.3 | async-start | bytes 5308416 | tf_op jit(solution)/shard_map/all_gather | solution.py:762
  53.7 138.0 %all-gather.8.cloned.1.call-start = ((), (), s32[]{:S(2)}) async-start(), calls=%async_computation.4 | async-start | bytes 10616832 | tf_op jit(solution)/shard_map/all_gather | solution.py:806
  126.1 212.5 %reduce-scatter.3.cloned.1.call-start = ((), (), s32[]{:S(2)}) async-start(), calls=%async_computation.5 | async-start | bytes 10616832 | tf_op jit(solution)/shard_map/reduce_scatter | solution.py:873
  127.8 23.2 %collective-permute-start.13 = (bf16[2,1152,128]{2,1,0:T(8,128)(2,1)S(1)}, bf16[2,1152,128]{2,1,0:T(8,128)(2,1)S(1)}, u32[]{:S(2)}, u32[]{:S(2)}) collective-permute-start(bf16[2,1152,128]{2,1,0:T(8,128)(2,1)S(1)} %pad_maximum_fusion.9), channel_id=1, source_target_pairs={{0,4},{1,5},{2,6},{3,7},{4,0},{5,1},{6,2},{7,3},{8,12},{9,13},{10,... | collective-permute-start | bytes 1769480 | tf_op jit(solution)/shard_map/ppermute | solution.py:81
  171.7 19.2 %collective-permute-start.18 = (bf16[128,1536]{1,0:T(8,128)(2,1)}, bf16[128,1536]{1,0:T(8,128)(2,1)S(1)}, u32[]{:S(2)}, u32[]{:S(2)}) collective-permute-start(bf16[128,1536]{1,0:T(8,128)(2,1)} %get-tuple-element.304.rest_0_), channel_id=1, source_target_pairs={{0,8},{8,0},{16,24},{24,16},{1,9},{9,1},{17,25},{25,17},{2,10},{10... | collective-permute-start | bytes 1179656 | tf_op jit(solution)/shard_map/ppermute | solution.py:81
  174.0 31.2 %collective-permute-start.19 = (bf16[128,1536]{1,0:T(8,128)(2,1)}, bf16[128,1536]{1,0:T(8,128)(2,1)}, u32[]{:S(2)}, u32[]{:S(2)}) collective-permute-start(bf16[128,1536]{1,0:T(8,128)(2,1)} %get-tuple-element.304.rest_0_), channel_id=1, source_target_pairs={{0,16},{8,24},{16,0},{24,8},{1,17},{9,25},{17,1},{25,9},{2,18},{10... | collective-permute-start | bytes 1179656 | tf_op jit(solution)/shard_map/ppermute | solution.py:81
  174.9 30.3 %collective-permute-start.20 = (bf16[128,1536]{1,0:T(8,128)(2,1)}, bf16[128,1536]{1,0:T(8,128)(2,1)}, u32[]{:S(2)}, u32[]{:S(2)}) collective-permute-start(bf16[128,1536]{1,0:T(8,128)(2,1)} %get-tuple-element.304.rest_0_), channel_id=1, source_target_pairs={{0,24},{8,16},{16,8},{24,0},{1,25},{9,17},{17,9},{25,1},{2,26},{10... | collective-permute-start | bytes 1179656 | tf_op jit(solution)/shard_map/ppermute | solution.py:81
  219.8 27.9 %collective-permute-start.22 = (bf16[128,1536]{1,0:T(8,128)(2,1)S(1)}, bf16[128,1536]{1,0:T(8,128)(2,1)S(1)}, u32[]{:S(2)}, u32[]{:S(2)}) collective-permute-start(bf16[128,1536]{1,0:T(8,128)(2,1)S(1)} %get-tuple-element.326), channel_id=1, source_target_pairs={{0,16},{8,24},{16,0},{24,8},{1,17},{9,25},{17,1},{25,9},{2,18},{10... | collective-permute-start | bytes 1179656 | tf_op jit(solution)/shard_map/ppermute | solution.py:81
  222.5 26.0 %collective-permute-start.23 = (bf16[128,1536]{1,0:T(8,128)(2,1)S(1)}, bf16[128,1536]{1,0:T(8,128)(2,1)S(1)}, u32[]{:S(2)}, u32[]{:S(2)}) collective-permute-start(bf16[128,1536]{1,0:T(8,128)(2,1)S(1)} %get-tuple-element.327), channel_id=1, source_target_pairs={{0,24},{8,16},{16,8},{24,0},{1,25},{9,17},{17,9},{25,1},{2,26},{10... | collective-permute-start | bytes 1179656 | tf_op jit(solution)/shard_map/ppermute | solution.py:81
  249.2 180.3 %all-reduce.4.cloned.1.call-start = ((), (), s32[]{:S(2)}) async-start(), calls=%async_computation.6 | async-start | bytes 3145728 | tf_op jit(solution)/shard_map/psum | solution.py:920
  289.1 22.0 %collective-permute-start.33 = (bf16[64,1536]{1,0:T(8,128)(2,1)S(1)}, bf16[64,1536]{1,0:T(8,128)(2,1)S(1)}, u32[]{:S(2)}, u32[]{:S(2)}) collective-permute-start(bf16[64,1536]{1,0:T(8,128)(2,1)S(1)} %get-tuple-element.347.rest_1_), channel_id=1, source_target_pairs={{0,16},{8,24},{16,0},{24,8},{1,17},{9,25},{17,1},{25,9},{2,18},{10... | collective-permute-start | bytes 589832 | tf_op jit(solution)/shard_map/ppermute | solution.py:81
  303.3 22.1 %collective-permute-start.31 = (bf16[4,1152,128]{2,1,0:T(8,128)(2,1)S(1)}, bf16[4,1152,128]{2,1,0:T(8,128)(2,1)S(1)}, u32[]{:S(2)}, u32[]{:S(2)}) collective-permute-start(bf16[4,1152,128]{2,1,0:T(8,128)(2,1)S(1)} %get-tuple-element.371), channel_id=1, source_target_pairs={{0,1},{1,0},{2,3},{3,2},{4,5},{5,4},{6,7},{7,6},{8,9},{9,8},{10,11... | collective-permute-start | bytes 3538952 | tf_op jit(solution)/shard_map/ppermute | solution.py:81
  303.9 21.5 %collective-permute-start.32 = (bf16[2,1152,128]{2,1,0:T(8,128)(2,1)S(1)}, bf16[2,1152,128]{2,1,0:T(8,128)(2,1)S(1)}, u32[]{:S(2)}, u32[]{:S(2)}) collective-permute-start(bf16[2,1152,128]{2,1,0:T(8,128)(2,1)S(1)} %get-tuple-element.509), channel_id=1, source_target_pairs={{0,4},{1,5},{2,6},{3,7},{4,0},{5,1},{6,2},{7,3},{8,12},{9,13},{10,... | collective-permute-start | bytes 1769480 | tf_op jit(solution)/shard_map/ppermute | solution.py:81
  329.7 22.0 %collective-permute-start.36 = (bf16[4,1152,128]{2,1,0:T(8,128)(2,1)}, bf16[4,1152,128]{2,1,0:T(8,128)(2,1)}, u32[]{:S(2)}, u32[]{:S(2)}) collective-permute-start(bf16[4,1152,128]{2,1,0:T(8,128)(2,1)} %get-tuple-element.389), channel_id=1, source_target_pairs={{0,1},{1,0},{2,3},{3,2},{4,5},{5,4},{6,7},{7,6},{8,9},{9,8},{10,11... | collective-permute-start | bytes 3538952 | tf_op jit(solution)/shard_map/ppermute | solution.py:81
  331.1 20.7 %collective-permute-start.35 = (bf16[2,1152,128]{2,1,0:T(8,128)(2,1)}, bf16[2,1152,128]{2,1,0:T(8,128)(2,1)}, u32[]{:S(2)}, u32[]{:S(2)}) collective-permute-start(bf16[2,1152,128]{2,1,0:T(8,128)(2,1)} %get-tuple-element.507), channel_id=1, source_target_pairs={{0,4},{1,5},{2,6},{3,7},{4,0},{5,1},{6,2},{7,3},{8,12},{9,13},{10,... | collective-permute-start | bytes 1769480 | tf_op jit(solution)/shard_map/ppermute | solution.py:81
  335.3 36.8 %collective-permute-start.40 = (bf16[64,1536]{1,0:T(8,128)(2,1)S(1)}, bf16[64,1536]{1,0:T(8,128)(2,1)}, u32[]{:S(2)}, u32[]{:S(2)}) collective-permute-start(bf16[64,1536]{1,0:T(8,128)(2,1)S(1)} %copy-done.54), channel_id=1, source_target_pairs={{0,24},{8,16},{16,8},{24,0},{1,25},{9,17},{17,9},{25,1},{2,26},{10... | collective-permute-start | bytes 589832 | tf_op jit(solution)/shard_map/ppermute | solution.py:81
  359.8 133.7 %reduce-scatter.5.cloned.1.call-start = ((), (), s32[]{:S(2)}) async-start(), calls=%async_computation.7 | async-start | bytes 7077888 | tf_op jit(solution)/shard_map/reduce_scatter | solution.py:1034
  429.5 18.9 %collective-permute-start.45 = (bf16[128,1536]{1,0:T(8,128)(2,1)S(1)}, bf16[128,1536]{1,0:T(8,128)(2,1)S(1)}, u32[]{:S(2)}, u32[]{:S(2)}) collective-permute-start(bf16[128,1536]{1,0:T(8,128)(2,1)S(1)} %copy-done.75), channel_id=1, source_target_pairs={{0,8},{8,0},{16,24},{24,16},{1,9},{9,1},{17,25},{25,17},{2,10},{10... | collective-permute-start | bytes 1179656 | tf_op jit(solution)/shard_map/ppermute | solution.py:81
  429.7 29.8 %collective-permute-start.46 = (bf16[128,1536]{1,0:T(8,128)(2,1)S(1)}, bf16[128,1536]{1,0:T(8,128)(2,1)S(1)}, u32[]{:S(2)}, u32[]{:S(2)}) collective-permute-start(bf16[128,1536]{1,0:T(8,128)(2,1)S(1)} %get-tuple-element.446), channel_id=1, source_target_pairs={{0,16},{8,24},{16,0},{24,8},{1,17},{9,25},{17,1},{25,9},{2,18},{10... | collective-permute-start | bytes 1179656 | tf_op jit(solution)/shard_map/ppermute | solution.py:81
  432.1 27.4 %collective-permute-start.47 = (bf16[128,1536]{1,0:T(8,128)(2,1)S(1)}, bf16[128,1536]{1,0:T(8,128)(2,1)S(1)}, u32[]{:S(2)}, u32[]{:S(2)}) collective-permute-start(bf16[128,1536]{1,0:T(8,128)(2,1)S(1)} %get-tuple-element.447), channel_id=1, source_target_pairs={{0,24},{8,16},{16,8},{24,0},{1,25},{9,17},{17,9},{25,1},{2,26},{10... | collective-permute-start | bytes 1179656 | tf_op jit(solution)/shard_map/ppermute | solution.py:81
  460.3 35.6 %collective-permute-start.48 = (bf16[128,1536]{1,0:T(8,128)(2,1)S(1)}, bf16[128,1536]{1,0:T(8,128)(2,1)S(1)}, u32[]{:S(2)}, u32[]{:S(2)}) collective-permute-start(bf16[128,1536]{1,0:T(8,128)(2,1)S(1)} %token_grad.1.rest_0_), channel_id=1, source_target_pairs={{0,8},{8,0},{16,24},{24,16},{1,9},{9,1},{17,25},{25,17},{2,10},{10... | collective-permute-start | bytes 1179656 | tf_op jit(solution)/shard_map/ppermute | solution.py:81
  468.3 29.8 %collective-permute-start.49 = (bf16[128,1536]{1,0:T(8,128)(2,1)S(1)}, bf16[128,1536]{1,0:T(8,128)(2,1)S(1)}, u32[]{:S(2)}, u32[]{:S(2)}) collective-permute-start(bf16[128,1536]{1,0:T(8,128)(2,1)S(1)} %token_grad.1.rest_0_), channel_id=1, source_target_pairs={{0,16},{8,24},{16,0},{24,8},{1,17},{9,25},{17,1},{25,9},{2,18},{10... | collective-permute-start | bytes 1179656 | tf_op jit(solution)/shard_map/ppermute | solution.py:81
  469.2 29.0 %collective-permute-start.50 = (bf16[128,1536]{1,0:T(8,128)(2,1)S(1)}, bf16[128,1536]{1,0:T(8,128)(2,1)S(1)}, u32[]{:S(2)}, u32[]{:S(2)}) collective-permute-start(bf16[128,1536]{1,0:T(8,128)(2,1)S(1)} %token_grad.1.rest_0_), channel_id=1, source_target_pairs={{0,24},{8,16},{16,8},{24,0},{1,25},{9,17},{17,9},{25,1},{2,26},{10... | collective-permute-start | bytes 1179656 | tf_op jit(solution)/shard_map/ppermute | solution.py:81
  (230 other events, 1545.9 us)
Sparse Core Ops, SparseCore 0:
  12.0 41.6 all-gather.3
  56.1 44.4 all-gather.5
  126.2 64.1 all-gather.7
  249.3 86.3 reduce-scatter.2
  359.9 69.5 all-reduce.3
  432.7 60.7 reduce-scatter.4

commit v6 on v5

--- a/solution.py
+++ b/solution.py
@@ -13,7 +13,7 @@
 LOG2E = 1.4426950408889634
 LOW = jnp.bfloat16
 WIDE = jnp.float32
-VMEM_BYTES = 40 * 2**20
+VMEM_BYTES = 36 * 2**20
 
 
 def mm(left, right, ta=False, tb=False):

time: 519 us -> 523 us (level)
  no operation moved by 1% of the time
where the time goes in v6:
time: 523 us; the launch traced here: 515 us
  waiting for transfers between devices  200 us (38%)
  Pallas kernels  107 us (20%)
  starting transfers between devices  90.3 us (17%)
  local copies, waits for them, and re-layouts  85.2 us (16%)
  between operations  16.2 us (3%)
  other arithmetic  15.5 us (3%)
    ppermute x51, waiting for transfers between devices, xor_move(): lax.ppermute(value, axis, [(at, at ^ mask) for at in range(lax.axis_size(...  142 us
    ppermute x51, starting transfers between devices, xor_move(): lax.ppermute(value, axis, [(at, at ^ mask) for at in range(lax.axis_size(...  89.3 us
    unnamed x398, local copies, waits for them, and re-layouts  82.6 us
    pallas_call x22, Pallas kernels, run(): pl.pallas_call(kernel, grid=(1,), in_specs=specs, out_specs=[fixed(shape)...  74.5 us
    psum x1, waiting for transfers between devices, per_device(): result = lax.psum(after(mlp_rows, reduced_mlp, second[-1][0]), 'head')  24.1 us
    reduce_scatter x1, waiting for transfers between devices, per_device(): lax.psum_scatter(grad_in, 'seq', scatter_dimension=0, tiled=True)  21.3 us
    pallas_call x2, Pallas kernels, mlp_half(): pl.pallas_call(mlp_forward, grid=(blocks,), in_specs=[pl.BlockSpec((rows,...  13.3 us
    all_gather x1, waiting for transfers between devices, per_device(): w_in = lax.all_gather(packed, 'seq', axis=0, tiled=True)  12.4 us
  transfers between devices with their start and end apart: 57, of which 29 were waited for; matrix products, arithmetic and copies ran while one was open for 3% of the time, Pallas kernels for 20%

profile of v6, /device:TPU:0, one launch (start us, length us, event | category | flops | bytes accessed | tf_op | source)
XLA Modules:
  0.0 514.7 jit_solution(14883998316338984902)
XLA Ops:
  24.4 6.5 %collective-permute-done.4 = bf16[192,384]{1,0:T(8,128)(2,1)S(1)} collective-permute-done((bf16[192,384]{1,0:T(8,128)(2,1)S(1)}, bf16[192,384]{1,0:T(8,128)(2,1)S(1)}, u32[]{:S(2)}, u32[]{:S(2)}) %collective-permute-start.4) | collective-permute-done | bytes 147488 | tf_op jit(solution)/shard_map/ppermute | solution.py:81
  41.2 12.4 %all-gather.4.cloned.1.call-done.w_ref = bf16[1536,1536]{1,0:T(8,128)(2,1)} async-done(((bf16[192,1536]{1,0:T(8,128)(2,1)}), bf16[1536,1536]{1,0:T(8,128)(2,1)}) %all-gather.4.cloned.1.call-update) | async-done | bytes 4718608 | tf_op jit(solution)/shard_map/all_gather | solution.py:735
  58.7 9.2 %block_forward.3 = (f32[512,512]{1,0:T(8,128)S(1)}, bf16[1152,128]{1,0:T(8,128)(2,1)S(1)}, f32[512,128]{1,0:T(8,128)S(1)}, f32[512,512]{1,0:T(8,128)S(1)}, bf16[...) custom-call(s32[4]{0:T(128)S(1)} %get-tuple-element.527.place_ref, ...), custom_call_target="tpu_custom_call" | custom-call | flops 10000000000 | bytes 4194304 | tf_op jit(solution)/shard_map/block_forward/pallas_call | solution.py:598
  75.8 9.6 %block_forward.4 = (f32[512,512]{1,0:T(8,128)S(1)}, bf16[1152,128]{1,0:T(8,128)(2,1)S(1)}, f32[512,128]{1,0:T(8,128)S(1)}, f32[512,512]{1,0:T(8,128)S(1)}, bf16[...) custom-call(s32[4]{0:T(128)S(1)} %get-tuple-element.502.place_ref, ...), custom_call_target="tpu_custom_call" | custom-call | flops 10000000000 | bytes 4194304 | tf_op jit(solution)/shard_map/block_forward/pallas_call | solution.py:598
  92.4 9.2 %block_forward.5 = (f32[512,512]{1,0:T(8,128)S(1)}, bf16[1152,128]{1,0:T(8,128)(2,1)S(1)}, f32[512,128]{1,0:T(8,128)S(1)}, f32[512,512]{1,0:T(8,128)S(1)}, bf16[...) custom-call(s32[4]{0:T(128)S(1)} %get-tuple-element.526.place_ref, ...), custom_call_target="tpu_custom_call" | custom-call | flops 10000000000 | bytes 4194304 | tf_op jit(solution)/shard_map/block_forward/pallas_call | solution.py:598
  118.2 7.3 %collective-permute-done.11 = bf16[2,1152,128]{2,1,0:T(8,128)(2,1)S(1)} collective-permute-done((bf16[2,1152,128]{2,1,0:T(8,128)(2,1)S(1)}, bf16[2,1152,128]{2,1,0:T(8,128)(2,1)S(1)}, u32[]{:S(2)}, u32[]{:S(2)}) %collective-permute-start.11) | collective-permute-done | bytes 589856 | tf_op jit(solution)/shard_map/ppermute | solution.py:81
  133.3 17.1 %collective-permute-done.13 = bf16[2,1152,128]{2,1,0:T(8,128)(2,1)S(1)} collective-permute-done((bf16[2,1152,128]{2,1,0:T(8,128)(2,1)S(1)}, bf16[2,1152,128]{2,1,0:T(8,128)(2,1)S(1)}, u32[]{:S(2)}, u32[]{:S(2)}) %collective-permute-start.13) | collective-permute-done | bytes 589856 | tf_op jit(solution)/shard_map/ppermute | solution.py:81
  160.9 6.7 %collective-permute-done.16.rest_2_ = bf16[128,384]{1,0:T(8,128)(2,1)S(1)} collective-permute-done((bf16[128,384]{1,0:T(8,128)(2,1)S(1)}, bf16[128,384]{1,0:T(8,128)(2,1)S(1)}, u32[]{:S(2)}, u32[]{:S(2)}) %collective-permute-start.16) | collective-permute-done | bytes 98336 | tf_op jit(solution)/shard_map/ppermute | solution.py:81
  175.8 14.5 %collective-permute-done.18.rest_1_ = bf16[128,1536]{1,0:T(8,128)(2,1)S(1)} collective-permute-done((bf16[128,1536]{1,0:T(8,128)(2,1)}, bf16[128,1536]{1,0:T(8,128)(2,1)S(1)}, u32[]{:S(2)}, u32[]{:S(2)}) %collective-permute-start.18) | collective-permute-done | bytes 393248 | tf_op jit(solution)/shard_map/ppermute | solution.py:81
  197.5 6.7 %mlp_forward.2 = (bf16[3,256,1024]{2,1,0:T(8,128)(2,1)S(1)}, bf16[128,1536]{1,0:T(8,128)(2,1)S(1)}, bf16[128,1536]{1,0:T(8,128)(2,1)S(1)}) custom-call(bf16[512,1536]{1,0:T(8,128)(2,1)S(1)} %copy-done.10, bf16[1536,3072]{1,0:T(8,128)(2,1)S(1)} %copy-done, bf16[1536,3072]{1,0:T(8,128)(2,1)S(1)} %copy-done, bf16[1536,3072]{1,0:T(8,128)(2,1)S(1)} %copy-done, ...), custom_call_target="tpu_custom_call" | custom-call | flops 5000000000 | bytes 16777216 | tf_op jit(solution)/shard_map/mlp_forward/pallas_call | solution.py:827
  204.2 6.9 %collective-permute-start.21 = (bf16[128,1536]{1,0:T(8,128)(2,1)S(1)}, bf16[128,1536]{1,0:T(8,128)(2,1)S(1)}, u32[]{:S(2)}, u32[]{:S(2)}) collective-permute-start(bf16[128,1536]{1,0:T(8,128)(2,1)S(1)} %get-tuple-element.317), channel_id=1, source_target_pairs={{0,8},{8,0},{16,24},{24,16},{1,9},{9,1},{17,25},{25,17},{2,10},{10... | collective-permute-start | bytes 1179656 | tf_op jit(solution)/shard_map/ppermute | solution.py:81
  211.1 6.7 %mlp_forward.3 = (bf16[3,256,1024]{2,1,0:T(8,128)(2,1)S(1)}, bf16[128,1536]{1,0:T(8,128)(2,1)S(1)}, bf16[128,1536]{1,0:T(8,128)(2,1)S(1)}) custom-call(bf16[512,1536]{1,0:T(8,128)(2,1)S(1)} %copy-done.10, bf16[1536,3072]{1,0:T(8,128)(2,1)S(1)} %copy-done.1, bf16[1536,3072]{1,0:T(8,128)(2,1)S(1)} %copy-done.1, bf16[1536,3072]{1,0:T(8,128)(2,1)S(1)} %copy-done.1, ...), custom_call_target="tpu_custom_call" | custom-call | flops 5000000000 | bytes 16777216 | tf_op jit(solution)/shard_map/mlp_forward/pallas_call | solution.py:827
  223.1 12.1 %mlp_grads.1 = (bf16[1536,3072]{1,0:T(8,128)(2,1)S(1)}, bf16[128,1536]{1,0:T(8,128)(2,1)S(1)}, bf16[128,1536]{1,0:T(8,128)(2,1)S(1)}, bf16[128,1536]{1,0:T(8,128)(2,1)S(1)}, bf16[128,1536]{1,0:T(8,128)(2,1)S(1)}) custom-call(bf16[512,1536]{1,0:T(8,128)(2,1)S(1)} %copy-done.10, bf16[3,256,1024]{2,1,0:T(8,128)(2,1)S(1)} %get-tuple-element.308.near_ref, ...), custom_call_target="tpu_custom_call" | custom-call | flops 10000000000 | bytes 16777216 | tf_op jit(solution)/shard_map/mlp_grads/pallas_call | solution.py:853
  259.9 7.3 %collective-permute-start.24 = (bf16[128,384]{1,0:T(8,128)(2,1)S(1)}, bf16[128,384]{1,0:T(8,128)(2,1)S(1)}, u32[]{:S(2)}, u32[]{:S(2)}) collective-permute-start(bf16[128,384]{1,0:T(8,128)(2,1)S(1)} %get-tuple-element.338), channel_id=1, source_target_pairs={{0,8},{8,0},{16,24},{24,16},{1,9},{9,1},{17,25},{25,17},{2,10},{10... | collective-permute-start | bytes 294920 | tf_op jit(solution)/shard_map/ppermute | solution.py:81
  270.6 6.1 %collective-permute-done.25.rest_2_ = bf16[128,384]{1,0:T(8,128)(2,1)S(1)} collective-permute-done((bf16[128,384]{1,0:T(8,128)(2,1)S(1)}, bf16[128,384]{1,0:T(8,128)(2,1)S(1)}, u32[]{:S(2)}, u32[]{:S(2)}) %collective-permute-start.25) | collective-permute-done | bytes 98336 | tf_op jit(solution)/shard_map/ppermute | solution.py:81
  292.4 11.8 %collective-permute-done.30.rest_4_ = bf16[64,1536]{1,0:T(8,128)(2,1)S(1)} collective-permute-done((bf16[64,1536]{1,0:T(8,128)(2,1)S(1)}, bf16[64,1536]{1,0:T(8,128)(2,1)S(1)}, u32[]{:S(2)}, u32[]{:S(2)}) %collective-permute-start.30) | collective-permute-done | bytes 196640 | tf_op jit(solution)/shard_map/ppermute | solution.py:81
  304.9 5.2 %collective-permute-start.32 = (bf16[2,1152,128]{2,1,0:T(8,128)(2,1)S(1)}, bf16[2,1152,128]{2,1,0:T(8,128)(2,1)S(1)}, u32[]{:S(2)}, u32[]{:S(2)}) collective-permute-start(bf16[2,1152,128]{2,1,0:T(8,128)(2,1)S(1)} %get-tuple-element.509), channel_id=1, source_target_pairs={{0,4},{1,5},{2,6},{3,7},{4,0},{5,1},{6,2},{7,3},{8,12},{9,13},{10,... | collective-permute-start | bytes 1769480 | tf_op jit(solution)/shard_map/ppermute | solution.py:81
  313.6 16.8 %collective-permute-done.32 = bf16[2,1152,128]{2,1,0:T(8,128)(2,1)S(1)} collective-permute-done((bf16[2,1152,128]{2,1,0:T(8,128)(2,1)S(1)}, bf16[2,1152,128]{2,1,0:T(8,128)(2,1)S(1)}, u32[]{:S(2)}, u32[]{:S(2)}) %collective-permute-start.32) | collective-permute-done | bytes 589856 | tf_op jit(solution)/shard_map/ppermute | solution.py:81
  371.4 5.3 %block_backward.4 = (bf16[512,512]{1,0:T(8,128)(2,1)S(1)}, bf16[512,128]{1,0:T(8,128)(2,1)S(1)}) custom-call(s32[4]{0:T(128)S(1)} %get-tuple-element.502.place_ref, f32[512,512]{1,0:T(8,128)S(1)} %copy-done.93, f32[512,128]{1,0:T(8,128)S(1)} %copy-done.83, bf16[512,512]{1,0:T(8,128)(2,1)S(1)} %copy-done.103, bf16[512,512]{1,0:T(8,128)(2,1)S(1)} %copy-done.105, ...), custom_call_target="tpu_custom_call" | custom-call | flops 5000000000 | bytes 4194304 | tf_op jit(solution)/shard_map/block_backward/pallas_call | solution.py:598
  410.0 24.1 %all-reduce.4.cloned.1.call-done = bf16[512,1536]{1,0:T(8,128)(2,1)} async-done(((bf16[512,1536]{1,0:T(8,128)(2,1)}), bf16[512,1536]{1,0:T(8,128)(2,1)}) %all-reduce.4.cloned.1.call-update) | async-done | bytes 1572880 | tf_op jit(solution)/shard_map/psum | solution.py:920
  440.1 11.4 %collective-permute-done.45.rest_1_ = bf16[128,1536]{1,0:T(8,128)(2,1)S(1)} collective-permute-done((bf16[128,1536]{1,0:T(8,128)(2,1)S(1)}, bf16[128,1536]{1,0:T(8,128)(2,1)S(1)}, u32[]{:S(2)}, u32[]{:S(2)}) %collective-permute-start.45) | collective-permute-done | bytes 393248 | tf_op jit(solution)/shard_map/ppermute | solution.py:81
  451.5 13.2 %collective-permute-done.46.rest_2_ = bf16[128,1536]{1,0:T(8,128)(2,1)S(1)} collective-permute-done((bf16[128,1536]{1,0:T(8,128)(2,1)S(1)}, bf16[128,1536]{1,0:T(8,128)(2,1)S(1)}, u32[]{:S(2)}, u32[]{:S(2)}) %collective-permute-start.46) | collective-permute-done | bytes 393248 | tf_op jit(solution)/shard_map/ppermute | solution.py:81
  465.4 7.4 %collective-permute-start.48 = (bf16[128,1536]{1,0:T(8,128)(2,1)S(1)}, bf16[128,1536]{1,0:T(8,128)(2,1)S(1)}, u32[]{:S(2)}, u32[]{:S(2)}) collective-permute-start(bf16[128,1536]{1,0:T(8,128)(2,1)S(1)} %token_grad.1.rest_0_), channel_id=1, source_target_pairs={{0,8},{8,0},{16,24},{24,16},{1,9},{9,1},{17,25},{25,17},{2,10},{10... | collective-permute-start | bytes 1179656 | tf_op jit(solution)/shard_map/ppermute | solution.py:81
  476.8 21.3 %reduce-scatter.5.cloned.1.call-done.in_ref = bf16[192,2048]{1,0:T(8,128)(2,1)} async-done(((bf16[1536,2048]{1,0:T(8,128)(2,1)}), bf16[192,2048]{1,0:T(8,128)(2,1)}) %reduce-scatter.5.cloned.1.call-update) | async-done | bytes 786448 | tf_op jit(solution)/shard_map/reduce_scatter | solution.py:1034
  (560 shorter events, 243.7 us)
Async XLA Ops:
  7.2 46.4 %all-gather.4.cloned.1.call-start = ((), (), s32[]{:S(2)}) async-start(), calls=%async_computation.2 | async-start | bytes 5308416 | tf_op jit(solution)/shard_map/all_gather | solution.py:735
  11.8 114.4 %all-gather.6.cloned.1.call-start = ((), (), s32[]{:S(2)}) async-start(), calls=%async_computation.3 | async-start | bytes 5308416 | tf_op jit(solution)/shard_map/all_gather | solution.py:762
  53.6 137.7 %all-gather.8.cloned.1.call-start = ((), (), s32[]{:S(2)}) async-start(), calls=%async_computation.4 | async-start | bytes 10616832 | tf_op jit(solution)/shard_map/all_gather | solution.py:806
  126.3 217.8 %reduce-scatter.3.cloned.1.call-start = ((), (), s32[]{:S(2)}) async-start(), calls=%async_computation.5 | async-start | bytes 10616832 | tf_op jit(solution)/shard_map/reduce_scatter | solution.py:873
  128.0 22.4 %collective-permute-start.13 = (bf16[2,1152,128]{2,1,0:T(8,128)(2,1)S(1)}, bf16[2,1152,128]{2,1,0:T(8,128)(2,1)S(1)}, u32[]{:S(2)}, u32[]{:S(2)}) collective-permute-start(bf16[2,1152,128]{2,1,0:T(8,128)(2,1)S(1)} %pad_maximum_fusion.9), channel_id=1, source_target_pairs={{0,4},{1,5},{2,6},{3,7},{4,0},{5,1},{6,2},{7,3},{8,12},{9,13},{10,... | collective-permute-start | bytes 1769480 | tf_op jit(solution)/shard_map/ppermute | solution.py:81
  171.1 19.2 %collective-permute-start.18 = (bf16[128,1536]{1,0:T(8,128)(2,1)}, bf16[128,1536]{1,0:T(8,128)(2,1)S(1)}, u32[]{:S(2)}, u32[]{:S(2)}) collective-permute-start(bf16[128,1536]{1,0:T(8,128)(2,1)} %get-tuple-element.304.rest_0_), channel_id=1, source_target_pairs={{0,8},{8,0},{16,24},{24,16},{1,9},{9,1},{17,25},{25,17},{2,10},{10... | collective-permute-start | bytes 1179656 | tf_op jit(solution)/shard_map/ppermute | solution.py:81
  173.4 30.7 %collective-permute-start.19 = (bf16[128,1536]{1,0:T(8,128)(2,1)}, bf16[128,1536]{1,0:T(8,128)(2,1)}, u32[]{:S(2)}, u32[]{:S(2)}) collective-permute-start(bf16[128,1536]{1,0:T(8,128)(2,1)} %get-tuple-element.304.rest_0_), channel_id=1, source_target_pairs={{0,16},{8,24},{16,0},{24,8},{1,17},{9,25},{17,1},{25,9},{2,18},{10... | collective-permute-start | bytes 1179656 | tf_op jit(solution)/shard_map/ppermute | solution.py:81
  174.3 29.8 %collective-permute-start.20 = (bf16[128,1536]{1,0:T(8,128)(2,1)}, bf16[128,1536]{1,0:T(8,128)(2,1)}, u32[]{:S(2)}, u32[]{:S(2)}) collective-permute-start(bf16[128,1536]{1,0:T(8,128)(2,1)} %get-tuple-element.304.rest_0_), channel_id=1, source_target_pairs={{0,24},{8,16},{16,8},{24,0},{1,25},{9,17},{17,9},{25,1},{2,26},{10... | collective-permute-start | bytes 1179656 | tf_op jit(solution)/shard_map/ppermute | solution.py:81
  219.0 27.9 %collective-permute-start.22 = (bf16[128,1536]{1,0:T(8,128)(2,1)S(1)}, bf16[128,1536]{1,0:T(8,128)(2,1)S(1)}, u32[]{:S(2)}, u32[]{:S(2)}) collective-permute-start(bf16[128,1536]{1,0:T(8,128)(2,1)S(1)} %get-tuple-element.326), channel_id=1, source_target_pairs={{0,16},{8,24},{16,0},{24,8},{1,17},{9,25},{17,1},{25,9},{2,18},{10... | collective-permute-start | bytes 1179656 | tf_op jit(solution)/shard_map/ppermute | solution.py:81
  221.7 26.0 %collective-permute-start.23 = (bf16[128,1536]{1,0:T(8,128)(2,1)S(1)}, bf16[128,1536]{1,0:T(8,128)(2,1)S(1)}, u32[]{:S(2)}, u32[]{:S(2)}) collective-permute-start(bf16[128,1536]{1,0:T(8,128)(2,1)S(1)} %get-tuple-element.327), channel_id=1, source_target_pairs={{0,24},{8,16},{16,8},{24,0},{1,25},{9,17},{17,9},{25,1},{2,26},{10... | collective-permute-start | bytes 1179656 | tf_op jit(solution)/shard_map/ppermute | solution.py:81
  248.4 185.7 %all-reduce.4.cloned.1.call-start = ((), (), s32[]{:S(2)}) async-start(), calls=%async_computation.6 | async-start | bytes 3145728 | tf_op jit(solution)/shard_map/psum | solution.py:920
  290.1 23.4 %collective-permute-start.33 = (bf16[64,1536]{1,0:T(8,128)(2,1)}, bf16[64,1536]{1,0:T(8,128)(2,1)S(1)}, u32[]{:S(2)}, u32[]{:S(2)}) collective-permute-start(bf16[64,1536]{1,0:T(8,128)(2,1)} %get-tuple-element.347.rest_1_), channel_id=1, source_target_pairs={{0,16},{8,24},{16,0},{24,8},{1,17},{9,25},{17,1},{25,9},{2,18},{10... | collective-permute-start | bytes 589832 | tf_op jit(solution)/shard_map/ppermute | solution.py:81
  304.3 26.1 %collective-permute-start.31 = (bf16[4,1152,128]{2,1,0:T(8,128)(2,1)S(1)}, bf16[4,1152,128]{2,1,0:T(8,128)(2,1)S(1)}, u32[]{:S(2)}, u32[]{:S(2)}) collective-permute-start(bf16[4,1152,128]{2,1,0:T(8,128)(2,1)S(1)} %get-tuple-element.371), channel_id=1, source_target_pairs={{0,1},{1,0},{2,3},{3,2},{4,5},{5,4},{6,7},{7,6},{8,9},{9,8},{10,11... | collective-permute-start | bytes 3538952 | tf_op jit(solution)/shard_map/ppermute | solution.py:81
  304.9 25.5 %collective-permute-start.32 = (bf16[2,1152,128]{2,1,0:T(8,128)(2,1)S(1)}, bf16[2,1152,128]{2,1,0:T(8,128)(2,1)S(1)}, u32[]{:S(2)}, u32[]{:S(2)}) collective-permute-start(bf16[2,1152,128]{2,1,0:T(8,128)(2,1)S(1)} %get-tuple-element.509), channel_id=1, source_target_pairs={{0,4},{1,5},{2,6},{3,7},{4,0},{5,1},{6,2},{7,3},{8,12},{9,13},{10,... | collective-permute-start | bytes 1769480 | tf_op jit(solution)/shard_map/ppermute | solution.py:81
  335.1 25.3 %collective-permute-start.36 = (bf16[4,1152,128]{2,1,0:T(8,128)(2,1)}, bf16[4,1152,128]{2,1,0:T(8,128)(2,1)}, u32[]{:S(2)}, u32[]{:S(2)}) collective-permute-start(bf16[4,1152,128]{2,1,0:T(8,128)(2,1)} %get-tuple-element.389), channel_id=1, source_target_pairs={{0,1},{1,0},{2,3},{3,2},{4,5},{5,4},{6,7},{7,6},{8,9},{9,8},{10,11... | collective-permute-start | bytes 3538952 | tf_op jit(solution)/shard_map/ppermute | solution.py:81
  336.5 24.0 %collective-permute-start.35 = (bf16[2,1152,128]{2,1,0:T(8,128)(2,1)}, bf16[2,1152,128]{2,1,0:T(8,128)(2,1)}, u32[]{:S(2)}, u32[]{:S(2)}) collective-permute-start(bf16[2,1152,128]{2,1,0:T(8,128)(2,1)} %get-tuple-element.507), channel_id=1, source_target_pairs={{0,4},{1,5},{2,6},{3,7},{4,0},{5,1},{6,2},{7,3},{8,12},{9,13},{10,... | collective-permute-start | bytes 1769480 | tf_op jit(solution)/shard_map/ppermute | solution.py:81
  340.3 19.5 %collective-permute-start.37 = (bf16[64,1536]{1,0:T(8,128)(2,1)S(1)}, bf16[64,1536]{1,0:T(8,128)(2,1)S(1)}, u32[]{:S(2)}, u32[]{:S(2)}) collective-permute-start(bf16[64,1536]{1,0:T(8,128)(2,1)S(1)} %get-tuple-element.346.rest_0_), channel_id=1, source_target_pairs={{0,24},{8,16},{16,8},{24,0},{1,25},{9,17},{17,9},{25,1},{2,26},{10... | collective-permute-start | bytes 589832 | tf_op jit(solution)/shard_map/ppermute | solution.py:81
  340.3 36.5 %collective-permute-start.40 = (bf16[64,1536]{1,0:T(8,128)(2,1)}, bf16[64,1536]{1,0:T(8,128)(2,1)}, u32[]{:S(2)}, u32[]{:S(2)}) collective-permute-start(bf16[64,1536]{1,0:T(8,128)(2,1)} %get-tuple-element.347.rest_1_), channel_id=1, source_target_pairs={{0,24},{8,16},{16,8},{24,0},{1,25},{9,17},{17,9},{25,1},{2,26},{10... | collective-permute-start | bytes 589832 | tf_op jit(solution)/shard_map/ppermute | solution.py:81
  366.0 132.2 %reduce-scatter.5.cloned.1.call-start = ((), (), s32[]{:S(2)}) async-start(), calls=%async_computation.7 | async-start | bytes 7077888 | tf_op jit(solution)/shard_map/reduce_scatter | solution.py:1034
  434.9 29.8 %collective-permute-start.46 = (bf16[128,1536]{1,0:T(8,128)(2,1)S(1)}, bf16[128,1536]{1,0:T(8,128)(2,1)S(1)}, u32[]{:S(2)}, u32[]{:S(2)}) collective-permute-start(bf16[128,1536]{1,0:T(8,128)(2,1)S(1)} %copy-done.70), channel_id=1, source_target_pairs={{0,16},{8,24},{16,0},{24,8},{1,17},{9,25},{17,1},{25,9},{2,18},{10... | collective-permute-start | bytes 1179656 | tf_op jit(solution)/shard_map/ppermute | solution.py:81
  436.6 28.1 %collective-permute-start.47 = (bf16[128,1536]{1,0:T(8,128)(2,1)S(1)}, bf16[128,1536]{1,0:T(8,128)(2,1)S(1)}, u32[]{:S(2)}, u32[]{:S(2)}) collective-permute-start(bf16[128,1536]{1,0:T(8,128)(2,1)S(1)} %get-tuple-element.447), channel_id=1, source_target_pairs={{0,24},{8,16},{16,8},{24,0},{1,25},{9,17},{17,9},{25,1},{2,26},{10... | collective-permute-start | bytes 1179656 | tf_op jit(solution)/shard_map/ppermute | solution.py:81
  465.4 35.0 %collective-permute-start.48 = (bf16[128,1536]{1,0:T(8,128)(2,1)S(1)}, bf16[128,1536]{1,0:T(8,128)(2,1)S(1)}, u32[]{:S(2)}, u32[]{:S(2)}) collective-permute-start(bf16[128,1536]{1,0:T(8,128)(2,1)S(1)} %token_grad.1.rest_0_), channel_id=1, source_target_pairs={{0,8},{8,0},{16,24},{24,16},{1,9},{9,1},{17,25},{25,17},{2,10},{10... | collective-permute-start | bytes 1179656 | tf_op jit(solution)/shard_map/ppermute | solution.py:81
  472.8 29.8 %collective-permute-start.49 = (bf16[128,1536]{1,0:T(8,128)(2,1)S(1)}, bf16[128,1536]{1,0:T(8,128)(2,1)S(1)}, u32[]{:S(2)}, u32[]{:S(2)}) collective-permute-start(bf16[128,1536]{1,0:T(8,128)(2,1)S(1)} %token_grad.1.rest_0_), channel_id=1, source_target_pairs={{0,16},{8,24},{16,0},{24,8},{1,17},{9,25},{17,1},{25,9},{2,18},{10... | collective-permute-start | bytes 1179656 | tf_op jit(solution)/shard_map/ppermute | solution.py:81
  473.9 28.7 %collective-permute-start.50 = (bf16[128,1536]{1,0:T(8,128)(2,1)S(1)}, bf16[128,1536]{1,0:T(8,128)(2,1)S(1)}, u32[]{:S(2)}, u32[]{:S(2)}) collective-permute-start(bf16[128,1536]{1,0:T(8,128)(2,1)S(1)} %token_grad.1.rest_0_), channel_id=1, source_target_pairs={{0,24},{8,16},{16,8},{24,0},{1,25},{9,17},{17,9},{25,1},{2,26},{10... | collective-permute-start | bytes 1179656 | tf_op jit(solution)/shard_map/ppermute | solution.py:81
  (230 other events, 1447.7 us)
Sparse Core Ops, SparseCore 0:
  12.0 41.6 all-gather.3
  56.1 44.6 all-gather.5
  126.4 64.9 all-gather.7
  248.5 89.6 reduce-scatter.2
  366.1 67.9 all-reduce.3
  437.3 60.7 reduce-scatter.4
